TPU v7x, 256 devices: a whole 4x4x8 slice. The times are simulated.
256 devices in a mesh: seq: 32 (over x, y, z_hi), head: 8 (over z_lo, core).
Axes of the slice: x: 4, y: 4, z: 8 (z_hi: 2, z_lo: 4; z = z_hi * 4 + z_lo), core: 2. Of those that a mesh axis runs over, the one named last changes fastest.
Arguments:
- query_rows: bfloat16 [8192, 3072], P('seq', 'head'), may hold values from -27 to 27
- key_rows: bfloat16 [8192, 3072], P('seq', 'head'), may hold values from -6 to 6
- value_rows: bfloat16 [8192, 3072], P('seq', 'head'), may hold values from -6 to 6
- rates: float32 [8192, 16], P('seq', 'head'), may hold values from 0.1 to 1
- fw_decay: float32 [32, 16], P('seq', 'head'), may hold values from 0 to 1
- fw_step: float32 [16], P('head'), may hold values from 0.03 to 0.15
- fast_gate: float32 [16, 192, 384], P('head'), may hold values from -0.4375 to 0.4375
- fast_up: float32 [16, 192, 384], P('head'), may hold values from -0.4375 to 0.4375
- fast_down: float32 [16, 384, 192], P('head'), may hold values from -0.3125 to 0.3125
- ttt_gain: float32 [3072], P('head'), may hold values from 0.1 to 1.9
- attn_gain: float32 [3072], P('head'), may hold values from 0.1 to 1.9
- out_proj: bfloat16 [3072, 3072], P('head'), may hold values from -0.109375 to 0.109375
Outputs:
- layer_out: bfloat16 [8192, 3072], P(('seq', 'head'))
All inputs are finite; a program needn't handle non-finite values.
Results may differ from a plain program's by a relative error of at most 0.0053.
Values may be sent and summed in bfloat16 or wider, within the bound.
No kernel may reach another device: no remote copies, remote signals or barrier semaphores. Data moves between devices by JAX's collectives and lax.ppermute only.
A program may use at most 192 MiB of HBM per device.

v0:
```python
import math

import jax
import jax.numpy as jnp
from jax import lax
from jax.sharding import PartitionSpec as P

WINDOW = 2048
NS_STEPS = 5


FULL_PRECISION = lax.Precision.HIGHEST
coef_a = 3.4445
coef_b = -4.775
coef_c = 2.0315


def passed_along(block, axis, distance):
    devices = range(lax.axis_size(axis))
    route = [(i - distance, i) for i in devices if i - distance in devices]
    return lax.ppermute(block, axis, route)


def entering(value, axis, join, neutral):
    count, mine = (lax.axis_size(axis), lax.axis_index(axis))
    pieces = jax.tree.map(lambda part: lax.all_gather(part, axis), value)
    running = jax.tree.map(
        lambda part, zero: jnp.full_like(part, 0) + jnp.asarray(zero, part.dtype), value, neutral
    )

    def hop(position, running):
        longer = join(running, jax.tree.map(lambda part: part[position], pieces))
        return jax.tree.map(lambda new, old: jnp.where(position < mine, new, old), longer, running)

    return lax.fori_loop(0, count - 1, hop, running)


def matmul(left_mat, right_mat):
    return jnp.dot(
        left_mat, right_mat, precision=FULL_PRECISION, preferred_element_type=jnp.float32
    )


def rms_rows(values):
    return values * lax.rsqrt(jnp.mean(values * values, axis=-1, keepdims=True) + 1e-06)


def silu_slope(pre_act):
    sigmoid_z = jax.nn.sigmoid(pre_act)
    return sigmoid_z * (1.0 + pre_act * (1.0 - sigmoid_z))


def orthogonalize(gradient):
    current = gradient / (jnp.sqrt(jnp.sum(gradient * gradient)) + 1e-07)
    for sweep_id in range(NS_STEPS):
        gram_mat = matmul(current, current.T)
        poly_mat = coef_b * gram_mat + coef_c * matmul(gram_mat, gram_mat)
        current = coef_a * current + matmul(poly_mat, current)
    return current


def fast_apply(inputs, gate_mat, up_mat, down_mat):
    return matmul(jax.nn.silu(matmul(inputs, gate_mat)) * matmul(inputs, up_mat), down_mat)


def fast_update(key_norm, targets, token_rates, gate_mat, up_mat, down_mat, step_size):
    pre_gate = matmul(key_norm, gate_mat)
    pre_up = matmul(key_norm, up_mat)
    active = jax.nn.silu(pre_gate)
    middle = active * pre_up
    out_grad = -token_rates[:, None] * targets
    grad_down = matmul(middle.T, out_grad)
    mid_grad = matmul(out_grad, down_mat.T)
    grad_gate = matmul(key_norm.T, mid_grad * pre_up * silu_slope(pre_gate))
    grad_up = matmul(key_norm.T, mid_grad * active)
    return (
        -step_size * orthogonalize(grad_gate),
        -step_size * orthogonalize(grad_up),
        -step_size * orthogonalize(grad_down.T).T,
    )


def window_attention(query_head, key_head, value_head, allowed, scale):
    scores = (
        lax.dot_general(
            query_head, key_head, (((1,), (1,)), ((), ())), preferred_element_type=jnp.float32
        )
        * scale
    )
    scores = jnp.where(allowed, scores, -jnp.inf)
    row_max = jnp.max(scores, axis=-1, keepdims=True)
    weights = jnp.exp(scores - row_max)
    row_total = jnp.sum(weights, axis=-1, keepdims=True)
    return (
        jnp.dot(weights.astype(jnp.bfloat16), value_head, preferred_element_type=jnp.float32)
        / row_total
    )


def split_heads(rows_mat, head_count):
    return rows_mat.reshape(rows_mat.shape[0], head_count, -1).transpose(1, 0, 2)


def compose(earlier_part, later_part):
    later_keep = later_part[0][:, None, None]
    return (
        earlier_part[0] * later_part[0],
        later_keep * earlier_part[1] + later_part[1],
        later_keep * earlier_part[2] + later_part[2],
        later_keep * earlier_part[3] + later_part[3],
    )


def local(
    query_rows,
    key_rows,
    value_rows,
    rates,
    fw_decay,
    fw_step,
    fast_gate,
    fast_up,
    fast_down,
    ttt_gain,
    attn_gain,
    out_proj,
):
    block_rows = query_rows.shape[0]
    heads_here = fast_gate.shape[0]
    head_dim = fast_gate.shape[1]
    scale = 1.0 / math.sqrt(head_dim)
    reach_back = WINDOW // block_rows
    device_pos = lax.axis_index("seq")
    earlier_blocks = []
    for offset in range(reach_back, 0, -1):
        earlier_blocks.append(passed_along((key_rows, value_rows), "seq", offset))
    window_keys = jnp.concatenate([shifted[0] for shifted in earlier_blocks] + [key_rows], axis=0)
    window_values = jnp.concatenate(
        [shifted[1] for shifted in earlier_blocks] + [value_rows], axis=0
    )
    query_heads = split_heads(query_rows, heads_here)
    key_heads = split_heads(key_rows, heads_here)
    value_heads = split_heads(value_rows, heads_here)
    key_norm = rms_rows(key_heads.astype(jnp.float32))
    upd_gate, upd_up, upd_down = jax.vmap(fast_update)(
        key_norm, value_heads.astype(jnp.float32), rates.T, fast_gate, fast_up, fast_down, fw_step
    )
    retention = fw_decay[0]
    identity = (
        jnp.ones_like(retention),
        jnp.zeros_like(upd_gate),
        jnp.zeros_like(upd_up),
        jnp.zeros_like(upd_down),
    )
    prefix = entering((retention, upd_gate, upd_up, upd_down), "seq", compose, identity)
    start = device_pos * block_rows
    token_pos = start + jnp.arange(block_rows, dtype=jnp.int32)[:, None]
    key_pos = start - WINDOW + jnp.arange(window_keys.shape[0], dtype=jnp.int32)[None, :]
    allowed = (key_pos <= token_pos) & (key_pos > token_pos - WINDOW) & (key_pos >= 0)
    attended_list = []
    for head_id in range(heads_here):
        low_col = head_id * head_dim
        attended_list.append(
            window_attention(
                query_rows[:, low_col : low_col + head_dim],
                window_keys[:, low_col : low_col + head_dim],
                window_values[:, low_col : low_col + head_dim],
                allowed,
                scale,
            )
        )
    attended = jnp.stack(attended_list)
    query_norm = rms_rows(query_heads.astype(jnp.float32))
    applied = jax.vmap(fast_apply)(
        query_norm, fast_gate + prefix[1], fast_up + prefix[2], fast_down + prefix[3]
    )
    mixed = rms_rows(applied) * ttt_gain.reshape(heads_here, 1, head_dim) + rms_rows(
        attended
    ) * attn_gain.reshape(heads_here, 1, head_dim)
    mixed = mixed.transpose(1, 0, 2).reshape(block_rows, heads_here * head_dim).astype(jnp.bfloat16)
    result = lax.psum_scatter(
        jnp.dot(mixed, out_proj, preferred_element_type=jnp.float32),
        "head",
        scatter_dimension=0,
        tiled=True,
    )
    return result.astype(jnp.bfloat16)


def solution(mesh):
    in_specs = (
        P("seq", "head"),
        P("seq", "head"),
        P("seq", "head"),
        P("seq", "head"),
        P("seq", "head"),
        P("head"),
        P("head", None, None),
        P("head", None, None),
        P("head", None, None),
        P("head"),
        P("head"),
        P("head", None),
    )
    out_specs = P(("seq", "head"), None)
    return jax.shard_map(local, mesh=mesh, in_specs=in_specs, out_specs=out_specs, check_vma=False)
```

profile of v0, /device:TPU:1, one launch (start us, length us, event | category | flops | bytes accessed | tf_op | source)
XLA Modules:
  0.0 1238.3 jit_solution(276079123272572044)
XLA Ops:
  7.9 3.1 fusion.85
  13.1 2.5 multiply_reduce_fusion
  29.3 2.6 multiply_reduce_fusion.1
  42.3 10.8 fusion.13
  53.2 2.8 multiply_reduce_fusion.2
  68.2 4.7 collective-permute-start
  72.9 11.9 collective-permute-start.1
  84.9 3.3 collective-permute-start.2
  90.1 4.6 collective-permute-start.4
  96.2 123.9 %all-gather.3 = f32[32,1,2]{2,1,0:T(1,128)} all-gather(f32[1,1,2]{2,1,0:T(1,128)} %bitcast.185), channel_id=1, replica_groups=mesh['seq'=32,'head'=8] {'seq'}, dimensions={0}, use_global_device_ids=true | all-gather | bytes 264 | tf_op jit(solution)/shard_map/all_gather | solution.py:26
  224.8 3.4 collective-permute-start.7
  231.4 4.2 collective-permute-start.9
  237.2 6.4 collective-permute-start.10
  243.7 5.0 collective-permute-start.11
  248.8 6.4 collective-permute-done.7
  255.2 9.4 collective-permute-start.12
  266.1 13.9 %collective-permute-done.9 = bf16[256,384]{1,0:T(8,128)(2,1)S(1)} collective-permute-done((bf16[256,384]{1,0:T(8,128)(2,1)S(1)}, bf16[256,384]{1,0:T(8,128)(2,1)S(1)}, u32[]{:S(2)}, u32[]{:S(2)}) %collective-permute-start.9) | collective-permute-done | bytes 196640 | tf_op jit(solution)/shard_map/ppermute | solution.py:21
  281.3 4.2 collective-permute-start.15
  285.5 16.1 %collective-permute-done.11 = bf16[256,384]{1,0:T(8,128)(2,1)S(1)} collective-permute-done((bf16[256,384]{1,0:T(8,128)(2,1)S(1)}, bf16[256,384]{1,0:T(8,128)(2,1)S(1)}, u32[]{:S(2)}, u32[]{:S(2)}) %collective-permute-start.11) | collective-permute-done | bytes 196640 | tf_op jit(solution)/shard_map/ppermute | solution.py:21
  301.7 22.1 %collective-permute-done.13 = bf16[256,384]{1,0:T(8,128)(2,1)S(1)} collective-permute-done((bf16[256,384]{1,0:T(8,128)(2,1)S(1)}, bf16[256,384]{1,0:T(8,128)(2,1)S(1)}, u32[]{:S(2)}, u32[]{:S(2)}) %collective-permute-start.13) | collective-permute-done | bytes 196640 | tf_op jit(solution)/shard_map/ppermute | solution.py:21
  323.8 10.5 collective-permute-done.15
  339.8 29.4 %all-gather.12.cloned.1.call-done = f32[64,384,192]{1,2,0:T(8,128)} async-done(((f32[2,384,192]{1,2,0:T(8,128)}), f32[64,384,192]{1,2,0:T(8,128)}) %all-gather.12.cloned.1.call-update) | async-done | bytes 18874384 | tf_op jit(solution)/shard_map/all_gather | solution.py:26
  369.2 267.2 %all-gather.10.cloned.1.call-done = f32[64,192,384]{2,1,0:T(8,128)} async-done(((f32[2,192,384]{2,1,0:T(8,128)}), f32[64,192,384]{2,1,0:T(8,128)}) %all-gather.10.cloned.1.call-update) | async-done | bytes 18874384 | tf_op jit(solution)/shard_map/all_gather | solution.py:26
  636.5 267.4 %all-gather.8.cloned.1.call-done = f32[64,192,384]{2,1,0:T(8,128)} async-done(((f32[2,192,384]{2,1,0:T(8,128)}), f32[64,192,384]{2,1,0:T(8,128)}) %all-gather.8.cloned.1.call-update) | async-done | bytes 18874384 | tf_op jit(solution)/shard_map/all_gather | solution.py:26
  903.8 278.5 %while.18 = (s32[]{:T(128)}, f32[2,192,384]{2,1,0:T(8,128)}, f32[2,192,384]{2,1,0:T(8,128)}, f32[2,384,192]{2,1,0:T(8,128)}, s32[]{:T(128)}, /*index=5*/f32[32,2...) while((s32[]{:T(128)}, f32[2,192,384]{2,1,0:T(8,128)}, ...), condition=%wide.region_6.7_spmd.clone, body=%wide.region_5.6_spmd.clone.sunk | while | flops 1769476 | bytes 7667887 | solution.py:35
  904.5 2.5 fusion.220
  912.0 2.9 fusion.220
  918.2 2.2 fusion.221
  921.1 2.9 fusion.220
  930.1 2.9 fusion.220
  939.2 2.9 fusion.220
  948.2 2.9 fusion.220
  957.2 2.9 fusion.220
  966.3 2.9 fusion.220
  975.3 2.9 fusion.220
  984.3 2.9 fusion.220
  993.3 2.9 fusion.220
  1002.4 2.9 fusion.220
  1011.4 2.9 fusion.220
  1017.5 2.2 fusion.221
  1020.4 2.9 fusion.220
  1029.4 2.9 fusion.220
  1038.4 2.9 fusion.220
  1047.5 2.9 fusion.220
  1056.5 2.9 fusion.220
  1065.6 2.9 fusion.220
  1074.6 2.9 fusion.220
  1080.7 2.2 fusion.221
  1083.6 2.9 fusion.220
  1092.7 2.9 fusion.220
  1101.7 2.9 fusion.220
  1110.7 2.9 fusion.220
  1119.8 2.9 fusion.220
  1128.8 2.9 fusion.220
  1137.8 2.9 fusion.220
  1144.0 2.2 fusion.221
  1146.9 2.9 fusion.220
  1155.9 2.9 fusion.220
  1164.9 2.9 fusion.220
  1174.0 2.9 fusion.220
  1182.3 2.4 fusion.75
  1184.8 2.3 convolution_multiply_fusion.2
  1188.9 2.7 fusion.128
  1191.5 38.2 %reduce-scatter.2.cloned.1.call-done = f32[32,3072]{1,0:T(8,128)} async-done(((f32[256,3072]{1,0:T(8,128)}), f32[32,3072]{1,0:T(8,128)}) %reduce-scatter.2.cloned.1.call-update) | async-done | bytes 393232 | tf_op jit(solution)/shard_map/reduce_scatter | solution.py:181
  (276 shorter events, 244.9 us)
Async XLA Ops:
  6.5 1182.3 %copy-start = (bf16[384,3072]{1,0:T(8,128)(2,1)S(1)}, bf16[384,3072]{1,0:T(8,128)(2,1)}, u32[]{:S(2)}) copy-start(bf16[384,3072]{1,0:T(8,128)(2,1)} %param.25) | copy-start | bytes 7077892
  6.5 4.4 copy-start.9
  6.5 362.7 %all-gather.12.cloned.1.call-start = ((), (), s32[]{:S(2)}) async-start(), calls=%async_computation.4 | async-start | bytes 19464192 | tf_op jit(solution)/shard_map/all_gather | solution.py:26
  7.8 5.2 copy-start.6
  7.8 5.2 copy-start.13
  24.7 1.7 copy-start.16
  25.8 2.3 copy-start.3
  28.1 608.4 %all-gather.10.cloned.1.call-start = ((), (), s32[]{:S(2)}) async-start(), calls=%async_computation.3 | async-start | bytes 19464192 | tf_op jit(solution)/shard_map/all_gather | solution.py:26
  29.3 2.6 copy-start.4
  53.1 850.7 %all-gather.8.cloned.1.call-start = ((), (), s32[]{:S(2)}) async-start(), calls=%async_computation.2 | async-start | bytes 19464192 | tf_op jit(solution)/shard_map/all_gather | solution.py:26
  65.9 2.3 copy-start.5
  66.5 29.4 %copy-start.11 = (bf16[256,384]{1,0:T(8,128)(2,1)S(1)}, bf16[256,384]{1,0:T(8,128)(2,1)}, u32[]{:S(2)}) copy-start(bf16[256,384]{1,0:T(8,128)(2,1)} %param.14) | copy-start | bytes 589828
  66.5 29.5 %copy-start.14 = (f32[384]{0:T(512)S(1)}, f32[384]{0:T(512)}, u32[]{:S(2)}) copy-start(f32[384]{0:T(512)} %param.23) | copy-start | bytes 4612
  66.5 29.6 %copy-start.15 = (f32[384]{0:T(512)S(1)}, f32[384]{0:T(512)}, u32[]{:S(2)}) copy-start(f32[384]{0:T(512)} %param.24) | copy-start | bytes 4612
  68.2 1161.5 %reduce-scatter.2.cloned.1.call-start = ((), (), s32[]{:S(2)}) async-start(), calls=%async_computation.1 | async-start | bytes 3538944 | tf_op jit(solution)/shard_map/reduce_scatter | solution.py:181
  68.2 152.0 %collective-permute-start = (bf16[256,384]{1,0:T(8,128)(2,1)S(1)}, bf16[256,384]{1,0:T(8,128)(2,1)}, u32[]{:S(2)}, u32[]{:S(2)}) collective-permute-start(bf16[256,384]{1,0:T(8,128)(2,1)S(1)} %copy-done.5), channel_id=1, source_target_pairs={{0,64},{8,72},{16,80},{24,88},{32,96},{40,104},{48,112},{56,120},{... | collective-permute-start | bytes 589832 | tf_op jit(solution)/shard_map/ppermute | solution.py:21
  72.9 149.6 %collective-permute-start.1 = (bf16[256,384]{1,0:T(8,128)(2,1)S(1)}, bf16[256,384]{1,0:T(8,128)(2,1)}, u32[]{:S(2)}, u32[]{:S(2)}) collective-permute-start(bf16[256,384]{1,0:T(8,128)(2,1)S(1)} %copy-done.5), channel_id=1, source_target_pairs={{0,56},{8,64},{16,72},{24,80},{32,88},{40,96},{48,104},{56,112},{6... | collective-permute-start | bytes 589832 | tf_op jit(solution)/shard_map/ppermute | solution.py:21
  84.9 139.9 %collective-permute-start.2 = (bf16[256,384]{1,0:T(8,128)(2,1)S(1)}, bf16[256,384]{1,0:T(8,128)(2,1)}, u32[]{:S(2)}, u32[]{:S(2)}) collective-permute-start(bf16[256,384]{1,0:T(8,128)(2,1)S(1)} %copy-done.5), channel_id=1, source_target_pairs={{0,48},{8,56},{16,64},{24,72},{32,80},{40,88},{48,96},{56,104},{64... | collective-permute-start | bytes 589832 | tf_op jit(solution)/shard_map/ppermute | solution.py:21
  88.1 141.0 %collective-permute-start.3 = (bf16[256,384]{1,0:T(8,128)(2,1)S(1)}, bf16[256,384]{1,0:T(8,128)(2,1)}, u32[]{:S(2)}, u32[]{:S(2)}) collective-permute-start(bf16[256,384]{1,0:T(8,128)(2,1)S(1)} %copy-done.5), channel_id=1, source_target_pairs={{0,40},{8,48},{16,56},{24,64},{32,72},{40,80},{48,88},{56,96},{64,... | collective-permute-start | bytes 589832 | tf_op jit(solution)/shard_map/ppermute | solution.py:21
  90.1 141.3 %collective-permute-start.4 = (bf16[256,384]{1,0:T(8,128)(2,1)S(1)}, bf16[256,384]{1,0:T(8,128)(2,1)}, u32[]{:S(2)}, u32[]{:S(2)}) collective-permute-start(bf16[256,384]{1,0:T(8,128)(2,1)S(1)} %copy-done.5), channel_id=1, source_target_pairs={{0,32},{8,40},{16,48},{24,56},{32,64},{40,72},{48,80},{56,88},{64,... | collective-permute-start | bytes 589832 | tf_op jit(solution)/shard_map/ppermute | solution.py:21
  220.2 17.0 %collective-permute-start.5 = (bf16[256,384]{1,0:T(8,128)(2,1)S(1)}, bf16[256,384]{1,0:T(8,128)(2,1)S(1)}, u32[]{:S(2)}, u32[]{:S(2)}) collective-permute-start(bf16[256,384]{1,0:T(8,128)(2,1)S(1)} %copy-done.5), channel_id=1, source_target_pairs={{0,24},{8,32},{16,40},{24,48},{32,56},{40,64},{48,72},{56,80},{64,... | collective-permute-start | bytes 589832 | tf_op jit(solution)/shard_map/ppermute | solution.py:21
  222.5 21.2 %collective-permute-start.6 = (bf16[256,384]{1,0:T(8,128)(2,1)S(1)}, bf16[256,384]{1,0:T(8,128)(2,1)S(1)}, u32[]{:S(2)}, u32[]{:S(2)}) collective-permute-start(bf16[256,384]{1,0:T(8,128)(2,1)S(1)} %copy-done.5), channel_id=1, source_target_pairs={{0,16},{8,24},{16,32},{24,40},{32,48},{40,56},{48,64},{56,72},{64,... | collective-permute-start | bytes 589832 | tf_op jit(solution)/shard_map/ppermute | solution.py:21
  224.8 30.5 %collective-permute-start.7 = (bf16[256,384]{1,0:T(8,128)(2,1)S(1)}, bf16[256,384]{1,0:T(8,128)(2,1)S(1)}, u32[]{:S(2)}, u32[]{:S(2)}) collective-permute-start(bf16[256,384]{1,0:T(8,128)(2,1)S(1)} %copy-done.5), channel_id=1, source_target_pairs={{0,8},{8,16},{16,24},{24,32},{32,40},{40,48},{48,56},{56,64},{64,7... | collective-permute-start | bytes 589832 | tf_op jit(solution)/shard_map/ppermute | solution.py:21
  229.2 35.5 %collective-permute-start.8 = (bf16[256,384]{1,0:T(8,128)(2,1)S(1)}, bf16[256,384]{1,0:T(8,128)(2,1)S(1)}, u32[]{:S(2)}, u32[]{:S(2)}) collective-permute-start(bf16[256,384]{1,0:T(8,128)(2,1)S(1)} %copy-done.6), channel_id=1, source_target_pairs={{0,64},{8,72},{16,80},{24,88},{32,96},{40,104},{48,112},{56,120},{... | collective-permute-start | bytes 589832 | tf_op jit(solution)/shard_map/ppermute | solution.py:21
  231.4 48.5 %collective-permute-start.9 = (bf16[256,384]{1,0:T(8,128)(2,1)S(1)}, bf16[256,384]{1,0:T(8,128)(2,1)S(1)}, u32[]{:S(2)}, u32[]{:S(2)}) collective-permute-start(bf16[256,384]{1,0:T(8,128)(2,1)S(1)} %copy-done.6), channel_id=1, source_target_pairs={{0,56},{8,64},{16,72},{24,80},{32,88},{40,96},{48,104},{56,112},{6... | collective-permute-start | bytes 589832 | tf_op jit(solution)/shard_map/ppermute | solution.py:21
  237.2 44.0 %collective-permute-start.10 = (bf16[256,384]{1,0:T(8,128)(2,1)S(1)}, bf16[256,384]{1,0:T(8,128)(2,1)S(1)}, u32[]{:S(2)}, u32[]{:S(2)}) collective-permute-start(bf16[256,384]{1,0:T(8,128)(2,1)S(1)} %copy-done.6), channel_id=1, source_target_pairs={{0,48},{8,56},{16,64},{24,72},{32,80},{40,88},{48,96},{56,104},{64... | collective-permute-start | bytes 589832 | tf_op jit(solution)/shard_map/ppermute | solution.py:21
  243.7 57.9 %collective-permute-start.11 = (bf16[256,384]{1,0:T(8,128)(2,1)S(1)}, bf16[256,384]{1,0:T(8,128)(2,1)S(1)}, u32[]{:S(2)}, u32[]{:S(2)}) collective-permute-start(bf16[256,384]{1,0:T(8,128)(2,1)S(1)} %copy-done.6), channel_id=1, source_target_pairs={{0,40},{8,48},{16,56},{24,64},{32,72},{40,80},{48,88},{56,96},{64,... | collective-permute-start | bytes 589832 | tf_op jit(solution)/shard_map/ppermute | solution.py:21
  255.2 46.4 %collective-permute-start.12 = (bf16[256,384]{1,0:T(8,128)(2,1)S(1)}, bf16[256,384]{1,0:T(8,128)(2,1)S(1)}, u32[]{:S(2)}, u32[]{:S(2)}) collective-permute-start(bf16[256,384]{1,0:T(8,128)(2,1)S(1)} %copy-done.6), channel_id=1, source_target_pairs={{0,32},{8,40},{16,48},{24,56},{32,64},{40,72},{48,80},{56,88},{64,... | collective-permute-start | bytes 589832 | tf_op jit(solution)/shard_map/ppermute | solution.py:21
  264.7 59.0 %collective-permute-start.13 = (bf16[256,384]{1,0:T(8,128)(2,1)S(1)}, bf16[256,384]{1,0:T(8,128)(2,1)S(1)}, u32[]{:S(2)}, u32[]{:S(2)}) collective-permute-start(bf16[256,384]{1,0:T(8,128)(2,1)S(1)} %copy-done.6), channel_id=1, source_target_pairs={{0,24},{8,32},{16,40},{24,48},{32,56},{40,64},{48,72},{56,80},{64,... | collective-permute-start | bytes 589832 | tf_op jit(solution)/shard_map/ppermute | solution.py:21
  279.9 43.9 %collective-permute-start.14 = (bf16[256,384]{1,0:T(8,128)(2,1)S(1)}, bf16[256,384]{1,0:T(8,128)(2,1)S(1)}, u32[]{:S(2)}, u32[]{:S(2)}) collective-permute-start(bf16[256,384]{1,0:T(8,128)(2,1)S(1)} %copy-done.6), channel_id=1, source_target_pairs={{0,16},{8,24},{16,32},{24,40},{32,48},{40,56},{48,64},{56,72},{64,... | collective-permute-start | bytes 589832 | tf_op jit(solution)/shard_map/ppermute | solution.py:21
  281.3 53.0 %collective-permute-start.15 = (bf16[256,384]{1,0:T(8,128)(2,1)S(1)}, bf16[256,384]{1,0:T(8,128)(2,1)S(1)}, u32[]{:S(2)}, u32[]{:S(2)}) collective-permute-start(bf16[256,384]{1,0:T(8,128)(2,1)S(1)} %copy-done.6), channel_id=1, source_target_pairs={{0,8},{8,16},{16,24},{24,32},{32,40},{40,48},{48,56},{56,64},{64,7... | collective-permute-start | bytes 589832 | tf_op jit(solution)/shard_map/ppermute | solution.py:21
  339.1 564.7 %copy-start.7 = (f32[1,256,192]{1,2,0:T(8,128)}, f32[1,256,192]{1,2,0:T(8,128)S(1)}, u32[]{:S(2)}) copy-start(f32[1,256,192]{1,2,0:T(8,128)S(1)} %fusion.55) | copy-start | bytes 589828
  1182.3 2.4 copy-start.10
  1184.7 2.4 copy-start.1
  1184.8 2.4 copy-start.2
  1187.1 1.5 copy-start.8
  1187.1 1.5 copy-start.12
Sparse Core Ops, SparseCore 0:
  28.2 340.9 all-gather.11
  372.6 263.8 all-gather.9
  639.8 263.9 all-gather.7
  1191.7 38.0 reduce-scatter.1
where the time goes:
time: 1260 us; the launch traced here: 1240 us
  waiting for transfers between devices  672 us (53%)
  other arithmetic  159 us (13%)
  local copies, waits for them, and re-layouts  131 us (10%)
  blocking collectives  124 us (10%)
  matrix products  72.3 us (6%)
  starting transfers between devices  65.6 us (5%)
  between operations  14.4 us (1%)
    all_gather x3, waiting for transfers between devices, entering(): pieces = jax.tree.map(lambda part: lax.all_gather(part, axis), value)  564 us
    select_n x62, other arithmetic, hop(): jnp.where(position < mine, new, old)  155 us
    all_gather x1, blocking collectives, entering(): pieces = jax.tree.map(lambda part: lax.all_gather(part, axis), value)  124 us
    dynamic_slice x62, local copies, waits for them, and re-layouts, hop(): longer = join(running, jax.tree.map(lambda part: part[position], pieces))  102 us
    ppermute x16, waiting for transfers between devices, passed_along(): return lax.ppermute(block, axis, route)  69.7 us
    dot_general x54, matrix products, matmul(): jnp.dot(left_mat, right_mat, precision=FULL_PRECISION, preferred_element_...  65.7 us
    ppermute x16, starting transfers between devices, passed_along(): return lax.ppermute(block, axis, route)  65.5 us
    reduce_scatter x1, waiting for transfers between devices, local(): lax.psum_scatter(jnp.dot(mixed, out_proj, preferred_element_type=jnp.floa...  38.2 us
  transfers between devices with their start and end apart: 20, of which 10 were waited for; matrix products, arithmetic and copies ran while one was open for 4% of the time, Pallas kernels for 0%

commit v1 on v0

v1 whole, which is shorter than its diff:
```python
import functools
import math

import jax
import jax.numpy as jnp
from jax import lax
from jax.experimental import pallas as pl
from jax.experimental.pallas import tpu as pltpu
from jax.sharding import Mesh, PartitionSpec as P

F32 = jnp.float32
BF16 = jnp.bfloat16
HD = 192
FD = 384
BLK = 256
WIDTH = 3072
NS_STEPS = 5
PAIRS = 16
CHUNK = 108
CROWS = 112
PAY = 400
COEF = (3.4445, -4.775, 2.0315)
VMEM_CAP = 32 * 1024 * 1024
VM = pl.BlockSpec(memory_space=pltpu.VMEM)
SM = pl.BlockSpec(memory_space=pltpu.SMEM)


def call(body, outs, ins, flops, nbytes, trans=0, scratch=(), in_specs=None):
    return pl.pallas_call(
        body,
        out_shape=outs,
        in_specs=in_specs or [VM] * len(ins),
        out_specs=jax.tree.map(lambda _: VM, outs),
        scratch_shapes=list(scratch),
        compiler_params=pltpu.CompilerParams(vmem_limit_bytes=VMEM_CAP),
        cost_estimate=pl.CostEstimate(flops=flops, bytes_accessed=nbytes, transcendentals=trans),
    )(*ins)


def nn(a, b):
    return lax.dot_general(a, b, (((1,), (0,)), ((), ())), preferred_element_type=F32)


def nt(a, b):
    return lax.dot_general(a, b, (((1,), (1,)), ((), ())), preferred_element_type=F32)


def split(x):
    hi = x.astype(BF16)
    return hi, (x - hi.astype(F32)).astype(BF16)


def nn3(a, b):
    return nn(a[0], b[0]) + (nn(a[0], b[1]) + nn(a[1], b[0]))


def nt3(a, b):
    return nt(a[0], b[0]) + (nt(a[0], b[1]) + nt(a[1], b[0]))


def three(x):
    hi = x.astype(BF16).astype(F32)
    mid = (x - hi).astype(BF16).astype(F32)
    low = x - hi - mid
    row = lax.broadcasted_iota(jnp.int32, x.shape, 0)
    return jnp.where(row == 0, hi, jnp.where(row == 1, mid, jnp.where(row == 2, low, 0.0)))


def pick(ref, zh):
    return jnp.where(zh == 0, ref[:, :HD], ref[:, HD:])


def pack_body(q_ref, k_ref, v_ref, r_ref, d_ref, own_ref, send_ref):
    zh = lax.axis_index("zh")
    for out_ref, who in ((own_ref, zh), (send_ref, 1 - zh)):
        out_ref[0:BLK, 0:HD] = pick(k_ref, who)
        out_ref[0:BLK, HD:] = pick(v_ref, who)
        q = pick(q_ref, who)
        out_ref[BLK : BLK + 128, 0:HD] = q[0:128]
        out_ref[BLK : BLK + 128, HD:] = q[128:256]
        rate = jnp.where(who == 0, r_ref[:, 0:1], r_ref[:, 1:2])
        rate_row = jnp.broadcast_to(rate, (BLK, 128)).T[0:16, :]
        decay = jnp.where(who == 0, d_ref[0, 0], d_ref[0, 1])
        row = jnp.concatenate([rate_row, jnp.full((16, 128), decay, F32)], axis=1)
        out_ref[384:400, :] = three(row).astype(BF16)


def tail(pay_ref):
    rows = pay_ref[384:400, :].astype(F32)
    return rows[0:1] + rows[1:2] + rows[2:3]


def queries(pay_ref):
    both = pay_ref[BLK : BLK + 128, :]
    return jnp.concatenate([both[:, :HD], both[:, HD:]], axis=0)


def fast_updates(pay_ref, g_ref, u_ref, d_ref, step_ref, work_ref):
    zh = lax.axis_index("zh")
    k = pay_ref[0:BLK, 0:HD]
    v = pay_ref[0:BLK, HD:]
    kf = k.astype(F32)
    rk = lax.rsqrt(jnp.mean(kf * kf, axis=1, keepdims=True) + 1e-6)
    rate = jnp.broadcast_to(tail(pay_ref)[:, :BLK], (128, BLK)).T[:, 0:1]
    gh, gl = split(g_ref[zh])
    uh, ul = split(u_ref[zh])
    dh, dl = split(d_ref[zh])
    pre_gate = rk * (nn(k, gh) + nn(k, gl))
    pre_up = rk * (nn(k, uh) + nn(k, ul))
    back = -rate * (nt(v, dh) + nt(v, dl))
    sig = jax.nn.sigmoid(pre_gate)
    act = pre_gate * sig
    mid_h, mid_l = split(-rate * (act * pre_up))
    gate_h, gate_l = split(rk * (back * pre_up * (sig * (1.0 + pre_gate * (1.0 - sig)))))
    up_h, up_l = split(rk * (back * act))
    kt = k.T
    vt = v.T
    work_ref[0] = nn(kt, gate_h) + nn(kt, gate_l)
    work_ref[1] = nn(kt, up_h) + nn(kt, up_l)
    work_ref[2] = nn(vt, mid_h) + nn(vt, mid_l)
    for i in range(3):
        grad = work_ref[i]
        norm = jnp.sqrt(jnp.sum(grad * grad, keepdims=True)) + 1e-7
        work_ref[i] = grad / norm

    def sweep(_, carry):
        for i in range(3):
            x = work_ref[i]
            xs = split(x)
            gram = nt3(xs, xs)
            gs = split(gram)
            poly = COEF[1] * gram + COEF[2] * nn3(gs, gs)
            work_ref[i] = COEF[0] * x + nn3(split(poly), xs)
        return carry

    lax.fori_loop(0, NS_STEPS, sweep, 0)
    return -step_ref[zh]


def first_body(pay_ref, g_ref, u_ref, d_ref, step_ref, upd_ref, work_ref):
    scale = fast_updates(pay_ref, g_ref, u_ref, d_ref, step_ref, work_ref)
    for i in range(3):
        upd_ref[i] = scale * work_ref[i]


def second_body(own_ref, pay_ref, upd_ref, g_ref, u_ref, d_ref, step_ref, even_ref, send_ref, work_ref, flat_ref):
    scale = fast_updates(pay_ref, g_ref, u_ref, d_ref, step_ref, work_ref)
    zh = lax.axis_index("zh")
    mine = tail(own_ref)[:, BLK:]
    theirs = tail(pay_ref)[:, BLK:]
    keep_even = jnp.where(zh == 0, mine, theirs)
    keep_odd = jnp.where(zh == 0, theirs, mine)
    flat_ref[PAIRS * CHUNK :, :] = jnp.zeros((64, 128), F32)
    for i in range(3):
        other = scale * work_ref[i]
        own = upd_ref[i]
        even = jnp.where(zh == 0, own, other)
        odd = jnp.where(zh == 0, other, own)
        even_ref[i] = even
        for j in range(3):
            cols = slice(j * 128, (j + 1) * 128)
            flat_ref[(3 * i + j) * HD : (3 * i + j + 1) * HD, :] = keep_odd * even[:, cols] + odd[:, cols]
    keep = three(jnp.broadcast_to(keep_even * keep_odd, (16, 128)))[0:4]
    for c in range(PAIRS):
        send_ref[c] = jnp.concatenate([flat_ref[c * CHUNK : (c + 1) * CHUNK, :], keep], axis=0).astype(BF16)


def scan_body(in_ref, out_ref):
    run = jnp.zeros((CROWS, 128), F32)
    for j in range(PAIRS):
        out_ref[j] = run.astype(BF16)
        if j < PAIRS - 1:
            here = in_ref[j].astype(F32)
            keep = here[CHUNK : CHUNK + 1] + here[CHUNK + 1 : CHUNK + 2] + here[CHUNK + 2 : CHUNK + 3]
            run = keep * run + here


def attend_body(own_ref, recv_ref, pair_ref, w1_ref, w2_ref, w3_ref, w4_ref, gain_ref, out_ref, score_ref):
    zh = lax.axis_index("zh")
    pair = lax.axis_index("x") * 4 + lax.axis_index("y")
    scale = 1.0 / math.sqrt(HD)
    wins = (pair_ref, w1_ref, w2_ref, w3_ref, w4_ref)
    q_own = queries(own_ref)
    q_recv = queries(recv_ref)
    gain = jnp.where(zh == 0, gain_ref[:, :HD], gain_ref[:, HD:])
    row = lax.broadcasted_iota(jnp.int32, (BLK, BLK), 0)
    col = lax.broadcasted_iota(jnp.int32, (BLK, BLK), 1)

    def rows_of(parity):
        slot = zh if parity == 0 else 1 - zh
        return pl.ds(pl.multiple_of(slot * BLK, BLK), BLK)

    for parity in range(2):
        q = jnp.where(zh == parity, q_own, q_recv)
        blocks = [(o, e) for o in (4, 3, 2, 1, 0) for e in (0, 1)]
        blocks = blocks[:9] if parity == 0 else blocks[1:]
        top = None
        for n, (o, e) in enumerate(blocks):
            k = wins[o][rows_of(e), 0:HD]
            s = nt(q, k) * scale
            if n == 0:
                s = jnp.where(col > row, s, -1e30)
            if n == 8:
                s = jnp.where(col <= row, s, -1e30)
            if o > 0:
                s = s + jnp.where(pair >= o, 0.0, -1e30)
            score_ref[n] = s
            top = s if top is None else jnp.maximum(top, s)
        top = jnp.max(top, axis=1, keepdims=True)
        total = None
        acc = None
        for n, (o, e) in enumerate(blocks):
            w = jnp.exp(score_ref[n] - top)
            total = w if total is None else total + w
            part = nn(w.astype(BF16), wins[o][rows_of(e), HD:])
            acc = part if acc is None else acc + part
        att = acc / jnp.sum(total, axis=1, keepdims=True)
        norm = lax.rsqrt(jnp.mean(att * att, axis=1, keepdims=True) + 1e-6)
        out_ref[parity] = att * norm * gain


def apply_body(pre_ref, even_ref, own_ref, recv_ref, g_ref, u_ref, d_ref, gain_ref, att_ref, out_ref, flat_ref):
    zh = lax.axis_index("zh")
    for c in range(PAIRS):
        flat_ref[c * CHUNK : (c + 1) * CHUNK, :] = pre_ref[c].astype(F32)[0:CHUNK]
    keep = jnp.where(zh == 0, tail(own_ref)[:, BLK : BLK + 1], tail(recv_ref)[:, BLK : BLK + 1])
    gain = jnp.where(zh == 0, gain_ref[:, :HD], gain_ref[:, HD:])
    q_own = queries(own_ref)
    q_recv = queries(recv_ref)
    base = (g_ref[zh], u_ref[zh], d_ref[zh].T)
    for parity in range(2):
        q = jnp.where(zh == parity, q_own, q_recv)
        qf = q.astype(F32)
        rq = lax.rsqrt(jnp.mean(qf * qf, axis=1, keepdims=True) + 1e-6)
        mats = []
        for i in range(3):
            state = jnp.concatenate(
                [flat_ref[(3 * i + j) * HD : (3 * i + j + 1) * HD, :] for j in range(3)], axis=1
            )
            if parity == 1:
                state = keep * state + even_ref[i]
            mats.append(split(base[i] + state))
        gate = rq * (nn(q, mats[0][0]) + nn(q, mats[0][1]))
        up = rq * (nn(q, mats[1][0]) + nn(q, mats[1][1]))
        applied = nt3(split(gate * jax.nn.sigmoid(gate) * up), mats[2])
        norm = lax.rsqrt(jnp.mean(applied * applied, axis=1, keepdims=True) + 1e-6)
        mixed = (applied * norm * gain + att_ref[parity]).astype(BF16)
        for c in range(2):
            for z in range(4):
                out_ref[c * 2 + parity, (z % 2) * 32 : (z % 2) * 32 + 32, (z // 2) * HD : (z // 2 + 1) * HD] = mixed[
                    z * 64 + c * 32 : z * 64 + c * 32 + 32
                ]


def project_body(mix_ref, own_ref, other_ref, out_ref):
    core = lax.axis_index("c")
    total = None
    for w_ref, which in ((own_ref, core), (other_ref, 1 - core)):
        for zh in range(2):
            part = mix_ref[which * 2 + zh]
            part = jnp.concatenate([part[:, :HD], part[:, HD:]], axis=0)
            part = nn(part, w_ref[zh * HD : (zh + 1) * HD, :])
            total = part if total is None else total + part
    out_ref[...] = total.astype(BF16)


def local(q, k, v, rates, decay, step, gate, up, down, ttt_gain, attn_gain, proj):
    sds = jax.ShapeDtypeStruct
    pay = sds((PAY, FD), BF16)
    own, send = call(
        pack_body, (pay, pay), (q, k, v, rates, decay), 0, 2_000_000, in_specs=[VM, VM, VM, VM, SM]
    )
    recv = lax.ppermute(send, "zh", [(0, 1), (1, 0)])
    proj_other = lax.ppermute(proj, "c", [(0, 1), (1, 0)])
    mats = sds((3, HD, FD), F32)
    work = pltpu.VMEM((3, HD, FD), F32)
    flat = pltpu.VMEM((PAIRS * CHUNK + 64, 128), F32)
    upd = call(
        first_body,
        mats,
        (own, gate, up, down, step),
        6_000_000_000,
        3_000_000,
        in_specs=[VM] * 4 + [SM],
        scratch=[work],
    )
    pair_kv = jnp.concatenate([own[:BLK], recv[:BLK]], axis=0)
    wins = [
        lax.ppermute(pair_kv, ("x", "y"), [(i, i + o) for i in range(PAIRS - o)]) for o in (1, 2, 3, 4)
    ]
    even, outgoing = call(
        second_body,
        (mats, sds((PAIRS, CROWS, 128), BF16)),
        (own, recv, upd, gate, up, down, step),
        6_000_000_000,
        4_000_000,
        in_specs=[VM] * 6 + [SM],
        scratch=[work, flat],
    )
    pieces = lax.all_to_all(outgoing, ("x", "y"), 0, 0, tiled=True)
    sums = call(scan_body, sds((PAIRS, CROWS, 128), BF16), (pieces,), 500_000, 1_000_000)
    prefix = lax.all_to_all(sums, ("x", "y"), 0, 0, tiled=True)
    att = call(
        attend_body,
        sds((2, BLK, HD), F32),
        (own, recv, pair_kv, *wins, attn_gain.reshape(1, FD)),
        1_000_000_000,
        3_000_000,
        1_200_000,
        scratch=[pltpu.VMEM((9, BLK, BLK), F32)],
    )
    mixed = call(
        apply_body,
        sds((4, 64, FD), BF16),
        (prefix, even, own, recv, gate, up, down, ttt_gain.reshape(1, FD), att),
        600_000_000,
        5_000_000,
        scratch=[flat],
    )
    mixed = lax.all_to_all(mixed, ("c", "zh"), 0, 0, tiled=True)
    tile = 512
    partial = pl.pallas_call(
        project_body,
        out_shape=sds((128, WIDTH), BF16),
        grid=(WIDTH // tile,),
        in_specs=[
            pl.BlockSpec((4, 64, FD), lambda i: (0, 0, 0)),
            pl.BlockSpec((FD, tile), lambda i: (0, i)),
            pl.BlockSpec((FD, tile), lambda i: (0, i)),
        ],
        out_specs=pl.BlockSpec((128, tile), lambda i: (0, i)),
        compiler_params=pltpu.CompilerParams(vmem_limit_bytes=VMEM_CAP),
        cost_estimate=pl.CostEstimate(flops=600_000_000, bytes_accessed=6_000_000, transcendentals=0),
    )(mixed, proj, proj_other)
    parts = lax.all_to_all(partial.reshape(4, 32, WIDTH), "zl", 0, 0, tiled=True)
    return jnp.sum(parts.astype(F32), axis=0).astype(BF16)


def solution(mesh):
    fine = Mesh(mesh.devices.reshape(4, 4, 2, 4, 2), ("x", "y", "zh", "zl", "c"))
    seq = ("x", "y", "zh")
    head = ("zl", "c")
    in_specs = (
        P(seq, head),
        P(seq, head),
        P(seq, head),
        P(seq, head),
        P(seq, head),
        P(head),
        P(head, None, None),
        P(head, None, None),
        P(head, None, None),
        P(head),
        P(head),
        P(head, None),
    )
    out_specs = P(("x", "y", "zh", "zl", "c"), None)
    return jax.shard_map(local, mesh=fine, in_specs=in_specs, out_specs=out_specs, check_vma=False)
```

time: 1260 us -> 167 us (0.13); the launches traced: 1240 us -> 166 us
  waiting for transfers between devices: 672 us -> 30.7 us
  other arithmetic: 159 us -> 1.6 us
  local copies, waits for them, and re-layouts: 131 us -> 16.9 us
  blocking collectives: 124 us -> 36.7 us
  matrix products: 72.3 us -> 0 us
  Pallas kernels: 0 us -> 44.5 us
  starting transfers between devices: 65.6 us -> 35.1 us
  between operations: 14.4 us -> 0.22 us
    all_gather x3 -> x0, waiting for transfers between devices: 564 us -> none  [entering(): pieces = jax.tree.map(lambda part: lax.all_gather(part, axis), value)]
    select_n x62 -> x0, other arithmetic: 155 us -> none  [hop(): jnp.where(position < mine, new, old)]
    all_gather x1 -> x0, blocking collectives: 124 us -> none  [entering(): pieces = jax.tree.map(lambda part: lax.all_gather(part, axis), value)]
    dynamic_slice x62 -> x0, local copies, waits for them, and re-layouts: 102 us -> none  [hop(): longer = join(running, jax.tree.map(lambda part: part[position], pieces))]
    dot_general x59 -> x0, matrix products: 72.3 us -> none  [the longest x54 65.7 us: matmul(): jnp.dot(left_mat, right_mat, precision=FULL_PRECISION, preferred_element_...]
    ppermute x16 -> x6, waiting for transfers between devices: 69.7 us -> 5.04 us  [the longest x4 5.03 us: local(): lax.ppermute(pair_kv, ('x', 'y'), [(i, i + o) for i in range(PAIRS - o)])]
    pallas_call x0 -> x7, Pallas kernels: none -> 44.5 us  [the longest x6 42.1 us: call(): pl.pallas_call(body, out_shape=outs, in_specs=in_specs or [VM] * len(ins)...]
    ppermute x16 -> x6, starting transfers between devices: 65.5 us -> 23.8 us  [the longest x4 15.4 us: local(): lax.ppermute(pair_kv, ('x', 'y'), [(i, i + o) for i in range(PAIRS - o)])]
  transfers between devices with their start and end apart: 20 -> 8, of which waited for: 10 -> 3; matrix products, arithmetic and copies ran while one was open for 4% -> 2% of each run, Pallas kernels for 0% -> 25%
where the time goes in v1:
time: 167 us; the launch traced here: 166 us
  Pallas kernels  44.5 us (27%)
  blocking collectives  36.7 us (22%)
  starting transfers between devices  35.1 us (21%)
  waiting for transfers between devices  30.7 us (18%)
  local copies, waits for them, and re-layouts  16.9 us (10%)
    pallas_call x6, Pallas kernels, call(): pl.pallas_call(body, out_shape=outs, in_specs=in_specs or [VM] * len(ins)...  42.1 us
    all_to_all x1, waiting for transfers between devices, local(): prefix = lax.all_to_all(sums, ('x', 'y'), 0, 0, tiled=True)  25.7 us
    all_to_all x1, blocking collectives, local(): lax.all_to_all(partial.reshape(4, 32, WIDTH), 'zl', 0, 0, tiled=True)  23.5 us
    unnamed x44, local copies, waits for them, and re-layouts  16 us
    ppermute x4, starting transfers between devices, local(): lax.ppermute(pair_kv, ('x', 'y'), [(i, i + o) for i in range(PAIRS - o)])  15.4 us
    all_to_all x1, blocking collectives, local(): mixed = lax.all_to_all(mixed, ('c', 'zh'), 0, 0, tiled=True)  13.1 us
    all_to_all x1, starting transfers between devices, local(): pieces = lax.all_to_all(outgoing, ('x', 'y'), 0, 0, tiled=True)  6.95 us
    ppermute x1, starting transfers between devices, local(): recv = lax.ppermute(send, 'zh', [(0, 1), (1, 0)])  5.17 us
  transfers between devices with their start and end apart: 8, of which 3 were waited for; matrix products, arithmetic and copies ran while one was open for 2% of the time, Pallas kernels for 25%

profile of v1, /device:TPU:1, one launch (start us, length us, event | category | flops | bytes accessed | tf_op | source)
XLA Modules:
  0.0 165.8 jit_solution(2083091550518216509)
XLA Ops:
  0.0 3.2 %collective-permute-start.5 = (bf16[384,3072]{1,0:T(8,128)(2,1)}, bf16[384,3072]{1,0:T(8,128)(2,1)S(1)}, u32[]{:S(2)}, u32[]{:S(2)}) collective-permute-start(bf16[384,3072]{1,0:T(8,128)(2,1)} %own_ref.1), channel_id=1, source_target_pairs={{0,1},{1,0},{2,3},{3,2},{4,5},{5,4},{6,7},{7,6},{8,9},{9,8},{10,11... | collective-permute-start | bytes 7077896 | tf_op jit(solution)/shard_map/ppermute | solution.py:274
  3.2 0.8 copy.13.r_ref
  4.1 0.0 copy-start.13
  4.1 0.9 copy-done.13
  5.0 0.0 copy-start.14
  5.0 0.9 copy-done.14
  5.9 0.0 copy-start.15
  5.9 0.9 copy-done.15
  6.8 0.7 copy-done.16
  7.5 2.1 %shard_map.118 = (bf16[400,384]{1,0:T(8,128)(2,1)S(1)}, bf16[400,384]{1,0:T(8,128)(2,1)}) custom-call(bf16[256,384]{1,0:T(8,128)(2,1)S(1)} %copy-done.13, bf16[256,384]{1,0:T(8,128)(2,1)S(1)} %copy-done.14, bf16[256,384]{1,0:T(8,128)(2,1)S(1)} %copy-done.15, f32[256,2]{1,0:T(8,128)S(1)} %copy.13.r_ref, f32[1,2]{1,0:T(1,128)S(1)} %copy-done.16), custom_call_target="tpu_custom_call" | custom-call | bytes 2000000 | tf_op jit(solution)/shard_map/pallas_call | solution.py:29
  9.6 5.2 %collective-permute-start = (bf16[400,384]{1,0:T(8,128)(2,1)}, bf16[400,384]{1,0:T(8,128)(2,1)}, u32[]{:S(2)}, u32[]{:S(2)}) collective-permute-start(bf16[400,384]{1,0:T(8,128)(2,1)} %get-tuple-element.10), channel_id=1, source_target_pairs={{0,8},{8,0},{1,9},{9,1},{2,10},{10,2},{3,11},{11,3},{4,12},{12,4},... | collective-permute-start | bytes 921608 | tf_op jit(solution)/shard_map/ppermute | solution.py:273
  14.7 1.3 copy.14.d_ref
  16.1 0.0 copy-start.4
  16.1 1.1 copy-done.4
  17.1 0.0 copy-start.7
  17.2 1.1 copy-done.7
  18.2 0.0 copy-start.17
  18.2 0.7 copy-done.17
  18.9 0.0 copy-start.5
  18.9 0.0 copy-start.8
  18.9 0.0 copy-start.18
  18.9 15.3 %shard_map.119.upd_ref = f32[3,192,384]{2,1,0:T(8,128)S(1)} custom-call(bf16[400,384]{1,0:T(8,128)(2,1)S(1)} %get-tuple-element.9.pay_ref.own_ref, f32[2,192,384]{2,1,0:T(8,128)S(1)} %copy-done.4, f32[2,192,384]{2,1,0:T(8,128)S(1)} %copy-done.7, f32[2,384,192]{2,1,0:T(8,128)S(1)} %copy.14.d_ref, f32[2]{0:T(128)S(1)} %copy-done.17), custom_call_target="tpu_custom_call" | custom-call | flops 6000000000 | bytes 3000000 | tf_op jit(solution)/shard_map/pallas_call | solution.py:29
  34.2 0.0 collective-permute-done.pay_ref.recv_ref
  34.2 0.0 copy-done.5
  34.2 0.0 copy-done.8
  34.2 0.0 copy-done.18
  34.2 16.1 %shard_map.120 = (f32[3,192,384]{2,1,0:T(8,128)S(1)}, bf16[16,112,128]{2,1,0:T(8,128)(2,1)S(1)}) custom-call(bf16[400,384]{1,0:T(8,128)(2,1)S(1)} %get-tuple-element.9.pay_ref.own_ref, bf16[400,384]{1,0:T(8,128)(2,1)} %collective-permute-done.pay_ref.recv_ref, f32[3,192,384]{2,1,0:T(8,128)S(1)} %shard_map.119.upd_ref, f32[2,192,384]{2,1,0:T(8,128)S(1)} %copy-done.5, ...), custom_call_target="tpu_custom_call" | custom-call | flops 6000000000 | bytes 4000000 | tf_op jit(solution)/shard_map/pallas_call | solution.py:29
  50.3 0.0 copy-start.2
  50.3 0.9 copy-done.2
  51.2 0.0 copy-start.12
  51.2 0.8 copy-done.12
  52.0 7.0 %all-to-all-start = ((bf16[16,112,128]{2,1,0:T(8,128)(2,1)}), bf16[16,112,128]{2,1,0:T(8,128)(2,1)}, u32[]{:S(2)}, u32[]{:S(2)}) async-start(bf16[16,112,128]{2,1,0:T(8,128)(2,1)} %copy-done.12), calls=%async_computation | async-start | bytes 917504 | tf_op jit(solution)/shard_map/all_to_all | solution.py:300
  59.0 0.9 slice.8
  60.0 0.8 pad_maximum_fusion.pair_ref
  60.7 4.0 %collective-permute-start.1 = (bf16[512,384]{1,0:T(8,128)(2,1)}, bf16[512,384]{1,0:T(8,128)(2,1)}, u32[]{:S(2)}, u32[]{:S(2)}) collective-permute-start(bf16[512,384]{1,0:T(8,128)(2,1)} %pad_maximum_fusion.pair_ref), channel_id=1, source_target_pairs={{0,16},{16,32},{32,48},{48,64},{64,80},{80,96},{96,112},{112,128},... | collective-permute-start | bytes 1179656 | tf_op jit(solution)/shard_map/ppermute | solution.py:289
  64.7 4.3 %collective-permute-start.2 = (bf16[512,384]{1,0:T(8,128)(2,1)}, bf16[512,384]{1,0:T(8,128)(2,1)}, u32[]{:S(2)}, u32[]{:S(2)}) collective-permute-start(bf16[512,384]{1,0:T(8,128)(2,1)} %pad_maximum_fusion.pair_ref), channel_id=1, source_target_pairs={{0,32},{16,48},{32,64},{48,80},{64,96},{80,112},{96,128},{112,144}... | collective-permute-start | bytes 1179656 | tf_op jit(solution)/shard_map/ppermute | solution.py:289
  69.0 4.0 %collective-permute-start.3 = (bf16[512,384]{1,0:T(8,128)(2,1)}, bf16[512,384]{1,0:T(8,128)(2,1)}, u32[]{:S(2)}, u32[]{:S(2)}) collective-permute-start(bf16[512,384]{1,0:T(8,128)(2,1)} %pad_maximum_fusion.pair_ref), channel_id=1, source_target_pairs={{0,48},{16,64},{32,80},{48,96},{64,112},{80,128},{96,144},{112,160... | collective-permute-start | bytes 1179656 | tf_op jit(solution)/shard_map/ppermute | solution.py:289
  73.0 3.1 %collective-permute-start.4 = (bf16[512,384]{1,0:T(8,128)(2,1)}, bf16[512,384]{1,0:T(8,128)(2,1)}, u32[]{:S(2)}, u32[]{:S(2)}) collective-permute-start(bf16[512,384]{1,0:T(8,128)(2,1)} %pad_maximum_fusion.pair_ref), channel_id=1, source_target_pairs={{0,64},{16,80},{32,96},{48,112},{64,128},{80,144},{96,160},{112,17... | collective-permute-start | bytes 1179656 | tf_op jit(solution)/shard_map/ppermute | solution.py:289
  76.1 0.0 all-to-all-done.in_ref
  76.1 1.1 shard_map.121
  77.3 0.0 copy-start.1
  77.3 0.8 copy-done.1
  78.0 4.4 %all-to-all-start.1 = ((bf16[16,112,128]{2,1,0:T(8,128)(2,1)}), bf16[16,112,128]{2,1,0:T(8,128)(2,1)}, u32[]{:S(2)}, u32[]{:S(2)}) async-start(bf16[16,112,128]{2,1,0:T(8,128)(2,1)} %copy-done.1), calls=%async_computation.1 | async-start | bytes 917504 | tf_op jit(solution)/shard_map/all_to_all | solution.py:302
  82.4 0.0 copy-done.19
  82.5 0.0 copy-done.20
  82.5 0.0 collective-permute-done.1.w1_ref
  82.5 0.3 collective-permute-done.2.w2_ref
  82.7 4.8 %collective-permute-done.3.w3_ref = bf16[512,384]{1,0:T(8,128)(2,1)} collective-permute-done((bf16[512,384]{1,0:T(8,128)(2,1)}, bf16[512,384]{1,0:T(8,128)(2,1)}, u32[]{:S(2)}, u32[]{:S(2)}) %collective-permute-start.3) | collective-permute-done | bytes 393248 | tf_op jit(solution)/shard_map/ppermute | solution.py:289
  87.5 0.0 collective-permute-done.4.w4_ref
  87.5 4.4 %shard_map.122.att_ref = f32[2,256,192]{2,1,0:T(8,128)S(1)} custom-call(bf16[400,384]{1,0:T(8,128)(2,1)S(1)} %get-tuple-element.9.pay_ref.own_ref, bf16[400,384]{1,0:T(8,128)(2,1)} %collective-permute-done.pay_ref.recv_ref, bf16[512,384]{1,0:T(8,128)(2,1)} %pad_maximum_fusion.pair_ref, bf16[512,384]{1,0:T(8,128)(2,1)} %collective-permute-done.1.w1_ref, ...), custom_call_target="tpu_custom_call" | custom-call | flops 1000000000 | bytes 3000000 | tf_op jit(solution)/shard_map/pallas_call | solution.py:29
  91.9 0.0 copy-start.10
  91.9 0.8 copy-done.10
  92.7 25.7 %all-to-all-done.1.pre_ref = bf16[16,112,128]{2,1,0:T(8,128)(2,1)} async-done(((bf16[16,112,128]{2,1,0:T(8,128)(2,1)}), bf16[16,112,128]{2,1,0:T(8,128)(2,1)}, u32[]{:S(2)}, u32[]{:S(2)}) %all-to-all-start.1) | async-done | bytes 458784 | tf_op jit(solution)/shard_map/all_to_all | solution.py:302
  118.4 1.2 copy-done.3
  119.5 1.1 copy-done.6
  120.6 1.1 copy-done.9
  121.7 1.0 copy-done.11
  122.7 3.1 %shard_map.123 = bf16[4,64,384]{2,1,0:T(8,128)(2,1)S(1)} custom-call(bf16[16,112,128]{2,1,0:T(8,128)(2,1)} %all-to-all-done.1.pre_ref, f32[3,192,384]{2,1,0:T(8,128)S(1)} %copy-done.3, bf16[400,384]{1,0:T(8,128)(2,1)S(1)} %get-tuple-element.9.pay_ref.own_ref, bf16[400,384]{1,0:T(8,128)(2,1)} %collective-permute-done.pay_ref.recv_ref, ...), custom_call_target="tpu_custom_call" | custom-call | flops 600000000 | bytes 5000000 | tf_op jit(solution)/shard_map/pallas_call | solution.py:29
  125.8 13.1 %all_to_all.20.mix_ref = bf16[4,64,384]{2,1,0:T(8,128)(2,1)S(1)} all-to-all(bf16[4,64,384]{2,1,0:T(8,128)(2,1)S(1)} %shard_map.123), channel_id=1, replica_groups=mesh['x'=4,'y'=4,'zh'=2,'zl'=4,'c'=2] {'c','zh'}, dimensions={0} | all-to-all | bytes 393216 | tf_op jit(solution)/shard_map/all_to_all | solution.py:320
  139.0 0.0 collective-permute-done.5.other_ref
  139.0 0.0 copy-done
  139.0 2.4 %shard_map.124 = bf16[128,3072]{1,0:T(8,128)(2,1)S(1)} custom-call(bf16[4,64,384]{2,1,0:T(8,128)(2,1)S(1)} %all_to_all.20.mix_ref, bf16[384,3072]{1,0:T(8,128)(2,1)S(1)} %copy-done, bf16[384,3072]{1,0:T(8,128)(2,1)S(1)} %collective-permute-done.5.other_ref), custom_call_target="tpu_custom_call" | custom-call | flops 600000000 | bytes 6000000 | tf_op jit(solution)/shard_map/pallas_call | solution.py:322
  141.4 23.5 %all_to_all.21 = bf16[4,32,3072]{2,1,0:T(8,128)(2,1)S(1)} all-to-all(bf16[4,32,3072]{2,1,0:T(8,128)(2,1)S(1)} %bitcast.1), channel_id=1, replica_groups=mesh['x'=4,'y'=4,'zh'=2,'zl'=4,'c'=2] {'zl'}, dimensions={0} | all-to-all | bytes 1572864 | tf_op jit(solution)/shard_map/all_to_all | solution.py:335
  164.9 0.8 reduce_sum.12
  (11 shorter events, 0.0 us)
Async XLA Ops:
  0.0 139.0 %collective-permute-start.5 = (bf16[384,3072]{1,0:T(8,128)(2,1)}, bf16[384,3072]{1,0:T(8,128)(2,1)S(1)}, u32[]{:S(2)}, u32[]{:S(2)}) collective-permute-start(bf16[384,3072]{1,0:T(8,128)(2,1)} %own_ref.1), channel_id=1, source_target_pairs={{0,1},{1,0},{2,3},{3,2},{4,5},{5,4},{6,7},{7,6},{8,9},{9,8},{10,11... | collective-permute-start | bytes 7077896 | tf_op jit(solution)/shard_map/ppermute | solution.py:274
  4.1 0.9 copy-start.13
  5.0 0.9 copy-start.14
  5.9 0.9 copy-start.15
  6.8 0.7 copy-start.16
  9.6 24.6 %collective-permute-start = (bf16[400,384]{1,0:T(8,128)(2,1)}, bf16[400,384]{1,0:T(8,128)(2,1)}, u32[]{:S(2)}, u32[]{:S(2)}) collective-permute-start(bf16[400,384]{1,0:T(8,128)(2,1)} %get-tuple-element.10), channel_id=1, source_target_pairs={{0,8},{8,0},{1,9},{9,1},{2,10},{10,2},{3,11},{11,3},{4,12},{12,4},... | collective-permute-start | bytes 921608 | tf_op jit(solution)/shard_map/ppermute | solution.py:273
  16.1 1.1 copy-start.4
  17.1 1.1 copy-start.7
  18.2 0.7 copy-start.17
  18.9 15.3 %copy-start.5 = (f32[2,192,384]{2,1,0:T(8,128)S(1)}, f32[2,192,384]{2,1,0:T(8,128)}, u32[]{:S(2)}) copy-start(f32[2,192,384]{2,1,0:T(8,128)} %g_ref.5) | copy-start | bytes 1769476
  18.9 15.3 %copy-start.8 = (f32[2,192,384]{2,1,0:T(8,128)S(1)}, f32[2,192,384]{2,1,0:T(8,128)}, u32[]{:S(2)}) copy-start(f32[2,192,384]{2,1,0:T(8,128)} %u_ref.5) | copy-start | bytes 1769476
  18.9 15.3 %copy-start.18 = (f32[2]{0:T(128)S(1)}, f32[2]{0:T(128)}, u32[]{:S(2)}) copy-start(f32[2]{0:T(128)} %step_ref.3) | copy-start | bytes 28
  50.3 0.9 copy-start.2
  51.2 0.8 copy-start.12
  52.0 30.4 %copy-start.19 = (f32[384]{0:T(512)S(1)}, f32[384]{0:T(512)}, u32[]{:S(2)}) copy-start(f32[384]{0:T(512)} %param.22) | copy-start | bytes 4612
  52.0 30.4 %copy-start.20 = (f32[384]{0:T(512)S(1)}, f32[384]{0:T(512)}, u32[]{:S(2)}) copy-start(f32[384]{0:T(512)} %param.21) | copy-start | bytes 4612
  52.0 24.1 %all-to-all-start = ((bf16[16,112,128]{2,1,0:T(8,128)(2,1)}), bf16[16,112,128]{2,1,0:T(8,128)(2,1)}, u32[]{:S(2)}, u32[]{:S(2)}) async-start(bf16[16,112,128]{2,1,0:T(8,128)(2,1)} %copy-done.12), calls=%async_computation | async-start | bytes 917504 | tf_op jit(solution)/shard_map/all_to_all | solution.py:300
  60.7 21.7 %collective-permute-start.1 = (bf16[512,384]{1,0:T(8,128)(2,1)}, bf16[512,384]{1,0:T(8,128)(2,1)}, u32[]{:S(2)}, u32[]{:S(2)}) collective-permute-start(bf16[512,384]{1,0:T(8,128)(2,1)} %pad_maximum_fusion.pair_ref), channel_id=1, source_target_pairs={{0,16},{16,32},{32,48},{48,64},{64,80},{80,96},{96,112},{112,128},... | collective-permute-start | bytes 1179656 | tf_op jit(solution)/shard_map/ppermute | solution.py:289
  64.7 18.0 %collective-permute-start.2 = (bf16[512,384]{1,0:T(8,128)(2,1)}, bf16[512,384]{1,0:T(8,128)(2,1)}, u32[]{:S(2)}, u32[]{:S(2)}) collective-permute-start(bf16[512,384]{1,0:T(8,128)(2,1)} %pad_maximum_fusion.pair_ref), channel_id=1, source_target_pairs={{0,32},{16,48},{32,64},{48,80},{64,96},{80,112},{96,128},{112,144}... | collective-permute-start | bytes 1179656 | tf_op jit(solution)/shard_map/ppermute | solution.py:289
  69.0 18.5 %collective-permute-start.3 = (bf16[512,384]{1,0:T(8,128)(2,1)}, bf16[512,384]{1,0:T(8,128)(2,1)}, u32[]{:S(2)}, u32[]{:S(2)}) collective-permute-start(bf16[512,384]{1,0:T(8,128)(2,1)} %pad_maximum_fusion.pair_ref), channel_id=1, source_target_pairs={{0,48},{16,64},{32,80},{48,96},{64,112},{80,128},{96,144},{112,160... | collective-permute-start | bytes 1179656 | tf_op jit(solution)/shard_map/ppermute | solution.py:289
  73.0 14.5 %collective-permute-start.4 = (bf16[512,384]{1,0:T(8,128)(2,1)}, bf16[512,384]{1,0:T(8,128)(2,1)}, u32[]{:S(2)}, u32[]{:S(2)}) collective-permute-start(bf16[512,384]{1,0:T(8,128)(2,1)} %pad_maximum_fusion.pair_ref), channel_id=1, source_target_pairs={{0,64},{16,80},{32,96},{48,112},{64,128},{80,144},{96,160},{112,17... | collective-permute-start | bytes 1179656 | tf_op jit(solution)/shard_map/ppermute | solution.py:289
  77.3 0.8 copy-start.1
  78.0 40.3 %all-to-all-start.1 = ((bf16[16,112,128]{2,1,0:T(8,128)(2,1)}), bf16[16,112,128]{2,1,0:T(8,128)(2,1)}, u32[]{:S(2)}, u32[]{:S(2)}) async-start(bf16[16,112,128]{2,1,0:T(8,128)(2,1)} %copy-done.1), calls=%async_computation.1 | async-start | bytes 917504 | tf_op jit(solution)/shard_map/all_to_all | solution.py:302
  91.9 0.8 copy-start.10
  118.4 1.2 copy-start.3
  119.5 1.1 copy-start.6
  120.6 1.1 copy-start.9
  121.7 1.0 copy-start.11
  122.7 16.3 %copy-start = (bf16[384,3072]{1,0:T(8,128)(2,1)S(1)}, bf16[384,3072]{1,0:T(8,128)(2,1)}, u32[]{:S(2)}) copy-start(bf16[384,3072]{1,0:T(8,128)(2,1)} %own_ref.1) | copy-start | bytes 7077892

commit v2 on v1

--- a/solution.py
+++ b/solution.py
@@ -20,18 +20,56 @@
 CROWS = 112
 PAY = 400
 COEF = (3.4445, -4.775, 2.0315)
-VMEM_CAP = 32 * 1024 * 1024
-VM = pl.BlockSpec(memory_space=pltpu.VMEM)
-SM = pl.BlockSpec(memory_space=pltpu.SMEM)
-
-
-def call(body, outs, ins, flops, nbytes, trans=0, scratch=(), in_specs=None):
+VMEM_CAP = 60 * 1024 * 1024
+
+
+class Lazy:
+    def __init__(self, copy, ref):
+        self.copy, self.ref = copy, ref
+
+    def get(self):
+        if self.copy is not None:
+            self.copy.wait()
+            self.copy = None
+        return self.ref
+
+
+def call(body, outs, ins, flops, nbytes, trans=0, scratch=(), mine=()):
+    outs = list(outs)
+    n_in, n_out = len(ins), len(outs)
+    shapes = [a.shape[1:] if i in mine else a.shape for i, a in enumerate(ins)]
+
+    def kernel(*refs):
+        in_refs, out_refs = refs[:n_in], refs[n_in : n_in + n_out]
+        rest = refs[n_in + n_out :]
+        in_vm, out_vm = rest[:n_in], rest[n_in : n_in + n_out]
+        in_sem, out_sem, extra = rest[n_in + n_out], rest[n_in + n_out + 1], rest[n_in + n_out + 2 :]
+        zh = lax.axis_index("zh")
+        lazy = []
+        for i in range(n_in):
+            src = in_refs[i].at[zh] if i in mine else in_refs[i]
+            copy = pltpu.make_async_copy(src, in_vm[i], in_sem.at[i])
+            copy.start()
+            lazy.append(Lazy(copy, in_vm[i]))
+        copies = [pltpu.make_async_copy(out_vm[i], out_refs[i], out_sem.at[i]) for i in range(n_out)]
+        body(*lazy, *out_vm, *extra)
+        for copy in copies:
+            copy.start()
+        for item in lazy:
+            item.get()
+        for copy in copies:
+            copy.wait()
+
+    any_spec = pl.BlockSpec(memory_space=pltpu.MemorySpace.HBM)
     return pl.pallas_call(
-        body,
+        kernel,
         out_shape=outs,
-        in_specs=in_specs or [VM] * len(ins),
-        out_specs=jax.tree.map(lambda _: VM, outs),
-        scratch_shapes=list(scratch),
+        in_specs=[any_spec] * n_in,
+        out_specs=[any_spec] * n_out,
+        scratch_shapes=[pltpu.VMEM(sh, a.dtype) for sh, a in zip(shapes, ins)]
+        + [pltpu.VMEM(o.shape, o.dtype) for o in outs]
+        + [pltpu.SemaphoreType.DMA((n_in,)), pltpu.SemaphoreType.DMA((n_out,))]
+        + list(scratch),
         compiler_params=pltpu.CompilerParams(vmem_limit_bytes=VMEM_CAP),
         cost_estimate=pl.CostEstimate(flops=flops, bytes_accessed=nbytes, transcendentals=trans),
     )(*ins)
@@ -66,23 +104,33 @@
     return jnp.where(row == 0, hi, jnp.where(row == 1, mid, jnp.where(row == 2, low, 0.0)))
 
 
-def pick(ref, zh):
-    return jnp.where(zh == 0, ref[:, :HD], ref[:, HD:])
-
-
-def pack_body(q_ref, k_ref, v_ref, r_ref, d_ref, own_ref, send_ref):
-    zh = lax.axis_index("zh")
-    for out_ref, who in ((own_ref, zh), (send_ref, 1 - zh)):
-        out_ref[0:BLK, 0:HD] = pick(k_ref, who)
-        out_ref[0:BLK, HD:] = pick(v_ref, who)
-        q = pick(q_ref, who)
-        out_ref[BLK : BLK + 128, 0:HD] = q[0:128]
-        out_ref[BLK : BLK + 128, HD:] = q[128:256]
-        rate = jnp.where(who == 0, r_ref[:, 0:1], r_ref[:, 1:2])
-        rate_row = jnp.broadcast_to(rate, (BLK, 128)).T[0:16, :]
-        decay = jnp.where(who == 0, d_ref[0, 0], d_ref[0, 1])
-        row = jnp.concatenate([rate_row, jnp.full((16, 128), decay, F32)], axis=1)
-        out_ref[384:400, :] = three(row).astype(BF16)
+def pick(ref, who):
+    return jnp.where(who == 0, ref[:, :HD], ref[:, HD:])
+
+
+def one_of(row, who):
+    return jnp.where(who == 0, row[0:1], row[1:2])
+
+
+def fill(out_ref, q, k, v, rate_row, decay):
+    out_ref[0:BLK, 0:HD] = k
+    out_ref[0:BLK, HD:] = v
+    out_ref[BLK : BLK + 128, 0:HD] = q[0:128]
+    out_ref[BLK : BLK + 128, HD:] = q[128:256]
+    row = jnp.concatenate([rate_row, jnp.broadcast_to(decay, (1, 128))], axis=1)
+    out_ref[384:400, :] = three(jnp.broadcast_to(row, (16, FD))).astype(BF16)
+
+
+def pack_body(q, k, v, r, d, send_ref):
+    who = 1 - lax.axis_index("zh")
+    fill(
+        send_ref,
+        pick(q.get(), who),
+        pick(k.get(), who),
+        pick(v.get(), who),
+        one_of(r.get()[...], who),
+        jnp.where(who == 0, d.get()[:, 0:1], d.get()[:, 1:2]),
+    )
 
 
 def tail(pay_ref):
@@ -95,19 +143,34 @@
     return jnp.concatenate([both[:, :HD], both[:, HD:]], axis=0)
 
 
-def fast_updates(pay_ref, g_ref, u_ref, d_ref, step_ref, work_ref):
-    zh = lax.axis_index("zh")
-    k = pay_ref[0:BLK, 0:HD]
-    v = pay_ref[0:BLK, HD:]
+def orthogonalize(mats):
+    norms = [jnp.sqrt(jnp.sum(m * m, keepdims=True)) + 1e-7 for m in mats]
+    mats = [m / n for m, n in zip(mats, norms)]
+    for _ in range(NS_STEPS):
+        parts = [split(x) for x in mats]
+        grams = []
+        for hi, lo in parts:
+            cross = nt(hi, lo)
+            grams.append(nt(hi, hi) + (cross + cross.T))
+        polys = []
+        for gram in grams:
+            hi, lo = split(gram)
+            cross = nn(hi, lo)
+            polys.append(split(COEF[1] * gram + COEF[2] * (nn(hi, hi) + (cross + cross.T))))
+        mats = [COEF[0] * x + nn3(p, s) for x, p, s in zip(mats, polys, parts)]
+    return mats
+
+
+def fast_updates(k, v, rate_row, g, u, dt, step):
     kf = k.astype(F32)
     rk = lax.rsqrt(jnp.mean(kf * kf, axis=1, keepdims=True) + 1e-6)
-    rate = jnp.broadcast_to(tail(pay_ref)[:, :BLK], (128, BLK)).T[:, 0:1]
-    gh, gl = split(g_ref[zh])
-    uh, ul = split(u_ref[zh])
-    dh, dl = split(d_ref[zh])
+    rate = jnp.broadcast_to(rate_row, (128, BLK)).T[:, 0:1]
+    gh, gl = split(g.get()[...])
     pre_gate = rk * (nn(k, gh) + nn(k, gl))
+    uh, ul = split(u.get()[...])
     pre_up = rk * (nn(k, uh) + nn(k, ul))
-    back = -rate * (nt(v, dh) + nt(v, dl))
+    dh, dl = split(dt.get()[...])
+    back = -rate * (nn(v, dh) + nn(v, dl))
     sig = jax.nn.sigmoid(pre_gate)
     act = pre_gate * sig
     mid_h, mid_l = split(-rate * (act * pre_up))
@@ -115,47 +178,54 @@
     up_h, up_l = split(rk * (back * act))
     kt = k.T
     vt = v.T
-    work_ref[0] = nn(kt, gate_h) + nn(kt, gate_l)
-    work_ref[1] = nn(kt, up_h) + nn(kt, up_l)
-    work_ref[2] = nn(vt, mid_h) + nn(vt, mid_l)
-    for i in range(3):
-        grad = work_ref[i]
-        norm = jnp.sqrt(jnp.sum(grad * grad, keepdims=True)) + 1e-7
-        work_ref[i] = grad / norm
-
-    def sweep(_, carry):
-        for i in range(3):
-            x = work_ref[i]
-            xs = split(x)
-            gram = nt3(xs, xs)
-            gs = split(gram)
-            poly = COEF[1] * gram + COEF[2] * nn3(gs, gs)
-            work_ref[i] = COEF[0] * x + nn3(split(poly), xs)
-        return carry
-
-    lax.fori_loop(0, NS_STEPS, sweep, 0)
-    return -step_ref[zh]
-
-
-def first_body(pay_ref, g_ref, u_ref, d_ref, step_ref, upd_ref, work_ref):
-    scale = fast_updates(pay_ref, g_ref, u_ref, d_ref, step_ref, work_ref)
-    for i in range(3):
-        upd_ref[i] = scale * work_ref[i]
-
-
-def second_body(own_ref, pay_ref, upd_ref, g_ref, u_ref, d_ref, step_ref, even_ref, send_ref, work_ref, flat_ref):
-    scale = fast_updates(pay_ref, g_ref, u_ref, d_ref, step_ref, work_ref)
+    grads = [
+        nn(kt, gate_h) + nn(kt, gate_l),
+        nn(kt, up_h) + nn(kt, up_l),
+        nn(vt, mid_h) + nn(vt, mid_l),
+    ]
+    row = step.get()[...]
+    scale = -jnp.where(lax.axis_index("zh") == 0, row[:, 0:1], row[:, 1:2])
+    return [scale * x for x in orthogonalize(grads)]
+
+
+def first_body(q, k, v, r, d, g, u, dt, step, upd_ref, own_ref):
     zh = lax.axis_index("zh")
-    mine = tail(own_ref)[:, BLK:]
+    key = pick(k.get(), zh)
+    value = pick(v.get(), zh)
+    rate_row = one_of(r.get()[...], zh)
+    fill(own_ref, pick(q.get(), zh), key, value, rate_row, jnp.where(zh == 0, d.get()[:, 0:1], d.get()[:, 1:2]))
+    for i, x in enumerate(fast_updates(key, value, rate_row, g, u, dt, step)):
+        upd_ref[i] = x
+
+
+def join_body(own_ref, recv_ref, out_ref, sem):
+    copies = [
+        pltpu.make_async_copy(ref.at[0:BLK], out_ref.at[i * BLK : (i + 1) * BLK], sem.at[i])
+        for i, ref in enumerate((own_ref, recv_ref))
+    ]
+    for copy in copies:
+        copy.start()
+    for copy in copies:
+        copy.wait()
+
+
+def second_body(pay, g, u, dt, step, own, upd, even_ref, send_ref, flat_ref):
+    pay_ref = pay.get()
+    others = fast_updates(
+        pay_ref[0:BLK, 0:HD], pay_ref[0:BLK, HD:], tail(pay_ref)[:, :BLK], g, u, dt, step
+    )
+    zh = lax.axis_index("zh")
+    upd_ref = upd.get()
+    mine = tail(own.get())[:, BLK:]
     theirs = tail(pay_ref)[:, BLK:]
     keep_even = jnp.where(zh == 0, mine, theirs)
     keep_odd = jnp.where(zh == 0, theirs, mine)
     flat_ref[PAIRS * CHUNK :, :] = jnp.zeros((64, 128), F32)
     for i in range(3):
-        other = scale * work_ref[i]
-        own = upd_ref[i]
-        even = jnp.where(zh == 0, own, other)
-        odd = jnp.where(zh == 0, other, own)
+        other = others[i]
+        own_upd = upd_ref[i]
+        even = jnp.where(zh == 0, own_upd, other)
+        odd = jnp.where(zh == 0, other, own_upd)
         even_ref[i] = even
         for j in range(3):
             cols = slice(j * 128, (j + 1) * 128)
@@ -165,7 +235,8 @@
         send_ref[c] = jnp.concatenate([flat_ref[c * CHUNK : (c + 1) * CHUNK, :], keep], axis=0).astype(BF16)
 
 
-def scan_body(in_ref, out_ref):
+def scan_body(pieces, out_ref):
+    in_ref = pieces.get()
     run = jnp.zeros((CROWS, 128), F32)
     for j in range(PAIRS):
         out_ref[j] = run.astype(BF16)
@@ -175,13 +246,14 @@
             run = keep * run + here
 
 
-def attend_body(own_ref, recv_ref, pair_ref, w1_ref, w2_ref, w3_ref, w4_ref, gain_ref, out_ref, score_ref):
+def attend_body(own, recv, pair_kv, w1, w2, w3, w4, gain_in, out_ref, score_ref):
     zh = lax.axis_index("zh")
     pair = lax.axis_index("x") * 4 + lax.axis_index("y")
     scale = 1.0 / math.sqrt(HD)
-    wins = (pair_ref, w1_ref, w2_ref, w3_ref, w4_ref)
-    q_own = queries(own_ref)
-    q_recv = queries(recv_ref)
+    q_own = queries(own.get())
+    q_recv = queries(recv.get())
+    gain_ref = gain_in.get()
+    wins = [w.get() for w in (pair_kv, w1, w2, w3, w4)]
     gain = jnp.where(zh == 0, gain_ref[:, :HD], gain_ref[:, HD:])
     row = lax.broadcasted_iota(jnp.int32, (BLK, BLK), 0)
     col = lax.broadcasted_iota(jnp.int32, (BLK, BLK), 1)
@@ -219,15 +291,18 @@
         out_ref[parity] = att * norm * gain
 
 
-def apply_body(pre_ref, even_ref, own_ref, recv_ref, g_ref, u_ref, d_ref, gain_ref, att_ref, out_ref, flat_ref):
+def apply_body(pre, even, own, recv, g, u, dt, gain_in, att, out_ref, flat_ref):
     zh = lax.axis_index("zh")
+    pre_ref, even_ref, own_ref, recv_ref, gain_ref, att_ref = [
+        x.get() for x in (pre, even, own, recv, gain_in, att)
+    ]
     for c in range(PAIRS):
         flat_ref[c * CHUNK : (c + 1) * CHUNK, :] = pre_ref[c].astype(F32)[0:CHUNK]
     keep = jnp.where(zh == 0, tail(own_ref)[:, BLK : BLK + 1], tail(recv_ref)[:, BLK : BLK + 1])
     gain = jnp.where(zh == 0, gain_ref[:, :HD], gain_ref[:, HD:])
     q_own = queries(own_ref)
     q_recv = queries(recv_ref)
-    base = (g_ref[zh], u_ref[zh], d_ref[zh].T)
+    base = [x.get()[...] for x in (g, u, dt)]
     for parity in range(2):
         q = jnp.where(zh == parity, q_own, q_recv)
         qf = q.astype(F32)
@@ -264,58 +339,72 @@
     out_ref[...] = total.astype(BF16)
 
 
+def total_body(parts, out_ref):
+    ref = parts.get()
+    out_ref[...] = sum(ref[i].astype(F32) for i in range(4)).astype(BF16)
+
+
 def local(q, k, v, rates, decay, step, gate, up, down, ttt_gain, attn_gain, proj):
     sds = jax.ShapeDtypeStruct
     pay = sds((PAY, FD), BF16)
-    own, send = call(
-        pack_body, (pay, pay), (q, k, v, rates, decay), 0, 2_000_000, in_specs=[VM, VM, VM, VM, SM]
-    )
+    rates = rates.T
+    down = jnp.swapaxes(down, 1, 2)
+    step = step.reshape(1, 2)
+    (send,) = call(pack_body, [pay], (q, k, v, rates, decay), 0, 1_000_000)
     recv = lax.ppermute(send, "zh", [(0, 1), (1, 0)])
     proj_other = lax.ppermute(proj, "c", [(0, 1), (1, 0)])
     mats = sds((3, HD, FD), F32)
-    work = pltpu.VMEM((3, HD, FD), F32)
     flat = pltpu.VMEM((PAIRS * CHUNK + 64, 128), F32)
-    upd = call(
+    upd, own = call(
         first_body,
-        mats,
-        (own, gate, up, down, step),
+        [mats, pay],
+        (q, k, v, rates, decay, gate, up, down, step),
         6_000_000_000,
         3_000_000,
-        in_specs=[VM] * 4 + [SM],
-        scratch=[work],
-    )
-    pair_kv = jnp.concatenate([own[:BLK], recv[:BLK]], axis=0)
+        mine=(5, 6, 7),
+    )
+    pair_kv = pl.pallas_call(
+        join_body,
+        out_shape=sds((2 * BLK, FD), BF16),
+        in_specs=[pl.BlockSpec(memory_space=pltpu.MemorySpace.HBM)] * 2,
+        out_specs=pl.BlockSpec(memory_space=pltpu.MemorySpace.HBM),
+        scratch_shapes=[pltpu.SemaphoreType.DMA((2,))],
+        compiler_params=pltpu.CompilerParams(vmem_limit_bytes=VMEM_CAP),
+        cost_estimate=pl.CostEstimate(flops=0, bytes_accessed=800_000, transcendentals=0),
+    )(own, recv)
     wins = [
         lax.ppermute(pair_kv, ("x", "y"), [(i, i + o) for i in range(PAIRS - o)]) for o in (1, 2, 3, 4)
     ]
     even, outgoing = call(
         second_body,
-        (mats, sds((PAIRS, CROWS, 128), BF16)),
-        (own, recv, upd, gate, up, down, step),
+        [mats, sds((PAIRS, CROWS, 128), BF16)],
+        (recv, gate, up, down, step, own, upd),
         6_000_000_000,
         4_000_000,
-        in_specs=[VM] * 6 + [SM],
-        scratch=[work, flat],
-    )
+        scratch=[flat],
+        mine=(1, 2, 3),
+    )
+    outgoing, *wins = lax.optimization_barrier((outgoing, *wins))
     pieces = lax.all_to_all(outgoing, ("x", "y"), 0, 0, tiled=True)
-    sums = call(scan_body, sds((PAIRS, CROWS, 128), BF16), (pieces,), 500_000, 1_000_000)
+    (sums,) = call(scan_body, [sds((PAIRS, CROWS, 128), BF16)], (pieces,), 500_000, 1_000_000)
     prefix = lax.all_to_all(sums, ("x", "y"), 0, 0, tiled=True)
-    att = call(
+    (att,) = call(
         attend_body,
-        sds((2, BLK, HD), F32),
+        [sds((2, BLK, HD), F32)],
         (own, recv, pair_kv, *wins, attn_gain.reshape(1, FD)),
         1_000_000_000,
         3_000_000,
         1_200_000,
         scratch=[pltpu.VMEM((9, BLK, BLK), F32)],
     )
-    mixed = call(
+    (mixed,) = call(
         apply_body,
-        sds((4, 64, FD), BF16),
+        [sds((4, 64, FD), BF16)],
         (prefix, even, own, recv, gate, up, down, ttt_gain.reshape(1, FD), att),
         600_000_000,
         5_000_000,
         scratch=[flat],
+        mine=(4, 5, 6),
     )
     mixed = lax.all_to_all(mixed, ("c", "zh"), 0, 0, tiled=True)
     tile = 512
@@ -333,7 +422,8 @@
         cost_estimate=pl.CostEstimate(flops=600_000_000, bytes_accessed=6_000_000, transcendentals=0),
     )(mixed, proj, proj_other)
     parts = lax.all_to_all(partial.reshape(4, 32, WIDTH), "zl", 0, 0, tiled=True)
-    return jnp.sum(parts.astype(F32), axis=0).astype(BF16)
+    (result,) = call(total_body, [sds((32, WIDTH), BF16)], (parts,), 400_000, 1_000_000)
+    return result
 
 
 def solution(mesh):

time: 167 us -> 170 us (1.018)
  blocking collectives: 36.7 us -> 79.5 us
  waiting for transfers between devices: 30.7 us -> 2.09 us
  local copies, waits for them, and re-layouts: 16.9 us -> 4 us
  Pallas kernels: 44.5 us -> 55.3 us
  starting transfers between devices: 35.1 us -> 28.1 us
    all_to_all x0 -> x1, blocking collectives: none -> 34.2 us  [local(): pieces = lax.all_to_all(outgoing, ('x', 'y'), 0, 0, tiled=True)]
    all_to_all x1, waiting for transfers between devices: 25.7 us -> 2.07 us  [local(): prefix = lax.all_to_all(sums, ('x', 'y'), 0, 0, tiled=True)]
    unnamed x44 -> x12, local copies, waits for them, and re-layouts: 16 us -> 2.9 us
    pallas_call x6 -> x8, Pallas kernels: 42.1 us -> 49.4 us  [the longest x7 36.4 us: call(): pl.pallas_call(kernel, out_shape=outs, in_specs=[any_spec] * n_in, out_sp...]
    all_to_all x1 -> x0, starting transfers between devices: 6.95 us -> none  [local(): pieces = lax.all_to_all(outgoing, ('x', 'y'), 0, 0, tiled=True)]
    all_to_all x1, blocking collectives: 23.5 us -> 29 us  [local(): lax.all_to_all(partial.reshape(4, 32, WIDTH), 'zl', 0, 0, tiled=True)]
    ppermute x4, waiting for transfers between devices: 5.03 us -> 0.01 us  [local(): lax.ppermute(pair_kv, ('x', 'y'), [(i, i + o) for i in range(PAIRS - o)])]
    pallas_call x1, Pallas kernels: 2.44 us -> 5.89 us  [local(): pl.pallas_call(project_body, out_shape=sds((128, WIDTH), BF16), grid=(WID...]
  transfers between devices with their start and end apart: 8 -> 7, of which waited for: 3 -> 1; matrix products, arithmetic and copies ran while one was open for 2% -> 1% of each run, Pallas kernels for 25% -> 28%
where the time goes in v2:
time: 170 us; the launch traced here: 169 us
  blocking collectives  79.5 us (47%)
  Pallas kernels  55.3 us (33%)
  starting transfers between devices  28.1 us (17%)
  local copies, waits for them, and re-layouts  4 us (2%)
  waiting for transfers between devices  2.09 us (1%)
    pallas_call x7, Pallas kernels, call(): pl.pallas_call(kernel, out_shape=outs, in_specs=[any_spec] * n_in, out_sp...  36.4 us
    all_to_all x1, blocking collectives, local(): pieces = lax.all_to_all(outgoing, ('x', 'y'), 0, 0, tiled=True)  34.2 us
    all_to_all x1, blocking collectives, local(): lax.all_to_all(partial.reshape(4, 32, WIDTH), 'zl', 0, 0, tiled=True)  29 us
    all_to_all x1, blocking collectives, local(): mixed = lax.all_to_all(mixed, ('c', 'zh'), 0, 0, tiled=True)  16.3 us
    ppermute x4, starting transfers between devices, local(): lax.ppermute(pair_kv, ('x', 'y'), [(i, i + o) for i in range(PAIRS - o)])  15.5 us
    pallas_call x1, Pallas kernels, local(): pl.pallas_call(join_body, out_shape=sds((2 * BLK, FD), BF16), in_specs=[p...  13 us
    pallas_call x1, Pallas kernels, local(): pl.pallas_call(project_body, out_shape=sds((128, WIDTH), BF16), grid=(WID...  5.89 us
    ppermute x1, starting transfers between devices, local(): recv = lax.ppermute(send, 'zh', [(0, 1), (1, 0)])  5.26 us
  transfers between devices with their start and end apart: 7, of which 1 were waited for; matrix products, arithmetic and copies ran while one was open for 1% of the time, Pallas kernels for 28%

profile of v2, /device:TPU:1, one launch (start us, length us, event | category | flops | bytes accessed | tf_op | source)
XLA Modules:
  0.0 169.3 jit_solution(3697727579796224979)
XLA Ops:
  0.0 3.2 %collective-permute-start.5 = (bf16[384,3072]{1,0:T(8,128)(2,1)}, bf16[384,3072]{1,0:T(8,128)(2,1)S(1)}, u32[]{:S(2)}, u32[]{:S(2)}) collective-permute-start(bf16[384,3072]{1,0:T(8,128)(2,1)} %own_ref.1), channel_id=1, source_target_pairs={{0,1},{1,0},{2,3},{3,2},{4,5},{5,4},{6,7},{7,6},{8,9},{9,8},{10,11... | collective-permute-start | bytes 7077896 | tf_op jit(solution)/shard_map/ppermute | solution.py:355
  3.2 2.2 %shard_map.118 = bf16[400,384]{1,0:T(8,128)(2,1)} custom-call(bf16[256,384]{1,0:T(8,128)(2,1)} %refs_0_.3, bf16[256,384]{1,0:T(8,128)(2,1)} %refs_1_.4, bf16[256,384]{1,0:T(8,128)(2,1)} %refs_2_.4, f32[2,256]{1,0:T(2,128)} %bitcast.8, f32[1,2]{1,0:T(1,128)} %refs_4_.4), custom_call_target="tpu_custom_call" | custom-call | bytes 1000000 | tf_op jit(solution)/shard_map/pallas_call | solution.py:64
  5.4 5.3 %collective-permute-start = (bf16[400,384]{1,0:T(8,128)(2,1)}, bf16[400,384]{1,0:T(8,128)(2,1)S(1)}, u32[]{:S(2)}, u32[]{:S(2)}) collective-permute-start(bf16[400,384]{1,0:T(8,128)(2,1)} %shard_map.118), channel_id=1, source_target_pairs={{0,8},{8,0},{1,9},{9,1},{2,10},{10,2},{3,11},{11,3},{4,12},{12,4},... | collective-permute-start | bytes 921608 | tf_op jit(solution)/shard_map/ppermute | solution.py:354
  10.7 10.3 %shard_map.119 = (f32[3,192,384]{2,1,0:T(8,128)}, bf16[400,384]{1,0:T(8,128)(2,1)}) custom-call(bf16[256,384]{1,0:T(8,128)(2,1)} %refs_0_.3, bf16[256,384]{1,0:T(8,128)(2,1)} %refs_1_.4, bf16[256,384]{1,0:T(8,128)(2,1)} %refs_2_.4, f32[2,256]{1,0:T(2,128)} %bitcast.9, f32[1,2]{1,0:T(1,128)} %refs_4_.4, f32[2,192,384]{2,1,0:T(8,128)} %refs_4_.5, ...), custom_call_target="tpu_custom_call" | custom-call | flops 6000000000 | bytes 3000000 | tf_op jit(solution)/shard_map/pallas_call | solution.py:64
  20.9 0.0 collective-permute-done.refs_0_.recv_ref.refs_1_.refs_3_
  21.0 0.0 copy-start.2
  21.0 0.7 copy-done.2
  21.7 13.0 %shard_map.121.refs_2_ = bf16[512,384]{1,0:T(8,128)(2,1)} custom-call(bf16[400,384]{1,0:T(8,128)(2,1)} %get-tuple-element.14.refs_5_.own_ref.refs_0_.refs_2_, bf16[400,384]{1,0:T(8,128)(2,1)} %copy-done.2), custom_call_target="tpu_custom_call" | custom-call | bytes 800000 | tf_op jit(solution)/shard_map/pallas_call | solution.py:366
  34.7 3.2 %collective-permute-start.1 = (bf16[512,384]{1,0:T(8,128)(2,1)}, bf16[512,384]{1,0:T(8,128)(2,1)S(1)}, u32[]{:S(2)}, u32[]{:S(2)}) collective-permute-start(bf16[512,384]{1,0:T(8,128)(2,1)} %shard_map.121.refs_2_), channel_id=1, source_target_pairs={{0,16},{16,32},{32,48},{48,64},{64,80},{80,96},{96,112},{112,128},... | collective-permute-start | bytes 1179656 | tf_op jit(solution)/shard_map/ppermute | solution.py:376
  37.9 5.2 %collective-permute-start.2 = (bf16[512,384]{1,0:T(8,128)(2,1)}, bf16[512,384]{1,0:T(8,128)(2,1)}, u32[]{:S(2)}, u32[]{:S(2)}) collective-permute-start(bf16[512,384]{1,0:T(8,128)(2,1)} %shard_map.121.refs_2_), channel_id=1, source_target_pairs={{0,32},{16,48},{32,64},{48,80},{64,96},{80,112},{96,128},{112,144}... | collective-permute-start | bytes 1179656 | tf_op jit(solution)/shard_map/ppermute | solution.py:376
  43.2 3.9 %collective-permute-start.3 = (bf16[512,384]{1,0:T(8,128)(2,1)}, bf16[512,384]{1,0:T(8,128)(2,1)}, u32[]{:S(2)}, u32[]{:S(2)}) collective-permute-start(bf16[512,384]{1,0:T(8,128)(2,1)} %shard_map.121.refs_2_), channel_id=1, source_target_pairs={{0,48},{16,64},{32,80},{48,96},{64,112},{80,128},{96,144},{112,160... | collective-permute-start | bytes 1179656 | tf_op jit(solution)/shard_map/ppermute | solution.py:376
  47.1 3.1 %collective-permute-start.4 = (bf16[512,384]{1,0:T(8,128)(2,1)}, bf16[512,384]{1,0:T(8,128)(2,1)}, u32[]{:S(2)}, u32[]{:S(2)}) collective-permute-start(bf16[512,384]{1,0:T(8,128)(2,1)} %shard_map.121.refs_2_), channel_id=1, source_target_pairs={{0,64},{16,80},{32,96},{48,112},{64,128},{80,144},{96,160},{112,17... | collective-permute-start | bytes 1179656 | tf_op jit(solution)/shard_map/ppermute | solution.py:376
  50.2 10.1 %shard_map.120 = (f32[3,192,384]{2,1,0:T(8,128)}, bf16[16,112,128]{2,1,0:T(8,128)(2,1)}) custom-call(bf16[400,384]{1,0:T(8,128)(2,1)} %copy-done.2, f32[2,192,384]{2,1,0:T(8,128)} %refs_4_.5, f32[2,192,384]{2,1,0:T(8,128)} %refs_5_.3, f32[2,192,384]{2,1,0:T(8,128)} %bitcast.6, f32[1,2]{1,0:T(1,128)} %bitcast.11, ...), custom_call_target="tpu_custom_call" | custom-call | flops 6000000000 | bytes 4000000 | tf_op jit(solution)/shard_map/pallas_call | solution.py:64
  60.4 0.0 copy-start.3
  60.4 0.0 copy-start.4
  60.4 0.0 collective-permute-done.1.refs_3_
  60.4 0.0 copy-start.5
  60.4 0.0 collective-permute-done.2.refs_4_
  60.5 0.0 collective-permute-done.3.refs_5_
  60.5 0.0 collective-permute-done.4.refs_6_
  60.5 34.2 %all_to_all.20.refs_0_ = bf16[16,112,128]{2,1,0:T(8,128)(2,1)} all-to-all(bf16[16,112,128]{2,1,0:T(8,128)(2,1)} %get-tuple-element.17), channel_id=1, replica_groups=mesh['x'=4,'y'=4,'zh'=2,'zl'=4,'c'=2] {'x','y'}, dimensions={0} | all-to-all | bytes 917504 | tf_op jit(solution)/shard_map/all_to_all | solution.py:388
  94.7 1.9 %shard_map.122 = bf16[16,112,128]{2,1,0:T(8,128)(2,1)} custom-call(bf16[16,112,128]{2,1,0:T(8,128)(2,1)} %all_to_all.20.refs_0_), custom_call_target="tpu_custom_call" | custom-call | flops 500000 | bytes 1000000 | tf_op jit(solution)/shard_map/pallas_call | solution.py:64
  96.6 4.0 %all-to-all-start.1 = ((bf16[16,112,128]{2,1,0:T(8,128)(2,1)}), bf16[16,112,128]{2,1,0:T(8,128)(2,1)S(1)}, u32[]{:S(2)}, u32[]{:S(2)}) async-start(bf16[16,112,128]{2,1,0:T(8,128)(2,1)} %shard_map.122), calls=%async_computation.1 | async-start | bytes 917504 | tf_op jit(solution)/shard_map/all_to_all | solution.py:390
  100.6 0.0 copy-done.3
  100.6 0.6 reshape.14.refs_7_
  101.2 0.0 copy-done.4
  101.2 0.5 reshape.13.refs_7_
  101.7 0.0 copy-done.5
  101.7 5.4 %shard_map.123.refs_8_ = f32[2,256,192]{2,1,0:T(8,128)} custom-call(bf16[400,384]{1,0:T(8,128)(2,1)} %get-tuple-element.14.refs_5_.own_ref.refs_0_.refs_2_, bf16[400,384]{1,0:T(8,128)(2,1)} %copy-done.2, bf16[512,384]{1,0:T(8,128)(2,1)} %shard_map.121.refs_2_, bf16[512,384]{1,0:T(8,128)(2,1)} %copy-done.5, bf16[512,384]{1,0:T(8,128)(2,1)} %collective-permute-done.2.refs_4_, ...), custom_call_target="tpu_custom_call" | custom-call | flops 1000000000 | bytes 3000000 | tf_op jit(solution)/shard_map/pallas_call | solution.py:64
  107.2 2.1 %all-to-all-done.1.refs_0_ = bf16[16,112,128]{2,1,0:T(8,128)(2,1)S(1)} async-done(((bf16[16,112,128]{2,1,0:T(8,128)(2,1)}), bf16[16,112,128]{2,1,0:T(8,128)(2,1)S(1)}, u32[]{:S(2)}, u32[]{:S(2)}) %all-to-all-start.1) | async-done | bytes 458784 | tf_op jit(solution)/shard_map/all_to_all | solution.py:390
  109.2 0.0 copy-start.1
  109.2 0.8 copy-done.1
  110.0 4.5 %shard_map.124 = bf16[4,64,384]{2,1,0:T(8,128)(2,1)} custom-call(bf16[16,112,128]{2,1,0:T(8,128)(2,1)} %copy-done.1, f32[3,192,384]{2,1,0:T(8,128)} %get-tuple-element.18.refs_1_, bf16[400,384]{1,0:T(8,128)(2,1)} %get-tuple-element.14.refs_5_.own_ref.refs_0_.refs_2_, bf16[400,384]{1,0:T(8,128)(2,1)} %copy-done.2, f32[2,192,384]{2,1,0:T(8,128)} %refs_4_.5, ...), custom_call_target="tpu_custom_call" | custom-call | flops 600000000 | bytes 5000000 | tf_op jit(solution)/shard_map/pallas_call | solution.py:64
  114.6 16.3 %all_to_all.21.mix_ref = bf16[4,64,384]{2,1,0:T(8,128)(2,1)} all-to-all(bf16[4,64,384]{2,1,0:T(8,128)(2,1)} %shard_map.124), channel_id=1, replica_groups=mesh['x'=4,'y'=4,'zh'=2,'zl'=4,'c'=2] {'c','zh'}, dimensions={0} | all-to-all | bytes 393216 | tf_op jit(solution)/shard_map/all_to_all | solution.py:409
  130.9 0.0 collective-permute-done.5.other_ref
  130.9 0.0 copy-start
  130.9 1.4 copy-done
  132.3 5.9 %shard_map.125 = bf16[128,3072]{1,0:T(8,128)(2,1)} custom-call(bf16[4,64,384]{2,1,0:T(8,128)(2,1)} %all_to_all.21.mix_ref, bf16[384,3072]{1,0:T(8,128)(2,1)} %own_ref.1, bf16[384,3072]{1,0:T(8,128)(2,1)} %copy-done), custom_call_target="tpu_custom_call" | custom-call | flops 600000000 | bytes 6000000 | tf_op jit(solution)/shard_map/pallas_call | solution.py:411
  138.2 29.0 %all_to_all.22.refs_0_ = bf16[4,32,3072]{2,1,0:T(8,128)(2,1)} all-to-all(bf16[4,32,3072]{2,1,0:T(8,128)(2,1)} %bitcast.4), channel_id=1, replica_groups=mesh['x'=4,'y'=4,'zh'=2,'zl'=4,'c'=2] {'zl'}, dimensions={0} | all-to-all | bytes 1572864 | tf_op jit(solution)/shard_map/all_to_all | solution.py:424
  167.2 1.9 %shard_map.126 = bf16[32,3072]{1,0:T(8,128)(2,1)} custom-call(bf16[4,32,3072]{2,1,0:T(8,128)(2,1)} %all_to_all.22.refs_0_), custom_call_target="tpu_custom_call" | custom-call | flops 400000 | bytes 1000000 | tf_op jit(solution)/shard_map/pallas_call | solution.py:64
Async XLA Ops:
  0.0 130.9 %collective-permute-start.5 = (bf16[384,3072]{1,0:T(8,128)(2,1)}, bf16[384,3072]{1,0:T(8,128)(2,1)S(1)}, u32[]{:S(2)}, u32[]{:S(2)}) collective-permute-start(bf16[384,3072]{1,0:T(8,128)(2,1)} %own_ref.1), channel_id=1, source_target_pairs={{0,1},{1,0},{2,3},{3,2},{4,5},{5,4},{6,7},{7,6},{8,9},{9,8},{10,11... | collective-permute-start | bytes 7077896 | tf_op jit(solution)/shard_map/ppermute | solution.py:355
  5.4 15.5 %collective-permute-start = (bf16[400,384]{1,0:T(8,128)(2,1)}, bf16[400,384]{1,0:T(8,128)(2,1)S(1)}, u32[]{:S(2)}, u32[]{:S(2)}) collective-permute-start(bf16[400,384]{1,0:T(8,128)(2,1)} %shard_map.118), channel_id=1, source_target_pairs={{0,8},{8,0},{1,9},{9,1},{2,10},{10,2},{3,11},{11,3},{4,12},{12,4},... | collective-permute-start | bytes 921608 | tf_op jit(solution)/shard_map/ppermute | solution.py:354
  21.0 0.7 copy-start.2
  34.7 25.7 %collective-permute-start.1 = (bf16[512,384]{1,0:T(8,128)(2,1)}, bf16[512,384]{1,0:T(8,128)(2,1)S(1)}, u32[]{:S(2)}, u32[]{:S(2)}) collective-permute-start(bf16[512,384]{1,0:T(8,128)(2,1)} %shard_map.121.refs_2_), channel_id=1, source_target_pairs={{0,16},{16,32},{32,48},{48,64},{64,80},{80,96},{96,112},{112,128},... | collective-permute-start | bytes 1179656 | tf_op jit(solution)/shard_map/ppermute | solution.py:376
  37.9 22.5 %collective-permute-start.2 = (bf16[512,384]{1,0:T(8,128)(2,1)}, bf16[512,384]{1,0:T(8,128)(2,1)}, u32[]{:S(2)}, u32[]{:S(2)}) collective-permute-start(bf16[512,384]{1,0:T(8,128)(2,1)} %shard_map.121.refs_2_), channel_id=1, source_target_pairs={{0,32},{16,48},{32,64},{48,80},{64,96},{80,112},{96,128},{112,144}... | collective-permute-start | bytes 1179656 | tf_op jit(solution)/shard_map/ppermute | solution.py:376
  43.2 17.3 %collective-permute-start.3 = (bf16[512,384]{1,0:T(8,128)(2,1)}, bf16[512,384]{1,0:T(8,128)(2,1)}, u32[]{:S(2)}, u32[]{:S(2)}) collective-permute-start(bf16[512,384]{1,0:T(8,128)(2,1)} %shard_map.121.refs_2_), channel_id=1, source_target_pairs={{0,48},{16,64},{32,80},{48,96},{64,112},{80,128},{96,144},{112,160... | collective-permute-start | bytes 1179656 | tf_op jit(solution)/shard_map/ppermute | solution.py:376
  47.1 13.4 %collective-permute-start.4 = (bf16[512,384]{1,0:T(8,128)(2,1)}, bf16[512,384]{1,0:T(8,128)(2,1)}, u32[]{:S(2)}, u32[]{:S(2)}) collective-permute-start(bf16[512,384]{1,0:T(8,128)(2,1)} %shard_map.121.refs_2_), channel_id=1, source_target_pairs={{0,64},{16,80},{32,96},{48,112},{64,128},{80,144},{96,160},{112,17... | collective-permute-start | bytes 1179656 | tf_op jit(solution)/shard_map/ppermute | solution.py:376
  60.4 40.2 %copy-start.3 = (f32[384]{0:T(512)S(1)}, f32[384]{0:T(512)}, u32[]{:S(2)}) copy-start(f32[384]{0:T(512)} %param.22) | copy-start | bytes 4612
  60.4 40.8 %copy-start.4 = (f32[384]{0:T(512)S(1)}, f32[384]{0:T(512)}, u32[]{:S(2)}) copy-start(f32[384]{0:T(512)} %param.21) | copy-start | bytes 4612
  60.4 41.3 %copy-start.5 = (bf16[512,384]{1,0:T(8,128)(2,1)}, bf16[512,384]{1,0:T(8,128)(2,1)S(1)}, u32[]{:S(2)}) copy-start(bf16[512,384]{1,0:T(8,128)(2,1)S(1)} %collective-permute-done.1.refs_3_) | copy-start | bytes 1179652
  96.6 12.7 %all-to-all-start.1 = ((bf16[16,112,128]{2,1,0:T(8,128)(2,1)}), bf16[16,112,128]{2,1,0:T(8,128)(2,1)S(1)}, u32[]{:S(2)}, u32[]{:S(2)}) async-start(bf16[16,112,128]{2,1,0:T(8,128)(2,1)} %shard_map.122), calls=%async_computation.1 | async-start | bytes 917504 | tf_op jit(solution)/shard_map/all_to_all | solution.py:390
  109.2 0.8 copy-start.1
  130.9 1.4 copy-start

commit v3 on v2

--- a/solution.py
+++ b/solution.py
@@ -21,6 +21,7 @@
 PAY = 400
 COEF = (3.4445, -4.775, 2.0315)
 VMEM_CAP = 60 * 1024 * 1024
+SMALL = 12 * 1024 * 1024
 
 
 class Lazy:
@@ -34,7 +35,7 @@
         return self.ref
 
 
-def call(body, outs, ins, flops, nbytes, trans=0, scratch=(), mine=()):
+def call(body, outs, ins, flops, nbytes, trans=0, scratch=(), mine=(), cap=VMEM_CAP):
     outs = list(outs)
     n_in, n_out = len(ins), len(outs)
     shapes = [a.shape[1:] if i in mine else a.shape for i, a in enumerate(ins)]
@@ -70,7 +71,7 @@
         + [pltpu.VMEM(o.shape, o.dtype) for o in outs]
         + [pltpu.SemaphoreType.DMA((n_in,)), pltpu.SemaphoreType.DMA((n_out,))]
         + list(scratch),
-        compiler_params=pltpu.CompilerParams(vmem_limit_bytes=VMEM_CAP),
+        compiler_params=pltpu.CompilerParams(vmem_limit_bytes=cap),
         cost_estimate=pl.CostEstimate(flops=flops, bytes_accessed=nbytes, transcendentals=trans),
     )(*ins)
 
@@ -198,15 +199,9 @@
         upd_ref[i] = x
 
 
-def join_body(own_ref, recv_ref, out_ref, sem):
-    copies = [
-        pltpu.make_async_copy(ref.at[0:BLK], out_ref.at[i * BLK : (i + 1) * BLK], sem.at[i])
-        for i, ref in enumerate((own_ref, recv_ref))
-    ]
-    for copy in copies:
-        copy.start()
-    for copy in copies:
-        copy.wait()
+def join_body(own, recv, out_ref):
+    out_ref[0:BLK] = own.get()[0:BLK]
+    out_ref[BLK:] = recv.get()[0:BLK]
 
 
 def second_body(pay, g, u, dt, step, own, upd, even_ref, send_ref, flat_ref):
@@ -363,15 +358,7 @@
         3_000_000,
         mine=(5, 6, 7),
     )
-    pair_kv = pl.pallas_call(
-        join_body,
-        out_shape=sds((2 * BLK, FD), BF16),
-        in_specs=[pl.BlockSpec(memory_space=pltpu.MemorySpace.HBM)] * 2,
-        out_specs=pl.BlockSpec(memory_space=pltpu.MemorySpace.HBM),
-        scratch_shapes=[pltpu.SemaphoreType.DMA((2,))],
-        compiler_params=pltpu.CompilerParams(vmem_limit_bytes=VMEM_CAP),
-        cost_estimate=pl.CostEstimate(flops=0, bytes_accessed=800_000, transcendentals=0),
-    )(own, recv)
+    (pair_kv,) = call(join_body, [sds((2 * BLK, FD), BF16)], (own, recv), 0, 800_000)
     wins = [
         lax.ppermute(pair_kv, ("x", "y"), [(i, i + o) for i in range(PAIRS - o)]) for o in (1, 2, 3, 4)
     ]
@@ -384,9 +371,9 @@
         scratch=[flat],
         mine=(1, 2, 3),
     )
-    outgoing, *wins = lax.optimization_barrier((outgoing, *wins))
+    outgoing, wins[1], wins[3] = lax.optimization_barrier((outgoing, wins[1], wins[3]))
     pieces = lax.all_to_all(outgoing, ("x", "y"), 0, 0, tiled=True)
-    (sums,) = call(scan_body, [sds((PAIRS, CROWS, 128), BF16)], (pieces,), 500_000, 1_000_000)
+    (sums,) = call(scan_body, [sds((PAIRS, CROWS, 128), BF16)], (pieces,), 500_000, 1_000_000, cap=SMALL)
     prefix = lax.all_to_all(sums, ("x", "y"), 0, 0, tiled=True)
     (att,) = call(
         attend_body,
@@ -418,11 +405,11 @@
             pl.BlockSpec((FD, tile), lambda i: (0, i)),
         ],
         out_specs=pl.BlockSpec((128, tile), lambda i: (0, i)),
-        compiler_params=pltpu.CompilerParams(vmem_limit_bytes=VMEM_CAP),
+        compiler_params=pltpu.CompilerParams(vmem_limit_bytes=SMALL),
         cost_estimate=pl.CostEstimate(flops=600_000_000, bytes_accessed=6_000_000, transcendentals=0),
     )(mixed, proj, proj_other)
     parts = lax.all_to_all(partial.reshape(4, 32, WIDTH), "zl", 0, 0, tiled=True)
-    (result,) = call(total_body, [sds((32, WIDTH), BF16)], (parts,), 400_000, 1_000_000)
+    (result,) = call(total_body, [sds((32, WIDTH), BF16)], (parts,), 400_000, 1_000_000, cap=SMALL)
     return result
 
 

time: 170 us -> 140 us (0.82)
  blocking collectives: 79.5 us -> 45 us
  Pallas kernels: 55.3 us -> 41.1 us
  starting transfers between devices: 28.1 us -> 38.1 us
  waiting for transfers between devices: 2.09 us -> 9.6 us
    all_to_all x1 -> x0, blocking collectives: 34.2 us -> none  [local(): pieces = lax.all_to_all(outgoing, ('x', 'y'), 0, 0, tiled=True)]
    pallas_call x1 -> x0, Pallas kernels: 13 us -> none  [local(): pl.pallas_call(join_body, out_shape=sds((2 * BLK, FD), BF16), in_specs=[p...]
    all_to_all x0 -> x1, starting transfers between devices: none -> 9.81 us  [local(): pieces = lax.all_to_all(outgoing, ('x', 'y'), 0, 0, tiled=True)]
    all_to_all x1, waiting for transfers between devices: 2.07 us -> 8.6 us  [local(): prefix = lax.all_to_all(sums, ('x', 'y'), 0, 0, tiled=True)]
    pallas_call x7 -> x8, Pallas kernels: 36.4 us -> 36.6 us  [call(): pl.pallas_call(kernel, out_shape=outs, in_specs=[any_spec] * n_in, out_sp...]
  transfers between devices with their start and end apart: 7 -> 8, of which waited for: 1 -> 2; matrix products, arithmetic and copies ran while one was open for 1% -> 1% of each run, Pallas kernels for 28% -> 26%
where the time goes in v3:
time: 140 us; the launch traced here: 138 us
  blocking collectives  45 us (32%)
  Pallas kernels  41.1 us (29%)
  starting transfers between devices  38.1 us (27%)
  waiting for transfers between devices  9.6 us (7%)
  local copies, waits for them, and re-layouts  4.19 us (3%)
    pallas_call x8, Pallas kernels, call(): pl.pallas_call(kernel, out_shape=outs, in_specs=[any_spec] * n_in, out_sp...  36.6 us
    all_to_all x1, blocking collectives, local(): lax.all_to_all(partial.reshape(4, 32, WIDTH), 'zl', 0, 0, tiled=True)  30.3 us
    ppermute x4, starting transfers between devices, local(): lax.ppermute(pair_kv, ('x', 'y'), [(i, i + o) for i in range(PAIRS - o)])  15.7 us
    all_to_all x1, blocking collectives, local(): mixed = lax.all_to_all(mixed, ('c', 'zh'), 0, 0, tiled=True)  14.8 us
    all_to_all x1, starting transfers between devices, local(): pieces = lax.all_to_all(outgoing, ('x', 'y'), 0, 0, tiled=True)  9.81 us
    all_to_all x1, waiting for transfers between devices, local(): prefix = lax.all_to_all(sums, ('x', 'y'), 0, 0, tiled=True)  8.6 us
    ppermute x1, starting transfers between devices, local(): recv = lax.ppermute(send, 'zh', [(0, 1), (1, 0)])  5.26 us
    pallas_call x1, Pallas kernels, local(): pl.pallas_call(project_body, out_shape=sds((128, WIDTH), BF16), grid=(WID...  4.56 us
  transfers between devices with their start and end apart: 8, of which 2 were waited for; matrix products, arithmetic and copies ran while one was open for 1% of the time, Pallas kernels for 26%

profile of v3, /device:TPU:1, one launch (start us, length us, event | category | flops | bytes accessed | tf_op | source)
XLA Modules:
  0.0 138.4 jit_solution(13038714875609711261)
XLA Ops:
  0.0 3.2 %collective-permute-start.5 = (bf16[384,3072]{1,0:T(8,128)(2,1)}, bf16[384,3072]{1,0:T(8,128)(2,1)}, u32[]{:S(2)}, u32[]{:S(2)}) collective-permute-start(bf16[384,3072]{1,0:T(8,128)(2,1)} %own_ref.1), channel_id=1, source_target_pairs={{0,1},{1,0},{2,3},{3,2},{4,5},{5,4},{6,7},{7,6},{8,9},{9,8},{10,11... | collective-permute-start | bytes 7077896 | tf_op jit(solution)/shard_map/ppermute | solution.py:350
  3.2 2.2 %shard_map.118 = bf16[400,384]{1,0:T(8,128)(2,1)} custom-call(bf16[256,384]{1,0:T(8,128)(2,1)} %refs_0_.3, bf16[256,384]{1,0:T(8,128)(2,1)} %refs_1_.4, bf16[256,384]{1,0:T(8,128)(2,1)} %refs_2_.4, f32[2,256]{1,0:T(2,128)} %bitcast.8, f32[1,2]{1,0:T(1,128)} %refs_4_.4), custom_call_target="tpu_custom_call" | custom-call | bytes 1000000 | tf_op jit(solution)/shard_map/pallas_call | solution.py:65
  5.4 5.3 %collective-permute-start = (bf16[400,384]{1,0:T(8,128)(2,1)}, bf16[400,384]{1,0:T(8,128)(2,1)S(1)}, u32[]{:S(2)}, u32[]{:S(2)}) collective-permute-start(bf16[400,384]{1,0:T(8,128)(2,1)} %shard_map.118), channel_id=1, source_target_pairs={{0,8},{8,0},{1,9},{9,1},{2,10},{10,2},{3,11},{11,3},{4,12},{12,4},... | collective-permute-start | bytes 921608 | tf_op jit(solution)/shard_map/ppermute | solution.py:349
  10.7 10.3 %shard_map.119 = (f32[3,192,384]{2,1,0:T(8,128)}, bf16[400,384]{1,0:T(8,128)(2,1)}) custom-call(bf16[256,384]{1,0:T(8,128)(2,1)} %refs_0_.3, bf16[256,384]{1,0:T(8,128)(2,1)} %refs_1_.4, bf16[256,384]{1,0:T(8,128)(2,1)} %refs_2_.4, f32[2,256]{1,0:T(2,128)} %bitcast.9, f32[1,2]{1,0:T(1,128)} %refs_4_.4, f32[2,192,384]{2,1,0:T(8,128)} %refs_4_.5, ...), custom_call_target="tpu_custom_call" | custom-call | flops 6000000000 | bytes 3000000 | tf_op jit(solution)/shard_map/pallas_call | solution.py:65
  21.0 0.0 collective-permute-done.refs_0_.refs_1_.refs_3_
  21.0 0.0 copy-start.2
  21.0 0.7 copy-done.2
  21.7 1.9 %shard_map.121.refs_2_ = bf16[512,384]{1,0:T(8,128)(2,1)} custom-call(bf16[400,384]{1,0:T(8,128)(2,1)} %get-tuple-element.12.refs_5_.refs_0_.refs_2_, bf16[400,384]{1,0:T(8,128)(2,1)} %copy-done.2), custom_call_target="tpu_custom_call" | custom-call | bytes 800000 | tf_op jit(solution)/shard_map/pallas_call | solution.py:65
  23.6 4.8 %collective-permute-start.1 = (bf16[512,384]{1,0:T(8,128)(2,1)}, bf16[512,384]{1,0:T(8,128)(2,1)S(1)}, u32[]{:S(2)}, u32[]{:S(2)}) collective-permute-start(bf16[512,384]{1,0:T(8,128)(2,1)} %shard_map.121.refs_2_), channel_id=1, source_target_pairs={{0,32},{16,48},{32,64},{48,80},{64,96},{80,112},{96,128},{112,144}... | collective-permute-start | bytes 1179656 | tf_op jit(solution)/shard_map/ppermute | solution.py:363
  28.4 3.3 %collective-permute-start.2 = (bf16[512,384]{1,0:T(8,128)(2,1)}, bf16[512,384]{1,0:T(8,128)(2,1)S(1)}, u32[]{:S(2)}, u32[]{:S(2)}) collective-permute-start(bf16[512,384]{1,0:T(8,128)(2,1)} %shard_map.121.refs_2_), channel_id=1, source_target_pairs={{0,64},{16,80},{32,96},{48,112},{64,128},{80,144},{96,160},{112,17... | collective-permute-start | bytes 1179656 | tf_op jit(solution)/shard_map/ppermute | solution.py:363
  31.7 0.0 copy-start.3
  31.8 10.2 %shard_map.120 = (f32[3,192,384]{2,1,0:T(8,128)}, bf16[16,112,128]{2,1,0:T(8,128)(2,1)}) custom-call(bf16[400,384]{1,0:T(8,128)(2,1)} %copy-done.2, f32[2,192,384]{2,1,0:T(8,128)} %refs_4_.5, f32[2,192,384]{2,1,0:T(8,128)} %refs_5_.3, f32[2,192,384]{2,1,0:T(8,128)} %bitcast.6, f32[1,2]{1,0:T(1,128)} %bitcast.11, ...), custom_call_target="tpu_custom_call" | custom-call | flops 6000000000 | bytes 4000000 | tf_op jit(solution)/shard_map/pallas_call | solution.py:65
  41.9 0.0 copy-start.4
  41.9 0.0 copy-start.5
  41.9 0.0 collective-permute-done.1.refs_4_
  42.0 0.0 copy-start.6
  42.0 0.0 collective-permute-done.2.refs_6_
  42.0 0.0 copy-start.7
  42.0 9.8 %all-to-all-start = ((bf16[16,112,128]{2,1,0:T(8,128)(2,1)}), bf16[16,112,128]{2,1,0:T(8,128)(2,1)S(1)}, u32[]{:S(2)}, u32[]{:S(2)}) async-start(bf16[16,112,128]{2,1,0:T(8,128)(2,1)} %get-tuple-element.15), calls=%async_computation | async-start | bytes 917504 | tf_op jit(solution)/shard_map/all_to_all | solution.py:375
  51.8 0.0 copy-done.3
  51.8 3.3 %collective-permute-start.3 = (bf16[512,384]{1,0:T(8,128)(2,1)S(1)}, bf16[512,384]{1,0:T(8,128)(2,1)S(1)}, u32[]{:S(2)}, u32[]{:S(2)}) collective-permute-start(bf16[512,384]{1,0:T(8,128)(2,1)S(1)} %copy-done.3), channel_id=1, source_target_pairs={{0,16},{16,32},{32,48},{48,64},{64,80},{80,96},{96,112},{112,128},... | collective-permute-start | bytes 1179656 | tf_op jit(solution)/shard_map/ppermute | solution.py:363
  55.1 4.3 %collective-permute-start.4 = (bf16[512,384]{1,0:T(8,128)(2,1)S(1)}, bf16[512,384]{1,0:T(8,128)(2,1)S(1)}, u32[]{:S(2)}, u32[]{:S(2)}) collective-permute-start(bf16[512,384]{1,0:T(8,128)(2,1)S(1)} %copy-done.3), channel_id=1, source_target_pairs={{0,48},{16,64},{32,80},{48,96},{64,112},{80,128},{96,144},{112,160... | collective-permute-start | bytes 1179656 | tf_op jit(solution)/shard_map/ppermute | solution.py:363
  59.4 1.0 all-to-all-done.refs_0_
  60.4 1.2 shard_map.122
  61.6 4.0 %all-to-all-start.1 = ((bf16[16,112,128]{2,1,0:T(8,128)(2,1)}), bf16[16,112,128]{2,1,0:T(8,128)(2,1)S(1)}, u32[]{:S(2)}, u32[]{:S(2)}) async-start(bf16[16,112,128]{2,1,0:T(8,128)(2,1)} %shard_map.122), calls=%async_computation.1 | async-start | bytes 917504 | tf_op jit(solution)/shard_map/all_to_all | solution.py:377
  65.6 0.0 copy-done.4
  65.6 0.6 reshape.14.refs_7_
  66.2 0.0 copy-done.5
  66.2 0.6 reshape.13.refs_7_
  66.8 0.0 collective-permute-done.3.refs_3_
  66.8 0.0 copy-start.8
  66.8 0.0 collective-permute-done.4.refs_5_
  66.8 0.0 copy-done.6
  66.8 0.0 copy-done.7
  66.8 0.7 copy-done.8
  67.5 0.0 copy-start.9
  67.5 0.8 copy-done.9
  68.3 5.4 %shard_map.123.refs_8_ = f32[2,256,192]{2,1,0:T(8,128)} custom-call(bf16[400,384]{1,0:T(8,128)(2,1)} %get-tuple-element.12.refs_5_.refs_0_.refs_2_, bf16[400,384]{1,0:T(8,128)(2,1)} %copy-done.2, bf16[512,384]{1,0:T(8,128)(2,1)} %shard_map.121.refs_2_, bf16[512,384]{1,0:T(8,128)(2,1)} %copy-done.8, bf16[512,384]{1,0:T(8,128)(2,1)} %copy-done.6, ...), custom_call_target="tpu_custom_call" | custom-call | flops 1000000000 | bytes 3000000 | tf_op jit(solution)/shard_map/pallas_call | solution.py:65
  73.7 8.6 %all-to-all-done.1.refs_0_ = bf16[16,112,128]{2,1,0:T(8,128)(2,1)S(1)} async-done(((bf16[16,112,128]{2,1,0:T(8,128)(2,1)}), bf16[16,112,128]{2,1,0:T(8,128)(2,1)S(1)}, u32[]{:S(2)}, u32[]{:S(2)}) %all-to-all-start.1) | async-done | bytes 458784 | tf_op jit(solution)/shard_map/all_to_all | solution.py:377
  82.3 0.0 copy-start.1
  82.3 0.8 copy-done.1
  83.1 0.0 copy-start
  83.1 4.7 %shard_map.124 = bf16[4,64,384]{2,1,0:T(8,128)(2,1)} custom-call(bf16[16,112,128]{2,1,0:T(8,128)(2,1)} %copy-done.1, f32[3,192,384]{2,1,0:T(8,128)} %get-tuple-element.16.refs_1_, bf16[400,384]{1,0:T(8,128)(2,1)} %get-tuple-element.12.refs_5_.refs_0_.refs_2_, bf16[400,384]{1,0:T(8,128)(2,1)} %copy-done.2, f32[2,192,384]{2,1,0:T(8,128)} %refs_4_.5, ...), custom_call_target="tpu_custom_call" | custom-call | flops 600000000 | bytes 5000000 | tf_op jit(solution)/shard_map/pallas_call | solution.py:65
  87.8 14.8 %all_to_all.20.mix_ref = bf16[4,64,384]{2,1,0:T(8,128)(2,1)S(1)} all-to-all(bf16[4,64,384]{2,1,0:T(8,128)(2,1)} %shard_map.124), channel_id=1, replica_groups=mesh['x'=4,'y'=4,'zh'=2,'zl'=4,'c'=2] {'c','zh'}, dimensions={0} | all-to-all | bytes 393216 | tf_op jit(solution)/shard_map/all_to_all | solution.py:396
  102.5 0.0 collective-permute-done.5.other_ref
  102.6 0.0 copy-done
  102.6 4.6 %shard_map.125 = bf16[128,3072]{1,0:T(8,128)(2,1)S(1)} custom-call(bf16[4,64,384]{2,1,0:T(8,128)(2,1)S(1)} %all_to_all.20.mix_ref, bf16[384,3072]{1,0:T(8,128)(2,1)S(1)} %copy-done, bf16[384,3072]{1,0:T(8,128)(2,1)} %collective-permute-done.5.other_ref), custom_call_target="tpu_custom_call" | custom-call | flops 600000000 | bytes 6000000 | tf_op jit(solution)/shard_map/pallas_call | solution.py:398
  107.1 30.3 %all_to_all.21.refs_0_ = bf16[4,32,3072]{2,1,0:T(8,128)(2,1)S(1)} all-to-all(bf16[4,32,3072]{2,1,0:T(8,128)(2,1)S(1)} %bitcast.4), channel_id=1, replica_groups=mesh['x'=4,'y'=4,'zh'=2,'zl'=4,'c'=2] {'zl'}, dimensions={0} | all-to-all | bytes 1572864 | tf_op jit(solution)/shard_map/all_to_all | solution.py:411
  137.4 0.8 shard_map.126
Async XLA Ops:
  0.0 102.6 %collective-permute-start.5 = (bf16[384,3072]{1,0:T(8,128)(2,1)}, bf16[384,3072]{1,0:T(8,128)(2,1)}, u32[]{:S(2)}, u32[]{:S(2)}) collective-permute-start(bf16[384,3072]{1,0:T(8,128)(2,1)} %own_ref.1), channel_id=1, source_target_pairs={{0,1},{1,0},{2,3},{3,2},{4,5},{5,4},{6,7},{7,6},{8,9},{9,8},{10,11... | collective-permute-start | bytes 7077896 | tf_op jit(solution)/shard_map/ppermute | solution.py:350
  5.4 15.5 %collective-permute-start = (bf16[400,384]{1,0:T(8,128)(2,1)}, bf16[400,384]{1,0:T(8,128)(2,1)S(1)}, u32[]{:S(2)}, u32[]{:S(2)}) collective-permute-start(bf16[400,384]{1,0:T(8,128)(2,1)} %shard_map.118), channel_id=1, source_target_pairs={{0,8},{8,0},{1,9},{9,1},{2,10},{10,2},{3,11},{11,3},{4,12},{12,4},... | collective-permute-start | bytes 921608 | tf_op jit(solution)/shard_map/ppermute | solution.py:349
  21.0 0.7 copy-start.2
  23.6 18.4 %collective-permute-start.1 = (bf16[512,384]{1,0:T(8,128)(2,1)}, bf16[512,384]{1,0:T(8,128)(2,1)S(1)}, u32[]{:S(2)}, u32[]{:S(2)}) collective-permute-start(bf16[512,384]{1,0:T(8,128)(2,1)} %shard_map.121.refs_2_), channel_id=1, source_target_pairs={{0,32},{16,48},{32,64},{48,80},{64,96},{80,112},{96,128},{112,144}... | collective-permute-start | bytes 1179656 | tf_op jit(solution)/shard_map/ppermute | solution.py:363
  28.4 13.5 %collective-permute-start.2 = (bf16[512,384]{1,0:T(8,128)(2,1)}, bf16[512,384]{1,0:T(8,128)(2,1)S(1)}, u32[]{:S(2)}, u32[]{:S(2)}) collective-permute-start(bf16[512,384]{1,0:T(8,128)(2,1)} %shard_map.121.refs_2_), channel_id=1, source_target_pairs={{0,64},{16,80},{32,96},{48,112},{64,128},{80,144},{96,160},{112,17... | collective-permute-start | bytes 1179656 | tf_op jit(solution)/shard_map/ppermute | solution.py:363
  31.7 20.1 %copy-start.3 = (bf16[512,384]{1,0:T(8,128)(2,1)S(1)}, bf16[512,384]{1,0:T(8,128)(2,1)}, u32[]{:S(2)}) copy-start(bf16[512,384]{1,0:T(8,128)(2,1)} %shard_map.121.refs_2_) | copy-start | bytes 1179652
  41.9 23.7 %copy-start.4 = (f32[384]{0:T(512)S(1)}, f32[384]{0:T(512)}, u32[]{:S(2)}) copy-start(f32[384]{0:T(512)} %param.22) | copy-start | bytes 4612
  41.9 24.3 %copy-start.5 = (f32[384]{0:T(512)S(1)}, f32[384]{0:T(512)}, u32[]{:S(2)}) copy-start(f32[384]{0:T(512)} %param.21) | copy-start | bytes 4612
  42.0 24.8 %copy-start.6 = (bf16[512,384]{1,0:T(8,128)(2,1)}, bf16[512,384]{1,0:T(8,128)(2,1)S(1)}, u32[]{:S(2)}) copy-start(bf16[512,384]{1,0:T(8,128)(2,1)S(1)} %collective-permute-done.1.refs_4_) | copy-start | bytes 1179652
  42.0 24.8 %copy-start.7 = (bf16[512,384]{1,0:T(8,128)(2,1)}, bf16[512,384]{1,0:T(8,128)(2,1)S(1)}, u32[]{:S(2)}) copy-start(bf16[512,384]{1,0:T(8,128)(2,1)S(1)} %collective-permute-done.2.refs_6_) | copy-start | bytes 1179652
  42.0 18.4 %all-to-all-start = ((bf16[16,112,128]{2,1,0:T(8,128)(2,1)}), bf16[16,112,128]{2,1,0:T(8,128)(2,1)S(1)}, u32[]{:S(2)}, u32[]{:S(2)}) async-start(bf16[16,112,128]{2,1,0:T(8,128)(2,1)} %get-tuple-element.15), calls=%async_computation | async-start | bytes 917504 | tf_op jit(solution)/shard_map/all_to_all | solution.py:375
  51.8 15.0 %collective-permute-start.3 = (bf16[512,384]{1,0:T(8,128)(2,1)S(1)}, bf16[512,384]{1,0:T(8,128)(2,1)S(1)}, u32[]{:S(2)}, u32[]{:S(2)}) collective-permute-start(bf16[512,384]{1,0:T(8,128)(2,1)S(1)} %copy-done.3), channel_id=1, source_target_pairs={{0,16},{16,32},{32,48},{48,64},{64,80},{80,96},{96,112},{112,128},... | collective-permute-start | bytes 1179656 | tf_op jit(solution)/shard_map/ppermute | solution.py:363
  55.1 11.7 %collective-permute-start.4 = (bf16[512,384]{1,0:T(8,128)(2,1)S(1)}, bf16[512,384]{1,0:T(8,128)(2,1)S(1)}, u32[]{:S(2)}, u32[]{:S(2)}) collective-permute-start(bf16[512,384]{1,0:T(8,128)(2,1)S(1)} %copy-done.3), channel_id=1, source_target_pairs={{0,48},{16,64},{32,80},{48,96},{64,112},{80,128},{96,144},{112,160... | collective-permute-start | bytes 1179656 | tf_op jit(solution)/shard_map/ppermute | solution.py:363
  61.6 20.7 %all-to-all-start.1 = ((bf16[16,112,128]{2,1,0:T(8,128)(2,1)}), bf16[16,112,128]{2,1,0:T(8,128)(2,1)S(1)}, u32[]{:S(2)}, u32[]{:S(2)}) async-start(bf16[16,112,128]{2,1,0:T(8,128)(2,1)} %shard_map.122), calls=%async_computation.1 | async-start | bytes 917504 | tf_op jit(solution)/shard_map/all_to_all | solution.py:377
  66.8 0.7 copy-start.8
  67.5 0.8 copy-start.9
  82.3 0.8 copy-start.1
  83.1 19.5 %copy-start = (bf16[384,3072]{1,0:T(8,128)(2,1)S(1)}, bf16[384,3072]{1,0:T(8,128)(2,1)}, u32[]{:S(2)}) copy-start(bf16[384,3072]{1,0:T(8,128)(2,1)} %own_ref.1) | copy-start | bytes 7077892

commit v4 on v3

--- a/solution.py
+++ b/solution.py
@@ -241,47 +241,89 @@
             run = keep * run + here
 
 
-def attend_body(own, recv, pair_kv, w1, w2, w3, w4, gain_in, out_ref, score_ref):
+def scores_of(q, keys, blocks, score_ref, rows_of, pair):
+    row = lax.broadcasted_iota(jnp.int32, (BLK, BLK), 0)
+    col = lax.broadcasted_iota(jnp.int32, (BLK, BLK), 1)
+    top = None
+    for n, (o, e, kind) in enumerate(blocks):
+        s = nt(q, keys[o][rows_of(e), 0:HD]) * (1.0 / math.sqrt(HD))
+        if kind == "oldest":
+            s = jnp.where(col > row, s, -1e30)
+        if kind == "newest":
+            s = jnp.where(col <= row, s, -1e30)
+        if o > 0:
+            s = s + jnp.where(pair >= o, 0.0, -1e30)
+        score_ref[n] = s
+        top = s if top is None else jnp.maximum(top, s)
+    return jnp.max(top, axis=1, keepdims=True)
+
+
+def weighted(values, blocks, score_ref, rows_of, top):
+    total = None
+    acc = None
+    for n, (o, e, _) in enumerate(blocks):
+        w = jnp.exp(score_ref[n] - top)
+        total = w if total is None else total + w
+        part = nn(w.astype(BF16), values[o][rows_of(e), HD:])
+        acc = part if acc is None else acc + part
+    return jnp.sum(total, axis=1, keepdims=True), acc
+
+
+def window_blocks(parity, offsets):
+    blocks = [(o, e) for o in (4, 3, 2, 1, 0) for e in (0, 1)][parity : parity + 9]
+    kinds = ["oldest"] + ["inner"] * 7 + ["newest"]
+    return [(o, e, kind) for (o, e), kind in zip(blocks, kinds) if o in offsets]
+
+
+def ordered_rows(zh):
+    def rows_of(parity):
+        slot = zh if parity == 0 else 1 - zh
+        return pl.ds(pl.multiple_of(slot * BLK, BLK), BLK)
+
+    return rows_of
+
+
+def pair_index():
+    return lax.axis_index("x") * 4 + lax.axis_index("y")
+
+
+def attend_first_body(own, recv, pair_kv, w2, w4, acc_ref, stat_ref, score_ref):
     zh = lax.axis_index("zh")
-    pair = lax.axis_index("x") * 4 + lax.axis_index("y")
-    scale = 1.0 / math.sqrt(HD)
+    q_own = queries(own.get())
+    q_recv = queries(recv.get())
+    wins = {0: pair_kv.get(), 2: w2.get(), 4: w4.get()}
+    rows_of = ordered_rows(zh)
+    lane = lax.broadcasted_iota(jnp.int32, (BLK, 128), 1)
+    for parity in range(2):
+        q = jnp.where(zh == parity, q_own, q_recv)
+        blocks = window_blocks(parity, wins)
+        scores = score_ref.at[parity]
+        top = scores_of(q, wins, blocks, scores, rows_of, pair_index())
+        total, acc = weighted(wins, blocks, scores, rows_of, top)
+        acc_ref[parity] = acc
+        stat_ref[parity] = jnp.where(lane < 64, top, total)
+
+
+def attend_second_body(own, recv, w1, w3, acc_in, stat, gain_in, out_ref, score_ref):
+    zh = lax.axis_index("zh")
     q_own = queries(own.get())
     q_recv = queries(recv.get())
     gain_ref = gain_in.get()
-    wins = [w.get() for w in (pair_kv, w1, w2, w3, w4)]
+    wins = {1: w1.get(), 3: w3.get()}
     gain = jnp.where(zh == 0, gain_ref[:, :HD], gain_ref[:, HD:])
-    row = lax.broadcasted_iota(jnp.int32, (BLK, BLK), 0)
-    col = lax.broadcasted_iota(jnp.int32, (BLK, BLK), 1)
-
-    def rows_of(parity):
-        slot = zh if parity == 0 else 1 - zh
-        return pl.ds(pl.multiple_of(slot * BLK, BLK), BLK)
-
+    rows_of = ordered_rows(zh)
+    stats = stat.get()
+    before = acc_in.get()
     for parity in range(2):
         q = jnp.where(zh == parity, q_own, q_recv)
-        blocks = [(o, e) for o in (4, 3, 2, 1, 0) for e in (0, 1)]
-        blocks = blocks[:9] if parity == 0 else blocks[1:]
-        top = None
-        for n, (o, e) in enumerate(blocks):
-            k = wins[o][rows_of(e), 0:HD]
-            s = nt(q, k) * scale
-            if n == 0:
-                s = jnp.where(col > row, s, -1e30)
-            if n == 8:
-                s = jnp.where(col <= row, s, -1e30)
-            if o > 0:
-                s = s + jnp.where(pair >= o, 0.0, -1e30)
-            score_ref[n] = s
-            top = s if top is None else jnp.maximum(top, s)
-        top = jnp.max(top, axis=1, keepdims=True)
-        total = None
-        acc = None
-        for n, (o, e) in enumerate(blocks):
-            w = jnp.exp(score_ref[n] - top)
-            total = w if total is None else total + w
-            part = nn(w.astype(BF16), wins[o][rows_of(e), HD:])
-            acc = part if acc is None else acc + part
-        att = acc / jnp.sum(total, axis=1, keepdims=True)
+        blocks = window_blocks(parity, wins)
+        scores = score_ref.at[parity]
+        old_top = stats[parity, :, 0:1]
+        top = jnp.maximum(old_top, scores_of(q, wins, blocks, scores, rows_of, pair_index()))
+        total, acc = weighted(wins, blocks, scores, rows_of, top)
+        rescale = jnp.exp(old_top - top)
+        total = total + rescale * stats[parity, :, 64:65]
+        att = (acc + rescale * before[parity]) / total
         norm = lax.rsqrt(jnp.mean(att * att, axis=1, keepdims=True) + 1e-6)
         out_ref[parity] = att * norm * gain
 
@@ -371,18 +413,27 @@
         scratch=[flat],
         mine=(1, 2, 3),
     )
-    outgoing, wins[1], wins[3] = lax.optimization_barrier((outgoing, wins[1], wins[3]))
     pieces = lax.all_to_all(outgoing, ("x", "y"), 0, 0, tiled=True)
+    acc, stat = call(
+        attend_first_body,
+        [sds((2, BLK, HD), F32), sds((2, BLK, 128), F32)],
+        (own, recv, pair_kv, wins[1], wins[3]),
+        30000000000,
+        2_000_000,
+        600_000,
+        scratch=[pltpu.VMEM((2, 5, BLK, BLK), F32)],
+    )
+    pieces, acc = lax.optimization_barrier((pieces, acc))
     (sums,) = call(scan_body, [sds((PAIRS, CROWS, 128), BF16)], (pieces,), 500_000, 1_000_000, cap=SMALL)
     prefix = lax.all_to_all(sums, ("x", "y"), 0, 0, tiled=True)
     (att,) = call(
-        attend_body,
+        attend_second_body,
         [sds((2, BLK, HD), F32)],
-        (own, recv, pair_kv, *wins, attn_gain.reshape(1, FD)),
-        1_000_000_000,
-        3_000_000,
-        1_200_000,
-        scratch=[pltpu.VMEM((9, BLK, BLK), F32)],
+        (own, recv, wins[0], wins[2], acc, stat, attn_gain.reshape(1, FD)),
+        500_000_000,
+        2_000_000,
+        600_000,
+        scratch=[pltpu.VMEM((2, 4, BLK, BLK), F32)],
     )
     (mixed,) = call(
         apply_body,

time: 140 us -> 141 us (level)
  waiting for transfers between devices: 9.6 us -> 16.5 us
  starting transfers between devices: 38.1 us -> 31.7 us
  blocking collectives: 45 us -> 42.2 us
  Pallas kernels: 41.1 us -> 43.8 us
    all_to_all x1, waiting for transfers between devices: 0.99 us -> 14.3 us  [local(): pieces = lax.all_to_all(outgoing, ('x', 'y'), 0, 0, tiled=True)]
    all_to_all x1, waiting for transfers between devices: 8.6 us -> 2.26 us  [local(): prefix = lax.all_to_all(sums, ('x', 'y'), 0, 0, tiled=True)]
    all_to_all x1, starting transfers between devices: 9.81 us -> 3.57 us  [local(): pieces = lax.all_to_all(outgoing, ('x', 'y'), 0, 0, tiled=True)]
    all_to_all x1, blocking collectives: 30.3 us -> 27.3 us  [local(): lax.all_to_all(partial.reshape(4, 32, WIDTH), 'zl', 0, 0, tiled=True)]
    pallas_call x8 -> x9, Pallas kernels: 36.6 us -> 39.3 us  [call(): pl.pallas_call(kernel, out_shape=outs, in_specs=[any_spec] * n_in, out_sp...]
    ppermute x1, starting transfers between devices: 5.26 us -> 7.83 us  [local(): recv = lax.ppermute(send, 'zh', [(0, 1), (1, 0)])]
    ppermute x1, starting transfers between devices: 3.24 us -> 0.96 us  [local(): proj_other = lax.ppermute(proj, 'c', [(0, 1), (1, 0)])]
    unnamed x20 -> x18, local copies, waits for them, and re-layouts: 3.03 us -> 3.91 us
where the time goes in v4:
time: 141 us; the launch traced here: 140 us
  Pallas kernels  43.8 us (31%)
  blocking collectives  42.2 us (30%)
  starting transfers between devices  31.7 us (22%)
  waiting for transfers between devices  16.5 us (12%)
  local copies, waits for them, and re-layouts  5.06 us (4%)
    pallas_call x9, Pallas kernels, call(): pl.pallas_call(kernel, out_shape=outs, in_specs=[any_spec] * n_in, out_sp...  39.3 us
    all_to_all x1, blocking collectives, local(): lax.all_to_all(partial.reshape(4, 32, WIDTH), 'zl', 0, 0, tiled=True)  27.3 us
    ppermute x4, starting transfers between devices, local(): lax.ppermute(pair_kv, ('x', 'y'), [(i, i + o) for i in range(PAIRS - o)])  15.6 us
    all_to_all x1, blocking collectives, local(): mixed = lax.all_to_all(mixed, ('c', 'zh'), 0, 0, tiled=True)  14.9 us
    all_to_all x1, waiting for transfers between devices, local(): pieces = lax.all_to_all(outgoing, ('x', 'y'), 0, 0, tiled=True)  14.3 us
    ppermute x1, starting transfers between devices, local(): recv = lax.ppermute(send, 'zh', [(0, 1), (1, 0)])  7.83 us
    pallas_call x1, Pallas kernels, local(): pl.pallas_call(project_body, out_shape=sds((128, WIDTH), BF16), grid=(WID...  4.57 us
    unnamed x18, local copies, waits for them, and re-layouts  3.91 us
  transfers between devices with their start and end apart: 8, of which 2 were waited for; matrix products, arithmetic and copies ran while one was open for 1% of the time, Pallas kernels for 26%

profile of v4, /device:TPU:1, one launch (start us, length us, event | category | flops | bytes accessed | tf_op | source)
XLA Modules:
  0.0 139.8 jit_solution(3227784022511982834)
XLA Ops:
  0.0 2.2 %shard_map.118 = bf16[400,384]{1,0:T(8,128)(2,1)} custom-call(bf16[256,384]{1,0:T(8,128)(2,1)} %refs_0_.3, bf16[256,384]{1,0:T(8,128)(2,1)} %refs_1_.4, bf16[256,384]{1,0:T(8,128)(2,1)} %refs_2_.4, f32[2,256]{1,0:T(2,128)} %bitcast.8, f32[1,2]{1,0:T(1,128)} %refs_4_.4), custom_call_target="tpu_custom_call" | custom-call | bytes 1000000 | tf_op jit(solution)/shard_map/pallas_call | solution.py:65
  2.2 7.8 %collective-permute-start = (bf16[400,384]{1,0:T(8,128)(2,1)}, bf16[400,384]{1,0:T(8,128)(2,1)S(1)}, u32[]{:S(2)}, u32[]{:S(2)}) collective-permute-start(bf16[400,384]{1,0:T(8,128)(2,1)} %shard_map.118), channel_id=1, source_target_pairs={{0,8},{8,0},{1,9},{9,1},{2,10},{10,2},{3,11},{11,3},{4,12},{12,4},... | collective-permute-start | bytes 921608 | tf_op jit(solution)/shard_map/ppermute | solution.py:391
  10.0 1.0 collective-permute-start.5
  11.0 10.3 %shard_map.119 = (f32[3,192,384]{2,1,0:T(8,128)}, bf16[400,384]{1,0:T(8,128)(2,1)}) custom-call(bf16[256,384]{1,0:T(8,128)(2,1)} %refs_0_.3, bf16[256,384]{1,0:T(8,128)(2,1)} %refs_1_.4, bf16[256,384]{1,0:T(8,128)(2,1)} %refs_2_.4, f32[2,256]{1,0:T(2,128)} %bitcast.9, f32[1,2]{1,0:T(1,128)} %refs_4_.4, f32[2,192,384]{2,1,0:T(8,128)} %refs_4_.5, ...), custom_call_target="tpu_custom_call" | custom-call | flops 6000000000 | bytes 3000000 | tf_op jit(solution)/shard_map/pallas_call | solution.py:65
  21.2 0.0 collective-permute-done.refs_0_.refs_1_.refs_3_
  21.3 0.0 copy-start.1
  21.3 0.7 copy-done.1
  22.0 1.8 %shard_map.121.refs_2_ = bf16[512,384]{1,0:T(8,128)(2,1)} custom-call(bf16[400,384]{1,0:T(8,128)(2,1)} %get-tuple-element.13.refs_5_.refs_0_.refs_2_, bf16[400,384]{1,0:T(8,128)(2,1)} %copy-done.1), custom_call_target="tpu_custom_call" | custom-call | bytes 800000 | tf_op jit(solution)/shard_map/pallas_call | solution.py:65
  23.8 4.8 %collective-permute-start.1 = (bf16[512,384]{1,0:T(8,128)(2,1)}, bf16[512,384]{1,0:T(8,128)(2,1)S(1)}, u32[]{:S(2)}, u32[]{:S(2)}) collective-permute-start(bf16[512,384]{1,0:T(8,128)(2,1)} %shard_map.121.refs_2_), channel_id=1, source_target_pairs={{0,32},{16,48},{32,64},{48,80},{64,96},{80,112},{96,128},{112,144}... | collective-permute-start | bytes 1179656 | tf_op jit(solution)/shard_map/ppermute | solution.py:405
  28.7 3.1 %collective-permute-start.2 = (bf16[512,384]{1,0:T(8,128)(2,1)}, bf16[512,384]{1,0:T(8,128)(2,1)S(1)}, u32[]{:S(2)}, u32[]{:S(2)}) collective-permute-start(bf16[512,384]{1,0:T(8,128)(2,1)} %shard_map.121.refs_2_), channel_id=1, source_target_pairs={{0,64},{16,80},{32,96},{48,112},{64,128},{80,144},{96,160},{112,17... | collective-permute-start | bytes 1179656 | tf_op jit(solution)/shard_map/ppermute | solution.py:405
  31.8 2.3 %collective-permute-start.3 = (bf16[512,384]{1,0:T(8,128)(2,1)}, bf16[512,384]{1,0:T(8,128)(2,1)S(1)}, u32[]{:S(2)}, u32[]{:S(2)}) collective-permute-start(bf16[512,384]{1,0:T(8,128)(2,1)} %shard_map.121.refs_2_), channel_id=1, source_target_pairs={{0,16},{16,32},{32,48},{48,64},{64,80},{80,96},{96,112},{112,128},... | collective-permute-start | bytes 1179656 | tf_op jit(solution)/shard_map/ppermute | solution.py:405
  34.1 5.3 %collective-permute-start.4 = (bf16[512,384]{1,0:T(8,128)(2,1)}, bf16[512,384]{1,0:T(8,128)(2,1)S(1)}, u32[]{:S(2)}, u32[]{:S(2)}) collective-permute-start(bf16[512,384]{1,0:T(8,128)(2,1)} %shard_map.121.refs_2_), channel_id=1, source_target_pairs={{0,48},{16,64},{32,80},{48,96},{64,112},{80,128},{96,144},{112,160... | collective-permute-start | bytes 1179656 | tf_op jit(solution)/shard_map/ppermute | solution.py:405
  39.4 10.1 %shard_map.120 = (f32[3,192,384]{2,1,0:T(8,128)}, bf16[16,112,128]{2,1,0:T(8,128)(2,1)}) custom-call(bf16[400,384]{1,0:T(8,128)(2,1)} %copy-done.1, f32[2,192,384]{2,1,0:T(8,128)} %refs_4_.5, f32[2,192,384]{2,1,0:T(8,128)} %refs_5_.3, f32[2,192,384]{2,1,0:T(8,128)} %bitcast.6, f32[1,2]{1,0:T(1,128)} %bitcast.11, ...), custom_call_target="tpu_custom_call" | custom-call | flops 6000000000 | bytes 4000000 | tf_op jit(solution)/shard_map/pallas_call | solution.py:65
  49.6 3.6 %all-to-all-start = ((bf16[16,112,128]{2,1,0:T(8,128)(2,1)}), bf16[16,112,128]{2,1,0:T(8,128)(2,1)S(1)}, u32[]{:S(2)}, u32[]{:S(2)}) async-start(bf16[16,112,128]{2,1,0:T(8,128)(2,1)} %get-tuple-element.15), calls=%async_computation | async-start | bytes 917504 | tf_op jit(solution)/shard_map/all_to_all | solution.py:416
  53.1 0.0 copy-start.5
  53.2 0.0 copy-start.6
  53.2 0.0 collective-permute-done.1.refs_3_
  53.2 0.0 copy-start.7
  53.2 0.0 collective-permute-done.2.refs_4_
  53.2 0.7 copy-done.7
  53.9 0.0 copy-start.8
  53.9 0.7 copy-done.8
  54.7 4.0 %shard_map.122 = (f32[2,256,192]{2,1,0:T(8,128)}, f32[2,256,128]{2,1,0:T(8,128)}) custom-call(bf16[400,384]{1,0:T(8,128)(2,1)} %get-tuple-element.13.refs_5_.refs_0_.refs_2_, bf16[400,384]{1,0:T(8,128)(2,1)} %copy-done.1, bf16[512,384]{1,0:T(8,128)(2,1)} %shard_map.121.refs_2_, bf16[512,384]{1,0:T(8,128)(2,1)} %copy-done.7, bf16[512,384]{1,0:T(8,128)(2,1)} %copy-done.8), custom_call_target="tpu_custom_call" | custom-call | flops 30000001024 | bytes 2000000 | tf_op jit(solution)/shard_map/pallas_call | solution.py:65
  58.7 14.3 %all-to-all-done.refs_0_ = bf16[16,112,128]{2,1,0:T(8,128)(2,1)S(1)} async-done(((bf16[16,112,128]{2,1,0:T(8,128)(2,1)}), bf16[16,112,128]{2,1,0:T(8,128)(2,1)S(1)}, u32[]{:S(2)}, u32[]{:S(2)}) %all-to-all-start) | async-done | bytes 458784 | tf_op jit(solution)/shard_map/all_to_all | solution.py:416
  72.9 1.2 shard_map.123
  74.1 3.8 %all-to-all-start.1 = ((bf16[16,112,128]{2,1,0:T(8,128)(2,1)}), bf16[16,112,128]{2,1,0:T(8,128)(2,1)S(1)}, u32[]{:S(2)}, u32[]{:S(2)}) async-start(bf16[16,112,128]{2,1,0:T(8,128)(2,1)} %shard_map.123), calls=%async_computation.1 | async-start | bytes 917504 | tf_op jit(solution)/shard_map/all_to_all | solution.py:428
  77.9 0.0 copy-done.5
  77.9 0.6 reshape.14.refs_6_
  78.5 0.0 copy-done.6
  78.5 0.6 reshape.13.refs_7_
  79.1 0.0 collective-permute-done.3.refs_2_
  79.1 0.0 copy-start.3
  79.1 0.0 collective-permute-done.4.refs_3_
  79.1 0.0 copy-start.4
  79.1 0.7 copy-done.3
  79.8 0.2 copy-done.4
  80.0 4.2 %shard_map.124.refs_8_ = f32[2,256,192]{2,1,0:T(8,128)} custom-call(bf16[400,384]{1,0:T(8,128)(2,1)} %get-tuple-element.13.refs_5_.refs_0_.refs_2_, bf16[400,384]{1,0:T(8,128)(2,1)} %copy-done.1, bf16[512,384]{1,0:T(8,128)(2,1)} %copy-done.3, bf16[512,384]{1,0:T(8,128)(2,1)} %copy-done.4, f32[2,256,192]{2,1,0:T(8,128)} %get-tuple-element.19.refs_4_, ...), custom_call_target="tpu_custom_call" | custom-call | flops 500000000 | bytes 2000000 | tf_op jit(solution)/shard_map/pallas_call | solution.py:65
  84.2 2.3 %all-to-all-done.1.refs_0_ = bf16[16,112,128]{2,1,0:T(8,128)(2,1)S(1)} async-done(((bf16[16,112,128]{2,1,0:T(8,128)(2,1)}), bf16[16,112,128]{2,1,0:T(8,128)(2,1)S(1)}, u32[]{:S(2)}, u32[]{:S(2)}) %all-to-all-start.1) | async-done | bytes 458784 | tf_op jit(solution)/shard_map/all_to_all | solution.py:428
  86.5 0.0 copy-start.2
  86.5 0.8 copy-done.2
  87.3 0.0 copy-start
  87.3 4.7 %shard_map.125 = bf16[4,64,384]{2,1,0:T(8,128)(2,1)} custom-call(bf16[16,112,128]{2,1,0:T(8,128)(2,1)} %copy-done.2, f32[3,192,384]{2,1,0:T(8,128)} %get-tuple-element.18.refs_1_, bf16[400,384]{1,0:T(8,128)(2,1)} %get-tuple-element.13.refs_5_.refs_0_.refs_2_, bf16[400,384]{1,0:T(8,128)(2,1)} %copy-done.1, f32[2,192,384]{2,1,0:T(8,128)} %refs_4_.5, ...), custom_call_target="tpu_custom_call" | custom-call | flops 600000000 | bytes 5000000 | tf_op jit(solution)/shard_map/pallas_call | solution.py:65
  92.0 14.9 %all_to_all.20.mix_ref = bf16[4,64,384]{2,1,0:T(8,128)(2,1)S(1)} all-to-all(bf16[4,64,384]{2,1,0:T(8,128)(2,1)} %shard_map.125), channel_id=1, replica_groups=mesh['x'=4,'y'=4,'zh'=2,'zl'=4,'c'=2] {'c','zh'}, dimensions={0} | all-to-all | bytes 393216 | tf_op jit(solution)/shard_map/all_to_all | solution.py:447
  106.9 0.0 collective-permute-done.5.other_ref
  106.9 0.0 copy-done
  106.9 4.6 %shard_map.126 = bf16[128,3072]{1,0:T(8,128)(2,1)S(1)} custom-call(bf16[4,64,384]{2,1,0:T(8,128)(2,1)S(1)} %all_to_all.20.mix_ref, bf16[384,3072]{1,0:T(8,128)(2,1)S(1)} %copy-done, bf16[384,3072]{1,0:T(8,128)(2,1)} %collective-permute-done.5.other_ref), custom_call_target="tpu_custom_call" | custom-call | flops 600000000 | bytes 6000000 | tf_op jit(solution)/shard_map/pallas_call | solution.py:449
  111.4 27.3 %all_to_all.21.refs_0_ = bf16[4,32,3072]{2,1,0:T(8,128)(2,1)S(1)} all-to-all(bf16[4,32,3072]{2,1,0:T(8,128)(2,1)S(1)} %bitcast.4), channel_id=1, replica_groups=mesh['x'=4,'y'=4,'zh'=2,'zl'=4,'c'=2] {'zl'}, dimensions={0} | all-to-all | bytes 1572864 | tf_op jit(solution)/shard_map/all_to_all | solution.py:462
  138.8 0.8 shard_map.127
Async XLA Ops:
  2.2 19.1 %collective-permute-start = (bf16[400,384]{1,0:T(8,128)(2,1)}, bf16[400,384]{1,0:T(8,128)(2,1)S(1)}, u32[]{:S(2)}, u32[]{:S(2)}) collective-permute-start(bf16[400,384]{1,0:T(8,128)(2,1)} %shard_map.118), channel_id=1, source_target_pairs={{0,8},{8,0},{1,9},{9,1},{2,10},{10,2},{3,11},{11,3},{4,12},{12,4},... | collective-permute-start | bytes 921608 | tf_op jit(solution)/shard_map/ppermute | solution.py:391
  10.0 96.8 %collective-permute-start.5 = (bf16[384,3072]{1,0:T(8,128)(2,1)}, bf16[384,3072]{1,0:T(8,128)(2,1)}, u32[]{:S(2)}, u32[]{:S(2)}) collective-permute-start(bf16[384,3072]{1,0:T(8,128)(2,1)} %own_ref.1), channel_id=1, source_target_pairs={{0,1},{1,0},{2,3},{3,2},{4,5},{5,4},{6,7},{7,6},{8,9},{9,8},{10,11... | collective-permute-start | bytes 7077896 | tf_op jit(solution)/shard_map/ppermute | solution.py:392
  21.3 0.7 copy-start.1
  23.8 29.3 %collective-permute-start.1 = (bf16[512,384]{1,0:T(8,128)(2,1)}, bf16[512,384]{1,0:T(8,128)(2,1)S(1)}, u32[]{:S(2)}, u32[]{:S(2)}) collective-permute-start(bf16[512,384]{1,0:T(8,128)(2,1)} %shard_map.121.refs_2_), channel_id=1, source_target_pairs={{0,32},{16,48},{32,64},{48,80},{64,96},{80,112},{96,128},{112,144}... | collective-permute-start | bytes 1179656 | tf_op jit(solution)/shard_map/ppermute | solution.py:405
  28.7 24.5 %collective-permute-start.2 = (bf16[512,384]{1,0:T(8,128)(2,1)}, bf16[512,384]{1,0:T(8,128)(2,1)S(1)}, u32[]{:S(2)}, u32[]{:S(2)}) collective-permute-start(bf16[512,384]{1,0:T(8,128)(2,1)} %shard_map.121.refs_2_), channel_id=1, source_target_pairs={{0,64},{16,80},{32,96},{48,112},{64,128},{80,144},{96,160},{112,17... | collective-permute-start | bytes 1179656 | tf_op jit(solution)/shard_map/ppermute | solution.py:405
  31.8 47.3 %collective-permute-start.3 = (bf16[512,384]{1,0:T(8,128)(2,1)}, bf16[512,384]{1,0:T(8,128)(2,1)S(1)}, u32[]{:S(2)}, u32[]{:S(2)}) collective-permute-start(bf16[512,384]{1,0:T(8,128)(2,1)} %shard_map.121.refs_2_), channel_id=1, source_target_pairs={{0,16},{16,32},{32,48},{48,64},{64,80},{80,96},{96,112},{112,128},... | collective-permute-start | bytes 1179656 | tf_op jit(solution)/shard_map/ppermute | solution.py:405
  34.1 45.0 %collective-permute-start.4 = (bf16[512,384]{1,0:T(8,128)(2,1)}, bf16[512,384]{1,0:T(8,128)(2,1)S(1)}, u32[]{:S(2)}, u32[]{:S(2)}) collective-permute-start(bf16[512,384]{1,0:T(8,128)(2,1)} %shard_map.121.refs_2_), channel_id=1, source_target_pairs={{0,48},{16,64},{32,80},{48,96},{64,112},{80,128},{96,144},{112,160... | collective-permute-start | bytes 1179656 | tf_op jit(solution)/shard_map/ppermute | solution.py:405
  49.6 23.4 %all-to-all-start = ((bf16[16,112,128]{2,1,0:T(8,128)(2,1)}), bf16[16,112,128]{2,1,0:T(8,128)(2,1)S(1)}, u32[]{:S(2)}, u32[]{:S(2)}) async-start(bf16[16,112,128]{2,1,0:T(8,128)(2,1)} %get-tuple-element.15), calls=%async_computation | async-start | bytes 917504 | tf_op jit(solution)/shard_map/all_to_all | solution.py:416
  53.1 24.8 %copy-start.5 = (f32[384]{0:T(512)S(1)}, f32[384]{0:T(512)}, u32[]{:S(2)}) copy-start(f32[384]{0:T(512)} %param.22) | copy-start | bytes 4612
  53.2 25.4 %copy-start.6 = (f32[384]{0:T(512)S(1)}, f32[384]{0:T(512)}, u32[]{:S(2)}) copy-start(f32[384]{0:T(512)} %param.21) | copy-start | bytes 4612
  53.2 0.8 copy-start.7
  53.9 0.7 copy-start.8
  74.1 12.4 %all-to-all-start.1 = ((bf16[16,112,128]{2,1,0:T(8,128)(2,1)}), bf16[16,112,128]{2,1,0:T(8,128)(2,1)S(1)}, u32[]{:S(2)}, u32[]{:S(2)}) async-start(bf16[16,112,128]{2,1,0:T(8,128)(2,1)} %shard_map.123), calls=%async_computation.1 | async-start | bytes 917504 | tf_op jit(solution)/shard_map/all_to_all | solution.py:428
  79.1 0.7 copy-start.3
  79.1 0.9 copy-start.4
  86.5 0.8 copy-start.2
  87.3 19.6 %copy-start = (bf16[384,3072]{1,0:T(8,128)(2,1)S(1)}, bf16[384,3072]{1,0:T(8,128)(2,1)}, u32[]{:S(2)}) copy-start(bf16[384,3072]{1,0:T(8,128)(2,1)} %own_ref.1) | copy-start | bytes 7077892

commit v5 on v4

--- a/solution.py
+++ b/solution.py
@@ -18,7 +18,7 @@
 PAIRS = 16
 CHUNK = 108
 CROWS = 112
-PAY = 400
+PAY = 272
 COEF = (3.4445, -4.775, 2.0315)
 VMEM_CAP = 60 * 1024 * 1024
 SMALL = 12 * 1024 * 1024
@@ -113,34 +113,37 @@
     return jnp.where(who == 0, row[0:1], row[1:2])
 
 
-def fill(out_ref, q, k, v, rate_row, decay):
+def fill(out_ref, k, v, rate_row, decay):
     out_ref[0:BLK, 0:HD] = k
     out_ref[0:BLK, HD:] = v
-    out_ref[BLK : BLK + 128, 0:HD] = q[0:128]
-    out_ref[BLK : BLK + 128, HD:] = q[128:256]
     row = jnp.concatenate([rate_row, jnp.broadcast_to(decay, (1, 128))], axis=1)
-    out_ref[384:400, :] = three(jnp.broadcast_to(row, (16, FD))).astype(BF16)
-
-
-def pack_body(q, k, v, r, d, send_ref):
+    out_ref[BLK:PAY, :] = three(jnp.broadcast_to(row, (16, FD))).astype(BF16)
+
+
+def fold_queries(out_ref, q):
+    out_ref[:, 0:HD] = q[0:128]
+    out_ref[:, HD:] = q[128:256]
+
+
+def pack_body(k, v, r, d, q, send_ref, query_ref):
     who = 1 - lax.axis_index("zh")
     fill(
         send_ref,
-        pick(q.get(), who),
         pick(k.get(), who),
         pick(v.get(), who),
         one_of(r.get()[...], who),
         jnp.where(who == 0, d.get()[:, 0:1], d.get()[:, 1:2]),
     )
+    fold_queries(query_ref, pick(q.get(), who))
 
 
 def tail(pay_ref):
-    rows = pay_ref[384:400, :].astype(F32)
+    rows = pay_ref[BLK:PAY, :].astype(F32)
     return rows[0:1] + rows[1:2] + rows[2:3]
 
 
-def queries(pay_ref):
-    both = pay_ref[BLK : BLK + 128, :]
+def queries(ref):
+    both = ref[...]
     return jnp.concatenate([both[:, :HD], both[:, HD:]], axis=0)
 
 
@@ -189,14 +192,23 @@
     return [scale * x for x in orthogonalize(grads)]
 
 
-def first_body(q, k, v, r, d, g, u, dt, step, upd_ref, own_ref):
+def first_body(k, v, r, d, g, u, dt, step, q, upd_ref, own_ref, query_ref):
     zh = lax.axis_index("zh")
     key = pick(k.get(), zh)
     value = pick(v.get(), zh)
     rate_row = one_of(r.get()[...], zh)
-    fill(own_ref, pick(q.get(), zh), key, value, rate_row, jnp.where(zh == 0, d.get()[:, 0:1], d.get()[:, 1:2]))
+    fill(own_ref, key, value, rate_row, jnp.where(zh == 0, d.get()[:, 0:1], d.get()[:, 1:2]))
     for i, x in enumerate(fast_updates(key, value, rate_row, g, u, dt, step)):
         upd_ref[i] = x
+    fold_queries(query_ref, pick(q.get(), zh))
+
+
+def relay_body(pair_kv, shifted, two_ref, three_ref):
+    y = lax.axis_index("y")
+    here = pair_kv.get()[...]
+    before = shifted.get()[...]
+    two_ref[...] = jnp.where(y < 2, here, before)
+    three_ref[...] = jnp.where(y < 1, here, before)
 
 
 def join_body(own, recv, out_ref):
@@ -287,11 +299,11 @@
     return lax.axis_index("x") * 4 + lax.axis_index("y")
 
 
-def attend_first_body(own, recv, pair_kv, w2, w4, acc_ref, stat_ref, score_ref):
+def attend_first_body(own, recv, pair_kv, shifted, w1, acc_ref, stat_ref, score_ref):
     zh = lax.axis_index("zh")
     q_own = queries(own.get())
     q_recv = queries(recv.get())
-    wins = {0: pair_kv.get(), 2: w2.get(), 4: w4.get()}
+    wins = {0: pair_kv.get(), 4: shifted.get(), 1: w1.get()}
     rows_of = ordered_rows(zh)
     lane = lax.broadcasted_iota(jnp.int32, (BLK, 128), 1)
     for parity in range(2):
@@ -304,12 +316,12 @@
         stat_ref[parity] = jnp.where(lane < 64, top, total)
 
 
-def attend_second_body(own, recv, w1, w3, acc_in, stat, gain_in, out_ref, score_ref):
+def attend_second_body(own, recv, w2, w3, acc_in, stat, gain_in, out_ref, score_ref):
     zh = lax.axis_index("zh")
     q_own = queries(own.get())
     q_recv = queries(recv.get())
     gain_ref = gain_in.get()
-    wins = {1: w1.get(), 3: w3.get()}
+    wins = {2: w2.get(), 3: w3.get()}
     gain = jnp.where(zh == 0, gain_ref[:, :HD], gain_ref[:, HD:])
     rows_of = ordered_rows(zh)
     stats = stat.get()
@@ -328,7 +340,7 @@
         out_ref[parity] = att * norm * gain
 
 
-def apply_body(pre, even, own, recv, g, u, dt, gain_in, att, out_ref, flat_ref):
+def apply_body(pre, even, own, recv, q_mine, q_theirs, g, u, dt, gain_in, att, out_ref, flat_ref):
     zh = lax.axis_index("zh")
     pre_ref, even_ref, own_ref, recv_ref, gain_ref, att_ref = [
         x.get() for x in (pre, even, own, recv, gain_in, att)
@@ -337,8 +349,8 @@
         flat_ref[c * CHUNK : (c + 1) * CHUNK, :] = pre_ref[c].astype(F32)[0:CHUNK]
     keep = jnp.where(zh == 0, tail(own_ref)[:, BLK : BLK + 1], tail(recv_ref)[:, BLK : BLK + 1])
     gain = jnp.where(zh == 0, gain_ref[:, :HD], gain_ref[:, HD:])
-    q_own = queries(own_ref)
-    q_recv = queries(recv_ref)
+    q_own = queries(q_mine.get())
+    q_recv = queries(q_theirs.get())
     base = [x.get()[...] for x in (g, u, dt)]
     for parity in range(2):
         q = jnp.where(zh == parity, q_own, q_recv)
@@ -387,23 +399,23 @@
     rates = rates.T
     down = jnp.swapaxes(down, 1, 2)
     step = step.reshape(1, 2)
-    (send,) = call(pack_body, [pay], (q, k, v, rates, decay), 0, 1_000_000)
+    folded = sds((128, FD), BF16)
+    send, send_q = call(pack_body, [pay, folded], (k, v, rates, decay, q), 0, 1_000_000)
     recv = lax.ppermute(send, "zh", [(0, 1), (1, 0)])
     proj_other = lax.ppermute(proj, "c", [(0, 1), (1, 0)])
     mats = sds((3, HD, FD), F32)
     flat = pltpu.VMEM((PAIRS * CHUNK + 64, 128), F32)
-    upd, own = call(
+    upd, own, own_q = call(
         first_body,
-        [mats, pay],
-        (q, k, v, rates, decay, gate, up, down, step),
+        [mats, pay, folded],
+        (k, v, rates, decay, gate, up, down, step, q),
         6_000_000_000,
         3_000_000,
-        mine=(5, 6, 7),
+        mine=(4, 5, 6),
     )
     (pair_kv,) = call(join_body, [sds((2 * BLK, FD), BF16)], (own, recv), 0, 800_000)
-    wins = [
-        lax.ppermute(pair_kv, ("x", "y"), [(i, i + o) for i in range(PAIRS - o)]) for o in (1, 2, 3, 4)
-    ]
+    shifted = lax.ppermute(pair_kv, "x", [(i, i + 1) for i in range(3)])
+    w1 = lax.ppermute(pair_kv, ("x", "y"), [(i, i + 1) for i in range(PAIRS - 1)])
     even, outgoing = call(
         second_body,
         [mats, sds((PAIRS, CROWS, 128), BF16)],
@@ -413,12 +425,18 @@
         scratch=[flat],
         mine=(1, 2, 3),
     )
+    window = sds((2 * BLK, FD), BF16)
+    two, three_back = call(relay_body, [window, window], (pair_kv, shifted), 0, 1_000_000)
+    outgoing, two, three_back, send_q = lax.optimization_barrier((outgoing, two, three_back, send_q))
+    w2 = lax.ppermute(two, "y", [(i, (i + 2) % 4) for i in range(4)])
+    w3 = lax.ppermute(three_back, "y", [(i, (i + 3) % 4) for i in range(4)])
+    recv_q = lax.ppermute(send_q, "zh", [(0, 1), (1, 0)])
     pieces = lax.all_to_all(outgoing, ("x", "y"), 0, 0, tiled=True)
     acc, stat = call(
         attend_first_body,
         [sds((2, BLK, HD), F32), sds((2, BLK, 128), F32)],
-        (own, recv, pair_kv, wins[1], wins[3]),
-        30000000000,
+        (own_q, recv_q, pair_kv, shifted, w1),
+        30_000_000_000,
         2_000_000,
         600_000,
         scratch=[pltpu.VMEM((2, 5, BLK, BLK), F32)],
@@ -429,7 +447,7 @@
     (att,) = call(
         attend_second_body,
         [sds((2, BLK, HD), F32)],
-        (own, recv, wins[0], wins[2], acc, stat, attn_gain.reshape(1, FD)),
+        (own_q, recv_q, w2, w3, acc, stat, attn_gain.reshape(1, FD)),
         500_000_000,
         2_000_000,
         600_000,
@@ -438,11 +456,11 @@
     (mixed,) = call(
         apply_body,
         [sds((4, 64, FD), BF16)],
-        (prefix, even, own, recv, gate, up, down, ttt_gain.reshape(1, FD), att),
+        (prefix, even, own, recv, own_q, recv_q, gate, up, down, ttt_gain.reshape(1, FD), att),
         600_000_000,
         5_000_000,
         scratch=[flat],
-        mine=(4, 5, 6),
+        mine=(6, 7, 8),
     )
     mixed = lax.all_to_all(mixed, ("c", "zh"), 0, 0, tiled=True)
     tile = 512

time: 141 us -> 137 us (0.972)
  blocking collectives: 42.2 us -> 37.4 us
  starting transfers between devices: 31.7 us -> 34.4 us
  waiting for transfers between devices: 16.5 us -> 14.1 us
  Pallas kernels: 43.8 us -> 45.6 us
    all_to_all x1, waiting for transfers between devices: 14.3 us -> 1.99 us  [local(): pieces = lax.all_to_all(outgoing, ('x', 'y'), 0, 0, tiled=True)]
    ppermute x4 -> x5, waiting for transfers between devices: 0.01 us -> 12.1 us  [the longest x1 11.5 us: local(): w3 = lax.ppermute(three_back, 'y', [(i, (i + 3) % 4) for i in range(4)])]
    ppermute x1, starting transfers between devices: 0.96 us -> 6.17 us  [local(): proj_other = lax.ppermute(proj, 'c', [(0, 1), (1, 0)])]
    ppermute x4 -> x5, starting transfers between devices: 15.6 us -> 11.1 us  [the longest x1 3.98 us: local(): lax.ppermute(pair_kv, ('x', 'y'), [(i, i + 1) for i in range(PAIRS - 1)])]
    all_to_all x1, blocking collectives: 27.3 us -> 24.1 us  [local(): lax.all_to_all(partial.reshape(4, 32, WIDTH), 'zl', 0, 0, tiled=True)]
    all_to_all x1, waiting for transfers between devices: 2.26 us -> 0.01 us  [local(): prefix = lax.all_to_all(sums, ('x', 'y'), 0, 0, tiled=True)]
    all_to_all x1, starting transfers between devices: 3.57 us -> 5.59 us  [local(): pieces = lax.all_to_all(outgoing, ('x', 'y'), 0, 0, tiled=True)]
    pallas_call x9 -> x10, Pallas kernels: 39.3 us -> 41 us  [call(): pl.pallas_call(kernel, out_shape=outs, in_specs=[any_spec] * n_in, out_sp...]
  transfers between devices with their start and end apart: 8 -> 9, of which waited for: 2 -> 3; matrix products, arithmetic and copies ran while one was open for 1% -> 1% of each run, Pallas kernels for 26% -> 27%
where the time goes in v5:
time: 137 us; the launch traced here: 136 us
  Pallas kernels  45.6 us (33%)
  blocking collectives  37.4 us (27%)
  starting transfers between devices  34.4 us (25%)
  waiting for transfers between devices  14.1 us (10%)
  local copies, waits for them, and re-layouts  3.99 us (3%)
    pallas_call x10, Pallas kernels, call(): pl.pallas_call(kernel, out_shape=outs, in_specs=[any_spec] * n_in, out_sp...  41 us
    all_to_all x1, blocking collectives, local(): lax.all_to_all(partial.reshape(4, 32, WIDTH), 'zl', 0, 0, tiled=True)  24.1 us
    all_to_all x1, blocking collectives, local(): mixed = lax.all_to_all(mixed, ('c', 'zh'), 0, 0, tiled=True)  13.3 us
    ppermute x1, waiting for transfers between devices, local(): w3 = lax.ppermute(three_back, 'y', [(i, (i + 3) % 4) for i in range(4)])  11.5 us
    ppermute x1, starting transfers between devices, local(): recv = lax.ppermute(send, 'zh', [(0, 1), (1, 0)])  7.83 us
    ppermute x1, starting transfers between devices, local(): proj_other = lax.ppermute(proj, 'c', [(0, 1), (1, 0)])  6.17 us
    all_to_all x1, starting transfers between devices, local(): pieces = lax.all_to_all(outgoing, ('x', 'y'), 0, 0, tiled=True)  5.59 us
    pallas_call x1, Pallas kernels, local(): pl.pallas_call(project_body, out_shape=sds((128, WIDTH), BF16), grid=(WID...  4.56 us
  transfers between devices with their start and end apart: 9, of which 3 were waited for; matrix products, arithmetic and copies ran while one was open for 1% of the time, Pallas kernels for 27%

profile of v5, /device:TPU:1, one launch (start us, length us, event | category | flops | bytes accessed | tf_op | source)
XLA Modules:
  0.0 135.8 jit_solution(9629533513445113299)
XLA Ops:
  0.0 2.1 %shard_map.118 = (bf16[272,384]{1,0:T(8,128)(2,1)}, bf16[128,384]{1,0:T(8,128)(2,1)}) custom-call(bf16[256,384]{1,0:T(8,128)(2,1)} %refs_0_.3, bf16[256,384]{1,0:T(8,128)(2,1)} %refs_1_.4, f32[2,256]{1,0:T(2,128)} %bitcast.8, f32[1,2]{1,0:T(1,128)} %refs_3_.3, bf16[256,384]{1,0:T(8,128)(2,1)} %refs_8_.1), custom_call_target="tpu_custom_call" | custom-call | bytes 1000000 | tf_op jit(solution)/shard_map/pallas_call | solution.py:65
  2.1 7.8 %collective-permute-start = (bf16[272,384]{1,0:T(8,128)(2,1)}, bf16[272,384]{1,0:T(8,128)(2,1)S(1)}, u32[]{:S(2)}, u32[]{:S(2)}) collective-permute-start(bf16[272,384]{1,0:T(8,128)(2,1)} %get-tuple-element.22), channel_id=1, source_target_pairs={{0,8},{8,0},{1,9},{9,1},{2,10},{10,2},{3,11},{11,3},{4,12},{12,4},... | collective-permute-start | bytes 626696 | tf_op jit(solution)/shard_map/ppermute | solution.py:404
  10.0 10.0 %shard_map.119 = (f32[3,192,384]{2,1,0:T(8,128)}, bf16[272,384]{1,0:T(8,128)(2,1)}, bf16[128,384]{1,0:T(8,128)(2,1)}) custom-call(bf16[256,384]{1,0:T(8,128)(2,1)} %refs_0_.3, bf16[256,384]{1,0:T(8,128)(2,1)} %refs_1_.4, f32[2,256]{1,0:T(2,128)} %bitcast.9, f32[1,2]{1,0:T(1,128)} %refs_3_.3, f32[2,192,384]{2,1,0:T(8,128)} %refs_6_.1, ...), custom_call_target="tpu_custom_call" | custom-call | flops 6000000000 | bytes 3000000 | tf_op jit(solution)/shard_map/pallas_call | solution.py:65
  20.0 0.0 collective-permute-done.refs_0_.refs_1_.refs_3_
  20.0 0.0 copy-start.2
  20.0 0.7 copy-done.2
  20.7 1.8 %shard_map.121.refs_0_.refs_2_ = bf16[512,384]{1,0:T(8,128)(2,1)} custom-call(bf16[272,384]{1,0:T(8,128)(2,1)} %get-tuple-element.23.refs_5_.refs_0_.refs_2_, bf16[272,384]{1,0:T(8,128)(2,1)} %copy-done.2), custom_call_target="tpu_custom_call" | custom-call | bytes 800000 | tf_op jit(solution)/shard_map/pallas_call | solution.py:65
  22.5 3.1 %collective-permute-start.1 = (bf16[512,384]{1,0:T(8,128)(2,1)}, bf16[512,384]{1,0:T(8,128)(2,1)S(1)}, u32[]{:S(2)}, u32[]{:S(2)}) collective-permute-start(bf16[512,384]{1,0:T(8,128)(2,1)} %shard_map.121.refs_0_.refs_2_), channel_id=1, source_target_pairs={{0,64},{64,128},{128,192},{1,65},{65,129},{129,193},{2,66},{66,130... | collective-permute-start | bytes 1179656 | tf_op jit(solution)/shard_map/ppermute | solution.py:417
  25.7 4.0 %collective-permute-start.3 = (bf16[512,384]{1,0:T(8,128)(2,1)}, bf16[512,384]{1,0:T(8,128)(2,1)}, u32[]{:S(2)}, u32[]{:S(2)}) collective-permute-start(bf16[512,384]{1,0:T(8,128)(2,1)} %shard_map.121.refs_0_.refs_2_), channel_id=1, source_target_pairs={{0,16},{16,32},{32,48},{48,64},{64,80},{80,96},{96,112},{112,128},... | collective-permute-start | bytes 1179656 | tf_op jit(solution)/shard_map/ppermute | solution.py:418
  29.7 0.0 copy-start.8
  29.7 0.0 copy-start
  29.7 10.2 %shard_map.120 = (f32[3,192,384]{2,1,0:T(8,128)}, bf16[16,112,128]{2,1,0:T(8,128)(2,1)}) custom-call(bf16[272,384]{1,0:T(8,128)(2,1)} %copy-done.2, f32[2,192,384]{2,1,0:T(8,128)} %refs_6_.1, f32[2,192,384]{2,1,0:T(8,128)} %refs_7_.1, f32[2,192,384]{2,1,0:T(8,128)} %bitcast.6, f32[1,2]{1,0:T(1,128)} %bitcast.11, ...), custom_call_target="tpu_custom_call" | custom-call | flops 6000000000 | bytes 4000000 | tf_op jit(solution)/shard_map/pallas_call | solution.py:65
  39.9 0.0 collective-permute-done.1.refs_1_.refs_3_
  39.9 0.0 copy-start.4
  39.9 0.7 copy-done.4
  40.6 2.1 %shard_map.122 = (bf16[512,384]{1,0:T(8,128)(2,1)}, bf16[512,384]{1,0:T(8,128)(2,1)}) custom-call(bf16[512,384]{1,0:T(8,128)(2,1)} %shard_map.121.refs_0_.refs_2_, bf16[512,384]{1,0:T(8,128)(2,1)} %copy-done.4), custom_call_target="tpu_custom_call" | custom-call | bytes 1000000 | tf_op jit(solution)/shard_map/pallas_call | solution.py:65
  42.8 0.0 copy-done.8
  42.8 0.2 collective-permute-start.2
  43.0 0.0 copy-done
  43.0 6.2 %collective-permute-start.6 = (bf16[384,3072]{1,0:T(8,128)(2,1)S(1)}, bf16[384,3072]{1,0:T(8,128)(2,1)}, u32[]{:S(2)}, u32[]{:S(2)}) collective-permute-start(bf16[384,3072]{1,0:T(8,128)(2,1)S(1)} %copy-done), channel_id=1, source_target_pairs={{0,1},{1,0},{2,3},{3,2},{4,5},{5,4},{6,7},{7,6},{8,9},{9,8},{10,11... | collective-permute-start | bytes 7077896 | tf_op jit(solution)/shard_map/ppermute | solution.py:405
  49.2 5.6 %all-to-all-start = ((bf16[16,112,128]{2,1,0:T(8,128)(2,1)}), bf16[16,112,128]{2,1,0:T(8,128)(2,1)S(1)}, u32[]{:S(2)}, u32[]{:S(2)}) async-start(bf16[16,112,128]{2,1,0:T(8,128)(2,1)} %get-tuple-element.29), calls=%async_computation | async-start | bytes 917504 | tf_op jit(solution)/shard_map/all_to_all | solution.py:434
  54.8 2.9 %collective-permute-start.4 = (bf16[512,384]{1,0:T(8,128)(2,1)}, bf16[512,384]{1,0:T(8,128)(2,1)S(1)}, u32[]{:S(2)}, u32[]{:S(2)}) collective-permute-start(bf16[512,384]{1,0:T(8,128)(2,1)} %get-tuple-element.35), channel_id=1, source_target_pairs={{0,32},{16,48},{32,0},{48,16},{1,33},{17,49},{33,1},{49,17},{2,34}... | collective-permute-start | bytes 1179656 | tf_op jit(solution)/shard_map/ppermute | solution.py:431
  57.6 0.9 collective-permute-start.5
  58.5 0.0 collective-permute-done.3.refs_4_
  58.5 0.0 collective-permute-done.2.refs_1_.refs_5_
  58.5 0.0 copy-start.5
  58.5 0.6 copy-done.5
  59.2 0.0 copy-start.6
  59.2 0.0 copy-start.7
  59.2 3.9 %shard_map.123 = (f32[2,256,192]{2,1,0:T(8,128)}, f32[2,256,128]{2,1,0:T(8,128)}) custom-call(bf16[128,384]{1,0:T(8,128)(2,1)} %get-tuple-element.30.refs_0_.refs_4_, bf16[128,384]{1,0:T(8,128)(2,1)} %copy-done.5, bf16[512,384]{1,0:T(8,128)(2,1)} %shard_map.121.refs_0_.refs_2_, bf16[512,384]{1,0:T(8,128)(2,1)} %copy-done.4, ...), custom_call_target="tpu_custom_call" | custom-call | flops 30000001024 | bytes 2000000 | tf_op jit(solution)/shard_map/pallas_call | solution.py:65
  63.0 2.0 %all-to-all-done.refs_0_ = bf16[16,112,128]{2,1,0:T(8,128)(2,1)S(1)} async-done(((bf16[16,112,128]{2,1,0:T(8,128)(2,1)}), bf16[16,112,128]{2,1,0:T(8,128)(2,1)S(1)}, u32[]{:S(2)}, u32[]{:S(2)}) %all-to-all-start) | async-done | bytes 458784 | tf_op jit(solution)/shard_map/all_to_all | solution.py:434
  65.0 1.2 shard_map.124
  66.2 3.8 %all-to-all-start.1 = ((bf16[16,112,128]{2,1,0:T(8,128)(2,1)}), bf16[16,112,128]{2,1,0:T(8,128)(2,1)S(1)}, u32[]{:S(2)}, u32[]{:S(2)}) async-start(bf16[16,112,128]{2,1,0:T(8,128)(2,1)} %shard_map.124), calls=%async_computation.1 | async-start | bytes 917504 | tf_op jit(solution)/shard_map/all_to_all | solution.py:446
  70.0 0.0 copy-done.6
  70.0 0.6 reshape.14.refs_6_
  70.6 0.0 copy-done.7
  70.6 0.6 reshape.13.refs_9_
  71.2 0.6 collective-permute-done.4.refs_2_
  71.8 0.0 copy-start.3
  71.8 11.5 %collective-permute-done.5.refs_3_ = bf16[512,384]{1,0:T(8,128)(2,1)} collective-permute-done((bf16[512,384]{1,0:T(8,128)(2,1)}, bf16[512,384]{1,0:T(8,128)(2,1)}, u32[]{:S(2)}, u32[]{:S(2)}) %collective-permute-start.5) | collective-permute-done | bytes 393248 | tf_op jit(solution)/shard_map/ppermute | solution.py:432
  83.2 0.0 copy-done.3
  83.2 4.1 %shard_map.125.refs_10_ = f32[2,256,192]{2,1,0:T(8,128)} custom-call(bf16[128,384]{1,0:T(8,128)(2,1)} %get-tuple-element.30.refs_0_.refs_4_, bf16[128,384]{1,0:T(8,128)(2,1)} %copy-done.5, bf16[512,384]{1,0:T(8,128)(2,1)} %copy-done.3, bf16[512,384]{1,0:T(8,128)(2,1)} %collective-permute-done.5.refs_3_, f32[2,256,192]{2,1,0:T(8,128)} %get-tuple-element.37.refs_4_, ...), custom_call_target="tpu_custom_call" | custom-call | flops 500000000 | bytes 2000000 | tf_op jit(solution)/shard_map/pallas_call | solution.py:65
  87.3 0.0 all-to-all-done.1.refs_0_
  87.4 0.0 copy-start.1
  87.4 0.8 copy-done.1
  88.1 4.7 %shard_map.126 = bf16[4,64,384]{2,1,0:T(8,128)(2,1)} custom-call(bf16[16,112,128]{2,1,0:T(8,128)(2,1)} %copy-done.1, f32[3,192,384]{2,1,0:T(8,128)} %get-tuple-element.34.refs_1_, bf16[272,384]{1,0:T(8,128)(2,1)} %get-tuple-element.23.refs_5_.refs_0_.refs_2_, bf16[272,384]{1,0:T(8,128)(2,1)} %copy-done.2, ...), custom_call_target="tpu_custom_call" | custom-call | flops 600000000 | bytes 5000000 | tf_op jit(solution)/shard_map/pallas_call | solution.py:65
  92.8 13.3 %all_to_all.20.mix_ref = bf16[4,64,384]{2,1,0:T(8,128)(2,1)S(1)} all-to-all(bf16[4,64,384]{2,1,0:T(8,128)(2,1)} %shard_map.126), channel_id=1, replica_groups=mesh['x'=4,'y'=4,'zh'=2,'zl'=4,'c'=2] {'c','zh'}, dimensions={0} | all-to-all | bytes 393216 | tf_op jit(solution)/shard_map/all_to_all | solution.py:465
  106.1 0.0 collective-permute-done.6.other_ref
  106.2 4.6 %shard_map.127 = bf16[128,3072]{1,0:T(8,128)(2,1)S(1)} custom-call(bf16[4,64,384]{2,1,0:T(8,128)(2,1)S(1)} %all_to_all.20.mix_ref, bf16[384,3072]{1,0:T(8,128)(2,1)S(1)} %copy-done, bf16[384,3072]{1,0:T(8,128)(2,1)} %collective-permute-done.6.other_ref), custom_call_target="tpu_custom_call" | custom-call | flops 600000000 | bytes 6000000 | tf_op jit(solution)/shard_map/pallas_call | solution.py:467
  110.7 24.1 %all_to_all.21.refs_0_ = bf16[4,32,3072]{2,1,0:T(8,128)(2,1)S(1)} all-to-all(bf16[4,32,3072]{2,1,0:T(8,128)(2,1)S(1)} %bitcast.4), channel_id=1, replica_groups=mesh['x'=4,'y'=4,'zh'=2,'zl'=4,'c'=2] {'zl'}, dimensions={0} | all-to-all | bytes 1572864 | tf_op jit(solution)/shard_map/all_to_all | solution.py:480
  134.8 0.8 shard_map.128
Async XLA Ops:
  2.1 17.9 %collective-permute-start = (bf16[272,384]{1,0:T(8,128)(2,1)}, bf16[272,384]{1,0:T(8,128)(2,1)S(1)}, u32[]{:S(2)}, u32[]{:S(2)}) collective-permute-start(bf16[272,384]{1,0:T(8,128)(2,1)} %get-tuple-element.22), channel_id=1, source_target_pairs={{0,8},{8,0},{1,9},{9,1},{2,10},{10,2},{3,11},{11,3},{4,12},{12,4},... | collective-permute-start | bytes 626696 | tf_op jit(solution)/shard_map/ppermute | solution.py:404
  20.0 0.7 copy-start.2
  22.5 17.4 %collective-permute-start.1 = (bf16[512,384]{1,0:T(8,128)(2,1)}, bf16[512,384]{1,0:T(8,128)(2,1)S(1)}, u32[]{:S(2)}, u32[]{:S(2)}) collective-permute-start(bf16[512,384]{1,0:T(8,128)(2,1)} %shard_map.121.refs_0_.refs_2_), channel_id=1, source_target_pairs={{0,64},{64,128},{128,192},{1,65},{65,129},{129,193},{2,66},{66,130... | collective-permute-start | bytes 1179656 | tf_op jit(solution)/shard_map/ppermute | solution.py:417
  25.7 32.8 %collective-permute-start.3 = (bf16[512,384]{1,0:T(8,128)(2,1)}, bf16[512,384]{1,0:T(8,128)(2,1)}, u32[]{:S(2)}, u32[]{:S(2)}) collective-permute-start(bf16[512,384]{1,0:T(8,128)(2,1)} %shard_map.121.refs_0_.refs_2_), channel_id=1, source_target_pairs={{0,16},{16,32},{32,48},{48,64},{64,80},{80,96},{96,112},{112,128},... | collective-permute-start | bytes 1179656 | tf_op jit(solution)/shard_map/ppermute | solution.py:418
  29.7 13.1 %copy-start.8 = (bf16[128,384]{1,0:T(8,128)(2,1)S(1)}, bf16[128,384]{1,0:T(8,128)(2,1)}, u32[]{:S(2)}) copy-start(bf16[128,384]{1,0:T(8,128)(2,1)} %get-tuple-element.31) | copy-start | bytes 294916
  29.7 13.3 %copy-start = (bf16[384,3072]{1,0:T(8,128)(2,1)S(1)}, bf16[384,3072]{1,0:T(8,128)(2,1)}, u32[]{:S(2)}) copy-start(bf16[384,3072]{1,0:T(8,128)(2,1)} %own_ref.1) | copy-start | bytes 7077892
  39.9 0.7 copy-start.4
  42.8 15.7 %collective-permute-start.2 = (bf16[128,384]{1,0:T(8,128)(2,1)S(1)}, bf16[128,384]{1,0:T(8,128)(2,1)S(1)}, u32[]{:S(2)}, u32[]{:S(2)}) collective-permute-start(bf16[128,384]{1,0:T(8,128)(2,1)S(1)} %copy-done.8), channel_id=1, source_target_pairs={{0,8},{8,0},{1,9},{9,1},{2,10},{10,2},{3,11},{11,3},{4,12},{12,4},... | collective-permute-start | bytes 294920 | tf_op jit(solution)/shard_map/ppermute | solution.py:433
  43.0 63.2 %collective-permute-start.6 = (bf16[384,3072]{1,0:T(8,128)(2,1)S(1)}, bf16[384,3072]{1,0:T(8,128)(2,1)}, u32[]{:S(2)}, u32[]{:S(2)}) collective-permute-start(bf16[384,3072]{1,0:T(8,128)(2,1)S(1)} %copy-done), channel_id=1, source_target_pairs={{0,1},{1,0},{2,3},{3,2},{4,5},{5,4},{6,7},{7,6},{8,9},{9,8},{10,11... | collective-permute-start | bytes 7077896 | tf_op jit(solution)/shard_map/ppermute | solution.py:405
  49.2 15.9 %all-to-all-start = ((bf16[16,112,128]{2,1,0:T(8,128)(2,1)}), bf16[16,112,128]{2,1,0:T(8,128)(2,1)S(1)}, u32[]{:S(2)}, u32[]{:S(2)}) async-start(bf16[16,112,128]{2,1,0:T(8,128)(2,1)} %get-tuple-element.29), calls=%async_computation | async-start | bytes 917504 | tf_op jit(solution)/shard_map/all_to_all | solution.py:434
  54.8 17.0 %collective-permute-start.4 = (bf16[512,384]{1,0:T(8,128)(2,1)}, bf16[512,384]{1,0:T(8,128)(2,1)S(1)}, u32[]{:S(2)}, u32[]{:S(2)}) collective-permute-start(bf16[512,384]{1,0:T(8,128)(2,1)} %get-tuple-element.35), channel_id=1, source_target_pairs={{0,32},{16,48},{32,0},{48,16},{1,33},{17,49},{33,1},{49,17},{2,34}... | collective-permute-start | bytes 1179656 | tf_op jit(solution)/shard_map/ppermute | solution.py:431
  57.6 25.6 %collective-permute-start.5 = (bf16[512,384]{1,0:T(8,128)(2,1)}, bf16[512,384]{1,0:T(8,128)(2,1)}, u32[]{:S(2)}, u32[]{:S(2)}) collective-permute-start(bf16[512,384]{1,0:T(8,128)(2,1)} %get-tuple-element.36), channel_id=1, source_target_pairs={{0,48},{16,0},{32,16},{48,32},{1,49},{17,1},{33,17},{49,33},{2,50}... | collective-permute-start | bytes 1179656 | tf_op jit(solution)/shard_map/ppermute | solution.py:432
  58.5 0.6 copy-start.5
  59.2 10.8 %copy-start.6 = (f32[384]{0:T(512)S(1)}, f32[384]{0:T(512)}, u32[]{:S(2)}) copy-start(f32[384]{0:T(512)} %param.22) | copy-start | bytes 4612
  59.2 11.4 %copy-start.7 = (f32[384]{0:T(512)S(1)}, f32[384]{0:T(512)}, u32[]{:S(2)}) copy-start(f32[384]{0:T(512)} %param.21) | copy-start | bytes 4612
  66.2 21.2 %all-to-all-start.1 = ((bf16[16,112,128]{2,1,0:T(8,128)(2,1)}), bf16[16,112,128]{2,1,0:T(8,128)(2,1)S(1)}, u32[]{:S(2)}, u32[]{:S(2)}) async-start(bf16[16,112,128]{2,1,0:T(8,128)(2,1)} %shard_map.124), calls=%async_computation.1 | async-start | bytes 917504 | tf_op jit(solution)/shard_map/all_to_all | solution.py:446
  71.8 11.5 %copy-start.3 = (bf16[512,384]{1,0:T(8,128)(2,1)}, bf16[512,384]{1,0:T(8,128)(2,1)S(1)}, u32[]{:S(2)}) copy-start(bf16[512,384]{1,0:T(8,128)(2,1)S(1)} %collective-permute-done.4.refs_2_) | copy-start | bytes 1179652
  87.4 0.8 copy-start.1

commit v6 on v5

--- a/solution.py
+++ b/solution.py
@@ -203,12 +203,9 @@
     fold_queries(query_ref, pick(q.get(), zh))
 
 
-def relay_body(pair_kv, shifted, two_ref, three_ref):
+def relay_body(pair_kv, shifted, out_ref):
     y = lax.axis_index("y")
-    here = pair_kv.get()[...]
-    before = shifted.get()[...]
-    two_ref[...] = jnp.where(y < 2, here, before)
-    three_ref[...] = jnp.where(y < 1, here, before)
+    out_ref[...] = jnp.where(y < 1, pair_kv.get()[...], shifted.get()[...])
 
 
 def join_body(own, recv, out_ref):
@@ -299,11 +296,11 @@
     return lax.axis_index("x") * 4 + lax.axis_index("y")
 
 
-def attend_first_body(own, recv, pair_kv, shifted, w1, acc_ref, stat_ref, score_ref):
+def attend_first_body(own, recv, pair_kv, shifted, w2, acc_ref, stat_ref, score_ref):
     zh = lax.axis_index("zh")
     q_own = queries(own.get())
     q_recv = queries(recv.get())
-    wins = {0: pair_kv.get(), 4: shifted.get(), 1: w1.get()}
+    wins = {0: pair_kv.get(), 4: shifted.get(), 2: w2.get()}
     rows_of = ordered_rows(zh)
     lane = lax.broadcasted_iota(jnp.int32, (BLK, 128), 1)
     for parity in range(2):
@@ -316,12 +313,12 @@
         stat_ref[parity] = jnp.where(lane < 64, top, total)
 
 
-def attend_second_body(own, recv, w2, w3, acc_in, stat, gain_in, out_ref, score_ref):
+def attend_second_body(own, recv, w1, w3, acc_in, stat, gain_in, out_ref, score_ref):
     zh = lax.axis_index("zh")
     q_own = queries(own.get())
     q_recv = queries(recv.get())
     gain_ref = gain_in.get()
-    wins = {2: w2.get(), 3: w3.get()}
+    wins = {1: w1.get(), 3: w3.get()}
     gain = jnp.where(zh == 0, gain_ref[:, :HD], gain_ref[:, HD:])
     rows_of = ordered_rows(zh)
     stats = stat.get()
@@ -376,10 +373,12 @@
                 ]
 
 
-def project_body(mix_ref, own_ref, other_ref, out_ref):
+def project_body(mix, own, other, out_ref):
     core = lax.axis_index("c")
+    mix_ref = mix.get()
     total = None
-    for w_ref, which in ((own_ref, core), (other_ref, 1 - core)):
+    for w, which in ((own, core), (other, 1 - core)):
+        w_ref = w.get()
         for zh in range(2):
             part = mix_ref[which * 2 + zh]
             part = jnp.concatenate([part[:, :HD], part[:, HD:]], axis=0)
@@ -414,8 +413,9 @@
         mine=(4, 5, 6),
     )
     (pair_kv,) = call(join_body, [sds((2 * BLK, FD), BF16)], (own, recv), 0, 800_000)
+    pair_kv, proj_other = lax.optimization_barrier((pair_kv, proj_other))
     shifted = lax.ppermute(pair_kv, "x", [(i, i + 1) for i in range(3)])
-    w1 = lax.ppermute(pair_kv, ("x", "y"), [(i, i + 1) for i in range(PAIRS - 1)])
+    w1, w2 = [lax.ppermute(pair_kv, ("x", "y"), [(i, i + o) for i in range(PAIRS - o)]) for o in (1, 2)]
     even, outgoing = call(
         second_body,
         [mats, sds((PAIRS, CROWS, 128), BF16)],
@@ -425,17 +425,15 @@
         scratch=[flat],
         mine=(1, 2, 3),
     )
-    window = sds((2 * BLK, FD), BF16)
-    two, three_back = call(relay_body, [window, window], (pair_kv, shifted), 0, 1_000_000)
-    outgoing, two, three_back, send_q = lax.optimization_barrier((outgoing, two, three_back, send_q))
-    w2 = lax.ppermute(two, "y", [(i, (i + 2) % 4) for i in range(4)])
-    w3 = lax.ppermute(three_back, "y", [(i, (i + 3) % 4) for i in range(4)])
+    (behind,) = call(relay_body, [sds((2 * BLK, FD), BF16)], (pair_kv, shifted), 0, 1_000_000)
+    outgoing, behind, send_q = lax.optimization_barrier((outgoing, behind, send_q))
+    w3 = lax.ppermute(behind, "y", [(i, (i + 3) % 4) for i in range(4)])
     recv_q = lax.ppermute(send_q, "zh", [(0, 1), (1, 0)])
     pieces = lax.all_to_all(outgoing, ("x", "y"), 0, 0, tiled=True)
     acc, stat = call(
         attend_first_body,
         [sds((2, BLK, HD), F32), sds((2, BLK, 128), F32)],
-        (own_q, recv_q, pair_kv, shifted, w1),
+        (own_q, recv_q, pair_kv, shifted, w2),
         30_000_000_000,
         2_000_000,
         600_000,
@@ -447,7 +445,7 @@
     (att,) = call(
         attend_second_body,
         [sds((2, BLK, HD), F32)],
-        (own_q, recv_q, w2, w3, acc, stat, attn_gain.reshape(1, FD)),
+        (own_q, recv_q, w1, w3, acc, stat, attn_gain.reshape(1, FD)),
         500_000_000,
         2_000_000,
         600_000,
@@ -463,20 +461,14 @@
         mine=(6, 7, 8),
     )
     mixed = lax.all_to_all(mixed, ("c", "zh"), 0, 0, tiled=True)
-    tile = 512
-    partial = pl.pallas_call(
+    (partial,) = call(
         project_body,
-        out_shape=sds((128, WIDTH), BF16),
-        grid=(WIDTH // tile,),
-        in_specs=[
-            pl.BlockSpec((4, 64, FD), lambda i: (0, 0, 0)),
-            pl.BlockSpec((FD, tile), lambda i: (0, i)),
-            pl.BlockSpec((FD, tile), lambda i: (0, i)),
-        ],
-        out_specs=pl.BlockSpec((128, tile), lambda i: (0, i)),
-        compiler_params=pltpu.CompilerParams(vmem_limit_bytes=SMALL),
-        cost_estimate=pl.CostEstimate(flops=600_000_000, bytes_accessed=6_000_000, transcendentals=0),
-    )(mixed, proj, proj_other)
+        [sds((128, WIDTH), BF16)],
+        (mixed, proj, proj_other),
+        600_000_000,
+        6_000_000,
+        cap=VMEM_CAP,
+    )
     parts = lax.all_to_all(partial.reshape(4, 32, WIDTH), "zl", 0, 0, tiled=True)
     (result,) = call(total_body, [sds((32, WIDTH), BF16)], (parts,), 400_000, 1_000_000, cap=SMALL)
     return result

time: 137 us -> 134 us (0.978)
  blocking collectives: 37.4 us -> 47 us
  waiting for transfers between devices: 14.1 us -> 5.14 us
  starting transfers between devices: 34.4 us -> 31.5 us
    ppermute x3, waiting for transfers between devices: 12.1 us -> 0.01 us  [the longest x2 0.01 us: local(): lax.ppermute(pair_kv, ('x', 'y'), [(i, i + o) for i in range(PAIRS - o)])]
    all_to_all x1, blocking collectives: 13.3 us -> 21.2 us  [local(): mixed = lax.all_to_all(mixed, ('c', 'zh'), 0, 0, tiled=True)]
    pallas_call x1 -> x0, Pallas kernels: 4.56 us -> none  [local(): pl.pallas_call(project_body, out_shape=sds((128, WIDTH), BF16), grid=(WID...]
    pallas_call x10 -> x11, Pallas kernels: 41 us -> 44.8 us  [call(): pl.pallas_call(kernel, out_shape=outs, in_specs=[any_spec] * n_in, out_sp...]
    ppermute x1, starting transfers between devices: 6.17 us -> 3.24 us  [local(): proj_other = lax.ppermute(proj, 'c', [(0, 1), (1, 0)])]
    ppermute x1, starting transfers between devices: 7.83 us -> 5.26 us  [local(): recv = lax.ppermute(send, 'zh', [(0, 1), (1, 0)])]
    all_to_all x1, waiting for transfers between devices: 0.01 us -> 2.18 us  [local(): prefix = lax.all_to_all(sums, ('x', 'y'), 0, 0, tiled=True)]
    ppermute x3, starting transfers between devices: 7.74 us -> 9.91 us  [the longest x2 7.33 us: local(): lax.ppermute(pair_kv, ('x', 'y'), [(i, i + o) for i in range(PAIRS - o)])]
  transfers between devices with their start and end apart: 9 -> 9, of which waited for: 3 -> 2; matrix products, arithmetic and copies ran while one was open for 1% -> 1% of each run, Pallas kernels for 27% -> 26%
where the time goes in v6:
time: 134 us
  blocking collectives  47 us (35%)
  Pallas kernels  44.8 us (33%)
  starting transfers between devices  31.5 us (24%)
  waiting for transfers between devices  5.14 us (4%)
  local copies, waits for them, and re-layouts  5.04 us (4%)
    pallas_call x11, Pallas kernels, call(): pl.pallas_call(kernel, out_shape=outs, in_specs=[any_spec] * n_in, out_sp...  44.8 us
    all_to_all x1, blocking collectives, local(): lax.all_to_all(partial.reshape(4, 32, WIDTH), 'zl', 0, 0, tiled=True)  25.8 us
    all_to_all x1, blocking collectives, local(): mixed = lax.all_to_all(mixed, ('c', 'zh'), 0, 0, tiled=True)  21.2 us
    ppermute x2, starting transfers between devices, local(): lax.ppermute(pair_kv, ('x', 'y'), [(i, i + o) for i in range(PAIRS - o)])  7.33 us
    ppermute x1, starting transfers between devices, local(): recv = lax.ppermute(send, 'zh', [(0, 1), (1, 0)])  5.26 us
    all_to_all x1, starting transfers between devices, local(): pieces = lax.all_to_all(outgoing, ('x', 'y'), 0, 0, tiled=True)  5.17 us
    unnamed x22, local copies, waits for them, and re-layouts  3.93 us
    all_to_all x1, starting transfers between devices, local(): prefix = lax.all_to_all(sums, ('x', 'y'), 0, 0, tiled=True)  3.79 us
  transfers between devices with their start and end apart: 9, of which 2 were waited for; matrix products, arithmetic and copies ran while one was open for 1% of the time, Pallas kernels for 26%

profile of v6, /device:TPU:1, one launch (start us, length us, event | category | flops | bytes accessed | tf_op | source)
XLA Modules:
  0.0 133.8 jit_solution(3750042020530076783)
XLA Ops:
  0.0 3.2 %collective-permute-start.1 = (bf16[384,3072]{1,0:T(8,128)(2,1)}, bf16[384,3072]{1,0:T(8,128)(2,1)S(1)}, u32[]{:S(2)}, u32[]{:S(2)}) collective-permute-start(bf16[384,3072]{1,0:T(8,128)(2,1)} %refs_1_.7), channel_id=1, source_target_pairs={{0,1},{1,0},{2,3},{3,2},{4,5},{5,4},{6,7},{7,6},{8,9},{9,8},{10,11... | collective-permute-start | bytes 7077896 | tf_op jit(solution)/shard_map/ppermute | solution.py:404
  3.2 2.1 %shard_map.118 = (bf16[272,384]{1,0:T(8,128)(2,1)}, bf16[128,384]{1,0:T(8,128)(2,1)}) custom-call(bf16[256,384]{1,0:T(8,128)(2,1)} %refs_0_.3, bf16[256,384]{1,0:T(8,128)(2,1)} %refs_1_.5, f32[2,256]{1,0:T(2,128)} %bitcast.8, f32[1,2]{1,0:T(1,128)} %refs_3_.3, bf16[256,384]{1,0:T(8,128)(2,1)} %refs_8_.1), custom_call_target="tpu_custom_call" | custom-call | bytes 1000000 | tf_op jit(solution)/shard_map/pallas_call | solution.py:65
  5.4 5.3 %collective-permute-start = (bf16[272,384]{1,0:T(8,128)(2,1)}, bf16[272,384]{1,0:T(8,128)(2,1)S(1)}, u32[]{:S(2)}, u32[]{:S(2)}) collective-permute-start(bf16[272,384]{1,0:T(8,128)(2,1)} %get-tuple-element.21), channel_id=1, source_target_pairs={{0,8},{8,0},{1,9},{9,1},{2,10},{10,2},{3,11},{11,3},{4,12},{12,4},... | collective-permute-start | bytes 626696 | tf_op jit(solution)/shard_map/ppermute | solution.py:403
  10.7 10.0 %shard_map.119 = (f32[3,192,384]{2,1,0:T(8,128)}, bf16[272,384]{1,0:T(8,128)(2,1)}, bf16[128,384]{1,0:T(8,128)(2,1)}) custom-call(bf16[256,384]{1,0:T(8,128)(2,1)} %refs_0_.3, bf16[256,384]{1,0:T(8,128)(2,1)} %refs_1_.5, f32[2,256]{1,0:T(2,128)} %bitcast.9, f32[1,2]{1,0:T(1,128)} %refs_3_.3, f32[2,192,384]{2,1,0:T(8,128)} %refs_6_.1, ...), custom_call_target="tpu_custom_call" | custom-call | flops 6000000000 | bytes 3000000 | tf_op jit(solution)/shard_map/pallas_call | solution.py:65
  20.7 0.0 collective-permute-done.refs_0_.refs_1_.refs_3_
  20.7 0.0 copy-start.3
  20.7 0.7 copy-done.3
  21.4 1.8 %shard_map.121.refs_0_.refs_2_ = bf16[512,384]{1,0:T(8,128)(2,1)} custom-call(bf16[272,384]{1,0:T(8,128)(2,1)} %get-tuple-element.22.refs_5_.refs_0_.refs_2_, bf16[272,384]{1,0:T(8,128)(2,1)} %copy-done.3), custom_call_target="tpu_custom_call" | custom-call | bytes 800000 | tf_op jit(solution)/shard_map/pallas_call | solution.py:65
  23.2 0.0 collective-permute-done.1.refs_2_
  23.3 0.0 copy-start
  23.3 3.1 %collective-permute-start.2 = (bf16[512,384]{1,0:T(8,128)(2,1)}, bf16[512,384]{1,0:T(8,128)(2,1)S(1)}, u32[]{:S(2)}, u32[]{:S(2)}) collective-permute-start(bf16[512,384]{1,0:T(8,128)(2,1)} %shard_map.121.refs_0_.refs_2_), channel_id=1, source_target_pairs={{0,64},{64,128},{128,192},{1,65},{65,129},{129,193},{2,66},{66,130... | collective-permute-start | bytes 1179656 | tf_op jit(solution)/shard_map/ppermute | solution.py:417
  26.4 5.0 %collective-permute-start.4 = (bf16[512,384]{1,0:T(8,128)(2,1)}, bf16[512,384]{1,0:T(8,128)(2,1)S(1)}, u32[]{:S(2)}, u32[]{:S(2)}) collective-permute-start(bf16[512,384]{1,0:T(8,128)(2,1)} %shard_map.121.refs_0_.refs_2_), channel_id=1, source_target_pairs={{0,32},{16,48},{32,64},{48,80},{64,96},{80,112},{96,128},{112,144}... | collective-permute-start | bytes 1179656 | tf_op jit(solution)/shard_map/ppermute | solution.py:418
  31.4 0.0 copy-start.2
  31.5 10.1 %shard_map.120 = (f32[3,192,384]{2,1,0:T(8,128)}, bf16[16,112,128]{2,1,0:T(8,128)(2,1)}) custom-call(bf16[272,384]{1,0:T(8,128)(2,1)} %copy-done.3, f32[2,192,384]{2,1,0:T(8,128)} %refs_6_.1, f32[2,192,384]{2,1,0:T(8,128)} %refs_7_.1, f32[2,192,384]{2,1,0:T(8,128)} %bitcast.6, f32[1,2]{1,0:T(1,128)} %bitcast.11, ...), custom_call_target="tpu_custom_call" | custom-call | flops 6000000000 | bytes 4000000 | tf_op jit(solution)/shard_map/pallas_call | solution.py:65
  41.6 0.0 copy-done
  41.6 0.0 collective-permute-done.2.refs_1_.refs_3_
  41.6 0.0 copy-start.6
  41.6 0.7 copy-done.6
  42.4 2.0 %shard_map.122 = bf16[512,384]{1,0:T(8,128)(2,1)} custom-call(bf16[512,384]{1,0:T(8,128)(2,1)} %shard_map.121.refs_0_.refs_2_, bf16[512,384]{1,0:T(8,128)(2,1)} %copy-done.6), custom_call_target="tpu_custom_call" | custom-call | bytes 1000000 | tf_op jit(solution)/shard_map/pallas_call | solution.py:65
  44.3 0.9 collective-permute-start.3
  45.2 0.0 copy-done.2
  45.2 2.3 %collective-permute-start.5 = (bf16[512,384]{1,0:T(8,128)(2,1)S(1)}, bf16[512,384]{1,0:T(8,128)(2,1)S(1)}, u32[]{:S(2)}, u32[]{:S(2)}) collective-permute-start(bf16[512,384]{1,0:T(8,128)(2,1)S(1)} %copy-done.2), channel_id=1, source_target_pairs={{0,16},{16,32},{32,48},{48,64},{64,80},{80,96},{96,112},{112,128},... | collective-permute-start | bytes 1179656 | tf_op jit(solution)/shard_map/ppermute | solution.py:418
  47.6 5.2 %all-to-all-start = ((bf16[16,112,128]{2,1,0:T(8,128)(2,1)}), bf16[16,112,128]{2,1,0:T(8,128)(2,1)S(1)}, u32[]{:S(2)}, u32[]{:S(2)}) async-start(bf16[16,112,128]{2,1,0:T(8,128)(2,1)} %get-tuple-element.27), calls=%async_computation | async-start | bytes 917504 | tf_op jit(solution)/shard_map/all_to_all | solution.py:432
  52.8 2.6 %collective-permute-start.6 = (bf16[512,384]{1,0:T(8,128)(2,1)}, bf16[512,384]{1,0:T(8,128)(2,1)S(1)}, u32[]{:S(2)}, u32[]{:S(2)}) collective-permute-start(bf16[512,384]{1,0:T(8,128)(2,1)} %shard_map.122), channel_id=1, source_target_pairs={{0,48},{16,0},{32,16},{48,32},{1,49},{17,1},{33,17},{49,33},{2,50}... | collective-permute-start | bytes 1179656 | tf_op jit(solution)/shard_map/ppermute | solution.py:430
  55.3 0.0 collective-permute-done.4.refs_4_
  55.3 0.0 copy-start.10
  55.3 0.0 collective-permute-done.3.refs_1_.refs_5_
  55.3 0.0 copy-start.7
  55.4 0.7 copy-done.10
  56.1 0.0 copy-done.7
  56.1 0.0 copy-start.8
  56.1 0.0 copy-start.9
  56.1 3.9 %shard_map.123 = (f32[2,256,192]{2,1,0:T(8,128)}, f32[2,256,128]{2,1,0:T(8,128)}) custom-call(bf16[128,384]{1,0:T(8,128)(2,1)} %get-tuple-element.28.refs_0_.refs_4_, bf16[128,384]{1,0:T(8,128)(2,1)} %copy-done.7, bf16[512,384]{1,0:T(8,128)(2,1)} %shard_map.121.refs_0_.refs_2_, bf16[512,384]{1,0:T(8,128)(2,1)} %copy-done.6, bf16[512,384]{1,0:T(8,128)(2,1)} %copy-done.10), custom_call_target="tpu_custom_call" | custom-call | flops 30000001024 | bytes 2000000 | tf_op jit(solution)/shard_map/pallas_call | solution.py:65
  60.0 2.9 %all-to-all-done.refs_0_ = bf16[16,112,128]{2,1,0:T(8,128)(2,1)S(1)} async-done(((bf16[16,112,128]{2,1,0:T(8,128)(2,1)}), bf16[16,112,128]{2,1,0:T(8,128)(2,1)S(1)}, u32[]{:S(2)}, u32[]{:S(2)}) %all-to-all-start) | async-done | bytes 458784 | tf_op jit(solution)/shard_map/all_to_all | solution.py:432
  62.9 1.2 shard_map.124
  64.1 3.8 %all-to-all-start.1 = ((bf16[16,112,128]{2,1,0:T(8,128)(2,1)}), bf16[16,112,128]{2,1,0:T(8,128)(2,1)S(1)}, u32[]{:S(2)}, u32[]{:S(2)}) async-start(bf16[16,112,128]{2,1,0:T(8,128)(2,1)} %shard_map.124), calls=%async_computation.1 | async-start | bytes 917504 | tf_op jit(solution)/shard_map/all_to_all | solution.py:444
  67.9 0.0 copy-done.8
  67.9 0.6 reshape.14.refs_6_
  68.5 0.0 copy-done.9
  68.5 0.5 reshape.13.refs_9_
  69.0 0.0 collective-permute-done.5.refs_2_
  69.0 0.0 copy-start.4
  69.0 0.0 collective-permute-done.6.refs_3_
  69.1 0.0 copy-start.5
  69.1 0.7 copy-done.4
  69.8 0.2 copy-done.5
  70.0 4.1 %shard_map.125.refs_10_ = f32[2,256,192]{2,1,0:T(8,128)} custom-call(bf16[128,384]{1,0:T(8,128)(2,1)} %get-tuple-element.28.refs_0_.refs_4_, bf16[128,384]{1,0:T(8,128)(2,1)} %copy-done.7, bf16[512,384]{1,0:T(8,128)(2,1)} %copy-done.4, bf16[512,384]{1,0:T(8,128)(2,1)} %copy-done.5, f32[2,256,192]{2,1,0:T(8,128)} %get-tuple-element.34.refs_4_, ...), custom_call_target="tpu_custom_call" | custom-call | flops 500000000 | bytes 2000000 | tf_op jit(solution)/shard_map/pallas_call | solution.py:65
  74.1 2.2 %all-to-all-done.1.refs_0_ = bf16[16,112,128]{2,1,0:T(8,128)(2,1)S(1)} async-done(((bf16[16,112,128]{2,1,0:T(8,128)(2,1)}), bf16[16,112,128]{2,1,0:T(8,128)(2,1)S(1)}, u32[]{:S(2)}, u32[]{:S(2)}) %all-to-all-start.1) | async-done | bytes 458784 | tf_op jit(solution)/shard_map/all_to_all | solution.py:444
  76.3 0.0 copy-start.1
  76.3 0.8 copy-done.1
  77.1 4.7 %shard_map.126 = bf16[4,64,384]{2,1,0:T(8,128)(2,1)} custom-call(bf16[16,112,128]{2,1,0:T(8,128)(2,1)} %copy-done.1, f32[3,192,384]{2,1,0:T(8,128)} %get-tuple-element.32.refs_1_, bf16[272,384]{1,0:T(8,128)(2,1)} %get-tuple-element.22.refs_5_.refs_0_.refs_2_, bf16[272,384]{1,0:T(8,128)(2,1)} %copy-done.3, ...), custom_call_target="tpu_custom_call" | custom-call | flops 600000000 | bytes 5000000 | tf_op jit(solution)/shard_map/pallas_call | solution.py:65
  81.8 21.2 %all_to_all.20.refs_0_ = bf16[4,64,384]{2,1,0:T(8,128)(2,1)} all-to-all(bf16[4,64,384]{2,1,0:T(8,128)(2,1)} %shard_map.126), channel_id=1, replica_groups=mesh['x'=4,'y'=4,'zh'=2,'zl'=4,'c'=2] {'c','zh'}, dimensions={0} | all-to-all | bytes 393216 | tf_op jit(solution)/shard_map/all_to_all | solution.py:463
  102.9 4.0 %shard_map.127 = bf16[128,3072]{1,0:T(8,128)(2,1)} custom-call(bf16[4,64,384]{2,1,0:T(8,128)(2,1)} %all_to_all.20.refs_0_, bf16[384,3072]{1,0:T(8,128)(2,1)} %refs_1_.7, bf16[384,3072]{1,0:T(8,128)(2,1)} %copy-done), custom_call_target="tpu_custom_call" | custom-call | flops 600000000 | bytes 6000000 | tf_op jit(solution)/shard_map/pallas_call | solution.py:65
  107.0 25.8 %all_to_all.21.refs_0_ = bf16[4,32,3072]{2,1,0:T(8,128)(2,1)S(1)} all-to-all(bf16[4,32,3072]{2,1,0:T(8,128)(2,1)} %bitcast.4), channel_id=1, replica_groups=mesh['x'=4,'y'=4,'zh'=2,'zl'=4,'c'=2] {'zl'}, dimensions={0} | all-to-all | bytes 1572864 | tf_op jit(solution)/shard_map/all_to_all | solution.py:472
  132.7 0.8 shard_map.128
Async XLA Ops:
  0.0 23.2 %collective-permute-start.1 = (bf16[384,3072]{1,0:T(8,128)(2,1)}, bf16[384,3072]{1,0:T(8,128)(2,1)S(1)}, u32[]{:S(2)}, u32[]{:S(2)}) collective-permute-start(bf16[384,3072]{1,0:T(8,128)(2,1)} %refs_1_.7), channel_id=1, source_target_pairs={{0,1},{1,0},{2,3},{3,2},{4,5},{5,4},{6,7},{7,6},{8,9},{9,8},{10,11... | collective-permute-start | bytes 7077896 | tf_op jit(solution)/shard_map/ppermute | solution.py:404
  5.4 15.3 %collective-permute-start = (bf16[272,384]{1,0:T(8,128)(2,1)}, bf16[272,384]{1,0:T(8,128)(2,1)S(1)}, u32[]{:S(2)}, u32[]{:S(2)}) collective-permute-start(bf16[272,384]{1,0:T(8,128)(2,1)} %get-tuple-element.21), channel_id=1, source_target_pairs={{0,8},{8,0},{1,9},{9,1},{2,10},{10,2},{3,11},{11,3},{4,12},{12,4},... | collective-permute-start | bytes 626696 | tf_op jit(solution)/shard_map/ppermute | solution.py:403
  20.7 0.7 copy-start.3
  23.3 18.3 %copy-start = (bf16[384,3072]{1,0:T(8,128)(2,1)}, bf16[384,3072]{1,0:T(8,128)(2,1)S(1)}, u32[]{:S(2)}) copy-start(bf16[384,3072]{1,0:T(8,128)(2,1)S(1)} %collective-permute-done.1.refs_2_) | copy-start | bytes 7077892
  23.3 18.3 %collective-permute-start.2 = (bf16[512,384]{1,0:T(8,128)(2,1)}, bf16[512,384]{1,0:T(8,128)(2,1)S(1)}, u32[]{:S(2)}, u32[]{:S(2)}) collective-permute-start(bf16[512,384]{1,0:T(8,128)(2,1)} %shard_map.121.refs_0_.refs_2_), channel_id=1, source_target_pairs={{0,64},{64,128},{128,192},{1,65},{65,129},{129,193},{2,66},{66,130... | collective-permute-start | bytes 1179656 | tf_op jit(solution)/shard_map/ppermute | solution.py:417
  26.4 28.9 %collective-permute-start.4 = (bf16[512,384]{1,0:T(8,128)(2,1)}, bf16[512,384]{1,0:T(8,128)(2,1)S(1)}, u32[]{:S(2)}, u32[]{:S(2)}) collective-permute-start(bf16[512,384]{1,0:T(8,128)(2,1)} %shard_map.121.refs_0_.refs_2_), channel_id=1, source_target_pairs={{0,32},{16,48},{32,64},{48,80},{64,96},{80,112},{96,128},{112,144}... | collective-permute-start | bytes 1179656 | tf_op jit(solution)/shard_map/ppermute | solution.py:418
  31.4 13.8 %copy-start.2 = (bf16[512,384]{1,0:T(8,128)(2,1)S(1)}, bf16[512,384]{1,0:T(8,128)(2,1)}, u32[]{:S(2)}) copy-start(bf16[512,384]{1,0:T(8,128)(2,1)} %shard_map.121.refs_0_.refs_2_) | copy-start | bytes 1179652
  41.6 0.7 copy-start.6
  44.3 11.0 %collective-permute-start.3 = (bf16[128,384]{1,0:T(8,128)(2,1)}, bf16[128,384]{1,0:T(8,128)(2,1)S(1)}, u32[]{:S(2)}, u32[]{:S(2)}) collective-permute-start(bf16[128,384]{1,0:T(8,128)(2,1)} %get-tuple-element.29), channel_id=1, source_target_pairs={{0,8},{8,0},{1,9},{9,1},{2,10},{10,2},{3,11},{11,3},{4,12},{12,4},... | collective-permute-start | bytes 294920 | tf_op jit(solution)/shard_map/ppermute | solution.py:431
  45.2 23.8 %collective-permute-start.5 = (bf16[512,384]{1,0:T(8,128)(2,1)S(1)}, bf16[512,384]{1,0:T(8,128)(2,1)S(1)}, u32[]{:S(2)}, u32[]{:S(2)}) collective-permute-start(bf16[512,384]{1,0:T(8,128)(2,1)S(1)} %copy-done.2), channel_id=1, source_target_pairs={{0,16},{16,32},{32,48},{48,64},{64,80},{80,96},{96,112},{112,128},... | collective-permute-start | bytes 1179656 | tf_op jit(solution)/shard_map/ppermute | solution.py:418
  47.6 15.4 %all-to-all-start = ((bf16[16,112,128]{2,1,0:T(8,128)(2,1)}), bf16[16,112,128]{2,1,0:T(8,128)(2,1)S(1)}, u32[]{:S(2)}, u32[]{:S(2)}) async-start(bf16[16,112,128]{2,1,0:T(8,128)(2,1)} %get-tuple-element.27), calls=%async_computation | async-start | bytes 917504 | tf_op jit(solution)/shard_map/all_to_all | solution.py:432
  52.8 16.3 %collective-permute-start.6 = (bf16[512,384]{1,0:T(8,128)(2,1)}, bf16[512,384]{1,0:T(8,128)(2,1)S(1)}, u32[]{:S(2)}, u32[]{:S(2)}) collective-permute-start(bf16[512,384]{1,0:T(8,128)(2,1)} %shard_map.122), channel_id=1, source_target_pairs={{0,48},{16,0},{32,16},{48,32},{1,49},{17,1},{33,17},{49,33},{2,50}... | collective-permute-start | bytes 1179656 | tf_op jit(solution)/shard_map/ppermute | solution.py:430
  55.3 0.8 copy-start.10
  55.3 0.8 copy-start.7
  56.1 11.8 %copy-start.8 = (f32[384]{0:T(512)S(1)}, f32[384]{0:T(512)}, u32[]{:S(2)}) copy-start(f32[384]{0:T(512)} %param.22) | copy-start | bytes 4612
  56.1 12.4 %copy-start.9 = (f32[384]{0:T(512)S(1)}, f32[384]{0:T(512)}, u32[]{:S(2)}) copy-start(f32[384]{0:T(512)} %param.21) | copy-start | bytes 4612
  64.1 12.1 %all-to-all-start.1 = ((bf16[16,112,128]{2,1,0:T(8,128)(2,1)}), bf16[16,112,128]{2,1,0:T(8,128)(2,1)S(1)}, u32[]{:S(2)}, u32[]{:S(2)}) async-start(bf16[16,112,128]{2,1,0:T(8,128)(2,1)} %shard_map.124), calls=%async_computation.1 | async-start | bytes 917504 | tf_op jit(solution)/shard_map/all_to_all | solution.py:444
  69.0 0.8 copy-start.4
  69.1 0.9 copy-start.5
  76.3 0.8 copy-start.1

commit v7 on v6

--- a/solution.py
+++ b/solution.py
@@ -203,11 +203,6 @@
     fold_queries(query_ref, pick(q.get(), zh))
 
 
-def relay_body(pair_kv, shifted, out_ref):
-    y = lax.axis_index("y")
-    out_ref[...] = jnp.where(y < 1, pair_kv.get()[...], shifted.get()[...])
-
-
 def join_body(own, recv, out_ref):
     out_ref[0:BLK] = own.get()[0:BLK]
     out_ref[BLK:] = recv.get()[0:BLK]
@@ -317,9 +312,8 @@
     zh = lax.axis_index("zh")
     q_own = queries(own.get())
     q_recv = queries(recv.get())
-    gain_ref = gain_in.get()
     wins = {1: w1.get(), 3: w3.get()}
-    gain = jnp.where(zh == 0, gain_ref[:, :HD], gain_ref[:, HD:])
+    gain = head_gain(gain_in, zh)
     rows_of = ordered_rows(zh)
     stats = stat.get()
     before = acc_in.get()
@@ -339,13 +333,11 @@
 
 def apply_body(pre, even, own, recv, q_mine, q_theirs, g, u, dt, gain_in, att, out_ref, flat_ref):
     zh = lax.axis_index("zh")
-    pre_ref, even_ref, own_ref, recv_ref, gain_ref, att_ref = [
-        x.get() for x in (pre, even, own, recv, gain_in, att)
-    ]
+    pre_ref, even_ref, own_ref, recv_ref, att_ref = [x.get() for x in (pre, even, own, recv, att)]
     for c in range(PAIRS):
         flat_ref[c * CHUNK : (c + 1) * CHUNK, :] = pre_ref[c].astype(F32)[0:CHUNK]
     keep = jnp.where(zh == 0, tail(own_ref)[:, BLK : BLK + 1], tail(recv_ref)[:, BLK : BLK + 1])
-    gain = jnp.where(zh == 0, gain_ref[:, :HD], gain_ref[:, HD:])
+    gain = head_gain(gain_in, zh)
     q_own = queries(q_mine.get())
     q_recv = queries(q_theirs.get())
     base = [x.get()[...] for x in (g, u, dt)]
@@ -392,6 +384,17 @@
     out_ref[...] = sum(ref[i].astype(F32) for i in range(4)).astype(BF16)
 
 
+def behind(pair_kv, distance):
+    return lax.ppermute(pair_kv, ("x", "y"), [(i, i + distance) for i in range(PAIRS - distance)])
+
+
+def head_gain(gain, zh):
+    rows = gain.get()[...]
+    first = jnp.concatenate([rows[0:1], rows[1:2, :64]], axis=1)
+    second = jnp.concatenate([rows[1:2, 64:], rows[2:3]], axis=1)
+    return jnp.where(zh == 0, first, second)
+
+
 def local(q, k, v, rates, decay, step, gate, up, down, ttt_gain, attn_gain, proj):
     sds = jax.ShapeDtypeStruct
     pay = sds((PAY, FD), BF16)
@@ -415,7 +418,7 @@
     (pair_kv,) = call(join_body, [sds((2 * BLK, FD), BF16)], (own, recv), 0, 800_000)
     pair_kv, proj_other = lax.optimization_barrier((pair_kv, proj_other))
     shifted = lax.ppermute(pair_kv, "x", [(i, i + 1) for i in range(3)])
-    w1, w2 = [lax.ppermute(pair_kv, ("x", "y"), [(i, i + o) for i in range(PAIRS - o)]) for o in (1, 2)]
+    w2 = behind(pair_kv, 2)
     even, outgoing = call(
         second_body,
         [mats, sds((PAIRS, CROWS, 128), BF16)],
@@ -425,16 +428,16 @@
         scratch=[flat],
         mine=(1, 2, 3),
     )
-    (behind,) = call(relay_body, [sds((2 * BLK, FD), BF16)], (pair_kv, shifted), 0, 1_000_000)
-    outgoing, behind, send_q = lax.optimization_barrier((outgoing, behind, send_q))
-    w3 = lax.ppermute(behind, "y", [(i, (i + 3) % 4) for i in range(4)])
+    even, later_kv, send_q = lax.optimization_barrier((even, pair_kv, send_q))
+    w1 = behind(later_kv, 1)
+    w3 = behind(later_kv, 3)
     recv_q = lax.ppermute(send_q, "zh", [(0, 1), (1, 0)])
     pieces = lax.all_to_all(outgoing, ("x", "y"), 0, 0, tiled=True)
     acc, stat = call(
         attend_first_body,
         [sds((2, BLK, HD), F32), sds((2, BLK, 128), F32)],
         (own_q, recv_q, pair_kv, shifted, w2),
-        30_000_000_000,
+        500_000_000,
         2_000_000,
         600_000,
         scratch=[pltpu.VMEM((2, 5, BLK, BLK), F32)],
@@ -445,7 +448,7 @@
     (att,) = call(
         attend_second_body,
         [sds((2, BLK, HD), F32)],
-        (own_q, recv_q, w1, w3, acc, stat, attn_gain.reshape(1, FD)),
+        (own_q, recv_q, w1, w3, acc, stat, attn_gain.reshape(3, 128)),
         500_000_000,
         2_000_000,
         600_000,
@@ -454,7 +457,7 @@
     (mixed,) = call(
         apply_body,
         [sds((4, 64, FD), BF16)],
-        (prefix, even, own, recv, own_q, recv_q, gate, up, down, ttt_gain.reshape(1, FD), att),
+        (prefix, even, own, recv, own_q, recv_q, gate, up, down, ttt_gain.reshape(3, 128), att),
         600_000_000,
         5_000_000,
         scratch=[flat],

time: 134 us -> 131 us (0.978)
  starting transfers between devices: 31.5 us -> 34.8 us
  blocking collectives: 47 us -> 44.3 us
  Pallas kernels: 44.8 us -> 42.9 us
  local copies, waits for them, and re-layouts: 5.04 us -> 3.25 us
    all_to_all x1, waiting for transfers between devices: 2.95 us -> 0.01 us  [local(): pieces = lax.all_to_all(outgoing, ('x', 'y'), 0, 0, tiled=True)]
    ppermute x3, starting transfers between devices: 9.91 us -> 12.6 us  [behind(): lax.ppermute(pair_kv, ('x', 'y'), [(i, i + distance) for i in range(PAIRS...]
    all_to_all x1, waiting for transfers between devices: 2.18 us -> 4.44 us  [local(): prefix = lax.all_to_all(sums, ('x', 'y'), 0, 0, tiled=True)]
    all_to_all x1, blocking collectives: 21.2 us -> 19 us  [local(): mixed = lax.all_to_all(mixed, ('c', 'zh'), 0, 0, tiled=True)]
    pallas_call x11 -> x10, Pallas kernels: 44.8 us -> 42.9 us  [call(): pl.pallas_call(kernel, out_shape=outs, in_specs=[any_spec] * n_in, out_sp...]
    all_to_all x1, starting transfers between devices: 3.79 us -> 5.66 us  [local(): prefix = lax.all_to_all(sums, ('x', 'y'), 0, 0, tiled=True)]
    unnamed x22 -> x20, local copies, waits for them, and re-layouts: 3.93 us -> 3.25 us
  transfers between devices with their start and end apart: 9 -> 9, of which waited for: 2 -> 1; matrix products, arithmetic and copies ran while one was open for 1% -> 0% of each run, Pallas kernels for 26% -> 26%
where the time goes in v7:
time: 131 us; the launch traced here: 130 us
  blocking collectives  44.3 us (34%)
  Pallas kernels  42.9 us (33%)
  starting transfers between devices  34.8 us (27%)
  waiting for transfers between devices  4.46 us (3%)
  local copies, waits for them, and re-layouts  3.25 us (2%)
    pallas_call x10, Pallas kernels, call(): pl.pallas_call(kernel, out_shape=outs, in_specs=[any_spec] * n_in, out_sp...  42.9 us
    all_to_all x1, blocking collectives, local(): lax.all_to_all(partial.reshape(4, 32, WIDTH), 'zl', 0, 0, tiled=True)  25.2 us
    all_to_all x1, blocking collectives, local(): mixed = lax.all_to_all(mixed, ('c', 'zh'), 0, 0, tiled=True)  19 us
    ppermute x3, starting transfers between devices, behind(): lax.ppermute(pair_kv, ('x', 'y'), [(i, i + distance) for i in range(PAIRS...  12.6 us
    all_to_all x1, starting transfers between devices, local(): prefix = lax.all_to_all(sums, ('x', 'y'), 0, 0, tiled=True)  5.66 us
    ppermute x1, starting transfers between devices, local(): recv = lax.ppermute(send, 'zh', [(0, 1), (1, 0)])  5.26 us
    all_to_all x1, waiting for transfers between devices, local(): prefix = lax.all_to_all(sums, ('x', 'y'), 0, 0, tiled=True)  4.44 us
    all_to_all x1, starting transfers between devices, local(): pieces = lax.all_to_all(outgoing, ('x', 'y'), 0, 0, tiled=True)  3.91 us
  transfers between devices with their start and end apart: 9, of which 1 were waited for; matrix products, arithmetic and copies ran while one was open for 0% of the time, Pallas kernels for 26%

profile of v7, /device:TPU:1, one launch (start us, length us, event | category | flops | bytes accessed | tf_op | source)
XLA Modules:
  0.0 130.1 jit_solution(13382551885439288347)
XLA Ops:
  0.0 3.2 %collective-permute-start.1 = (bf16[384,3072]{1,0:T(8,128)(2,1)}, bf16[384,3072]{1,0:T(8,128)(2,1)S(1)}, u32[]{:S(2)}, u32[]{:S(2)}) collective-permute-start(bf16[384,3072]{1,0:T(8,128)(2,1)} %refs_1_.7), channel_id=1, source_target_pairs={{0,1},{1,0},{2,3},{3,2},{4,5},{5,4},{6,7},{7,6},{8,9},{9,8},{10,11... | collective-permute-start | bytes 7077896 | tf_op jit(solution)/shard_map/ppermute | solution.py:407
  3.2 2.1 %shard_map.118 = (bf16[272,384]{1,0:T(8,128)(2,1)}, bf16[128,384]{1,0:T(8,128)(2,1)}) custom-call(bf16[256,384]{1,0:T(8,128)(2,1)} %refs_0_.3, bf16[256,384]{1,0:T(8,128)(2,1)} %refs_1_.5, f32[2,256]{1,0:T(2,128)} %bitcast.10, f32[1,2]{1,0:T(1,128)} %refs_3_.3, bf16[256,384]{1,0:T(8,128)(2,1)} %refs_8_.1), custom_call_target="tpu_custom_call" | custom-call | bytes 1000000 | tf_op jit(solution)/shard_map/pallas_call | solution.py:65
  5.4 5.3 %collective-permute-start = (bf16[272,384]{1,0:T(8,128)(2,1)}, bf16[272,384]{1,0:T(8,128)(2,1)S(1)}, u32[]{:S(2)}, u32[]{:S(2)}) collective-permute-start(bf16[272,384]{1,0:T(8,128)(2,1)} %get-tuple-element.21), channel_id=1, source_target_pairs={{0,8},{8,0},{1,9},{9,1},{2,10},{10,2},{3,11},{11,3},{4,12},{12,4},... | collective-permute-start | bytes 626696 | tf_op jit(solution)/shard_map/ppermute | solution.py:406
  10.7 10.0 %shard_map.119 = (f32[3,192,384]{2,1,0:T(8,128)}, bf16[272,384]{1,0:T(8,128)(2,1)}, bf16[128,384]{1,0:T(8,128)(2,1)}) custom-call(bf16[256,384]{1,0:T(8,128)(2,1)} %refs_0_.3, bf16[256,384]{1,0:T(8,128)(2,1)} %refs_1_.5, f32[2,256]{1,0:T(2,128)} %bitcast.11, f32[1,2]{1,0:T(1,128)} %refs_3_.3, f32[2,192,384]{2,1,0:T(8,128)} %refs_6_.1, ...), custom_call_target="tpu_custom_call" | custom-call | flops 6000000000 | bytes 3000000 | tf_op jit(solution)/shard_map/pallas_call | solution.py:65
  20.7 0.0 collective-permute-done.refs_0_.refs_1_.refs_3_
  20.7 0.0 copy-start.2
  20.7 0.7 copy-done.2
  21.4 1.8 %shard_map.121.refs_2_ = bf16[512,384]{1,0:T(8,128)(2,1)} custom-call(bf16[272,384]{1,0:T(8,128)(2,1)} %get-tuple-element.22.refs_5_.refs_0_.refs_2_, bf16[272,384]{1,0:T(8,128)(2,1)} %copy-done.2), custom_call_target="tpu_custom_call" | custom-call | bytes 800000 | tf_op jit(solution)/shard_map/pallas_call | solution.py:65
  23.2 0.0 collective-permute-done.1.refs_2_
  23.2 0.0 copy-start
  23.2 3.1 %collective-permute-start.3 = (bf16[512,384]{1,0:T(8,128)(2,1)}, bf16[512,384]{1,0:T(8,128)(2,1)S(1)}, u32[]{:S(2)}, u32[]{:S(2)}) collective-permute-start(bf16[512,384]{1,0:T(8,128)(2,1)} %shard_map.121.refs_2_), channel_id=1, source_target_pairs={{0,64},{64,128},{128,192},{1,65},{65,129},{129,193},{2,66},{66,130... | collective-permute-start | bytes 1179656 | tf_op jit(solution)/shard_map/ppermute | solution.py:420
  26.4 5.0 %collective-permute-start.4 = (bf16[512,384]{1,0:T(8,128)(2,1)}, bf16[512,384]{1,0:T(8,128)(2,1)S(1)}, u32[]{:S(2)}, u32[]{:S(2)}) collective-permute-start(bf16[512,384]{1,0:T(8,128)(2,1)} %shard_map.121.refs_2_), channel_id=1, source_target_pairs={{0,32},{16,48},{32,64},{48,80},{64,96},{80,112},{96,128},{112,144}... | collective-permute-start | bytes 1179656 | tf_op jit(solution)/shard_map/ppermute | solution.py:388
  31.4 0.0 copy-start.9
  31.4 0.0 copy-start.3
  31.4 10.2 %shard_map.120 = (f32[3,192,384]{2,1,0:T(8,128)}, bf16[16,112,128]{2,1,0:T(8,128)(2,1)}) custom-call(bf16[272,384]{1,0:T(8,128)(2,1)} %copy-done.2, f32[2,192,384]{2,1,0:T(8,128)} %refs_6_.1, f32[2,192,384]{2,1,0:T(8,128)} %refs_7_.1, f32[2,192,384]{2,1,0:T(8,128)} %bitcast.8, f32[1,2]{1,0:T(1,128)} %bitcast.15, ...), custom_call_target="tpu_custom_call" | custom-call | flops 6000000000 | bytes 4000000 | tf_op jit(solution)/shard_map/pallas_call | solution.py:65
  41.6 0.0 copy-done
  41.6 3.9 %all-to-all-start = ((bf16[16,112,128]{2,1,0:T(8,128)(2,1)}), bf16[16,112,128]{2,1,0:T(8,128)(2,1)S(1)}, u32[]{:S(2)}, u32[]{:S(2)}) async-start(bf16[16,112,128]{2,1,0:T(8,128)(2,1)} %get-tuple-element.24), calls=%async_computation | async-start | bytes 917504 | tf_op jit(solution)/shard_map/all_to_all | solution.py:435
  45.5 0.0 copy-done.9
  45.5 1.0 collective-permute-start.2
  46.5 0.0 copy-done.3
  46.5 3.3 %collective-permute-start.5 = (bf16[512,384]{1,0:T(8,128)(2,1)S(1)}, bf16[512,384]{1,0:T(8,128)(2,1)S(1)}, u32[]{:S(2)}, u32[]{:S(2)}) collective-permute-start(bf16[512,384]{1,0:T(8,128)(2,1)S(1)} %copy-done.3), channel_id=1, source_target_pairs={{0,16},{16,32},{32,48},{48,64},{64,80},{80,96},{96,112},{112,128},... | collective-permute-start | bytes 1179656 | tf_op jit(solution)/shard_map/ppermute | solution.py:388
  49.8 4.3 %collective-permute-start.6 = (bf16[512,384]{1,0:T(8,128)(2,1)S(1)}, bf16[512,384]{1,0:T(8,128)(2,1)S(1)}, u32[]{:S(2)}, u32[]{:S(2)}) collective-permute-start(bf16[512,384]{1,0:T(8,128)(2,1)S(1)} %copy-done.3), channel_id=1, source_target_pairs={{0,48},{16,64},{32,80},{48,96},{64,112},{80,128},{96,144},{112,160... | collective-permute-start | bytes 1179656 | tf_op jit(solution)/shard_map/ppermute | solution.py:388
  54.1 0.0 collective-permute-done.2.refs_1_.refs_5_
  54.1 0.0 copy-start.6
  54.1 0.0 collective-permute-done.3.refs_3_
  54.1 0.0 copy-start.7
  54.1 0.0 collective-permute-done.4.refs_4_
  54.1 0.0 copy-start.8
  54.2 0.6 copy-done.6
  54.8 0.1 copy-done.7
  54.9 0.2 copy-done.8
  55.1 3.8 %shard_map.122 = (f32[2,256,192]{2,1,0:T(8,128)}, f32[2,256,128]{2,1,0:T(8,128)}) custom-call(bf16[128,384]{1,0:T(8,128)(2,1)} %get-tuple-element.25.refs_0_.refs_4_, bf16[128,384]{1,0:T(8,128)(2,1)} %copy-done.6, bf16[512,384]{1,0:T(8,128)(2,1)} %shard_map.121.refs_2_, bf16[512,384]{1,0:T(8,128)(2,1)} %copy-done.7, bf16[512,384]{1,0:T(8,128)(2,1)} %copy-done.8), custom_call_target="tpu_custom_call" | custom-call | flops 500000000 | bytes 2000000 | tf_op jit(solution)/shard_map/pallas_call | solution.py:65
  58.9 0.0 all-to-all-done.refs_0_
  58.9 1.2 shard_map.123
  60.1 5.7 %all-to-all-start.1 = ((bf16[16,112,128]{2,1,0:T(8,128)(2,1)}), bf16[16,112,128]{2,1,0:T(8,128)(2,1)S(1)}, u32[]{:S(2)}, u32[]{:S(2)}) async-start(bf16[16,112,128]{2,1,0:T(8,128)(2,1)} %shard_map.123), calls=%async_computation.1 | async-start | bytes 917504 | tf_op jit(solution)/shard_map/all_to_all | solution.py:447
  65.8 0.0 collective-permute-done.5.refs_2_
  65.8 0.0 copy-start.4
  65.8 0.0 collective-permute-done.6.refs_3_
  65.8 0.0 copy-start.5
  65.8 0.7 copy-done.4
  66.5 0.2 copy-done.5
  66.7 4.1 %shard_map.124.refs_10_ = f32[2,256,192]{2,1,0:T(8,128)} custom-call(bf16[128,384]{1,0:T(8,128)(2,1)} %get-tuple-element.25.refs_0_.refs_4_, bf16[128,384]{1,0:T(8,128)(2,1)} %copy-done.6, bf16[512,384]{1,0:T(8,128)(2,1)} %copy-done.4, bf16[512,384]{1,0:T(8,128)(2,1)} %copy-done.5, f32[2,256,192]{2,1,0:T(8,128)} %get-tuple-element.34.refs_4_, ...), custom_call_target="tpu_custom_call" | custom-call | flops 500000000 | bytes 2000000 | tf_op jit(solution)/shard_map/pallas_call | solution.py:65
  70.8 4.4 %all-to-all-done.1.refs_0_ = bf16[16,112,128]{2,1,0:T(8,128)(2,1)S(1)} async-done(((bf16[16,112,128]{2,1,0:T(8,128)(2,1)}), bf16[16,112,128]{2,1,0:T(8,128)(2,1)S(1)}, u32[]{:S(2)}, u32[]{:S(2)}) %all-to-all-start.1) | async-done | bytes 458784 | tf_op jit(solution)/shard_map/all_to_all | solution.py:447
  75.3 0.0 copy-start.1
  75.3 0.8 copy-done.1
  76.0 4.7 %shard_map.125 = bf16[4,64,384]{2,1,0:T(8,128)(2,1)} custom-call(bf16[16,112,128]{2,1,0:T(8,128)(2,1)} %copy-done.1, f32[3,192,384]{2,1,0:T(8,128)} %get-tuple-element.32.refs_1_, bf16[272,384]{1,0:T(8,128)(2,1)} %get-tuple-element.22.refs_5_.refs_0_.refs_2_, bf16[272,384]{1,0:T(8,128)(2,1)} %copy-done.2, ...), custom_call_target="tpu_custom_call" | custom-call | flops 600000000 | bytes 5000000 | tf_op jit(solution)/shard_map/pallas_call | solution.py:65
  80.8 19.0 %all_to_all.20.refs_0_ = bf16[4,64,384]{2,1,0:T(8,128)(2,1)} all-to-all(bf16[4,64,384]{2,1,0:T(8,128)(2,1)} %shard_map.125), channel_id=1, replica_groups=mesh['x'=4,'y'=4,'zh'=2,'zl'=4,'c'=2] {'c','zh'}, dimensions={0} | all-to-all | bytes 393216 | tf_op jit(solution)/shard_map/all_to_all | solution.py:466
  99.8 4.0 %shard_map.126 = bf16[128,3072]{1,0:T(8,128)(2,1)} custom-call(bf16[4,64,384]{2,1,0:T(8,128)(2,1)} %all_to_all.20.refs_0_, bf16[384,3072]{1,0:T(8,128)(2,1)} %refs_1_.7, bf16[384,3072]{1,0:T(8,128)(2,1)} %copy-done), custom_call_target="tpu_custom_call" | custom-call | flops 600000000 | bytes 6000000 | tf_op jit(solution)/shard_map/pallas_call | solution.py:65
  103.8 25.2 %all_to_all.21.refs_0_ = bf16[4,32,3072]{2,1,0:T(8,128)(2,1)S(1)} all-to-all(bf16[4,32,3072]{2,1,0:T(8,128)(2,1)} %bitcast.6), channel_id=1, replica_groups=mesh['x'=4,'y'=4,'zh'=2,'zl'=4,'c'=2] {'zl'}, dimensions={0} | all-to-all | bytes 1572864 | tf_op jit(solution)/shard_map/all_to_all | solution.py:475
  129.0 0.8 shard_map.127
Async XLA Ops:
  0.0 23.2 %collective-permute-start.1 = (bf16[384,3072]{1,0:T(8,128)(2,1)}, bf16[384,3072]{1,0:T(8,128)(2,1)S(1)}, u32[]{:S(2)}, u32[]{:S(2)}) collective-permute-start(bf16[384,3072]{1,0:T(8,128)(2,1)} %refs_1_.7), channel_id=1, source_target_pairs={{0,1},{1,0},{2,3},{3,2},{4,5},{5,4},{6,7},{7,6},{8,9},{9,8},{10,11... | collective-permute-start | bytes 7077896 | tf_op jit(solution)/shard_map/ppermute | solution.py:407
  5.4 15.3 %collective-permute-start = (bf16[272,384]{1,0:T(8,128)(2,1)}, bf16[272,384]{1,0:T(8,128)(2,1)S(1)}, u32[]{:S(2)}, u32[]{:S(2)}) collective-permute-start(bf16[272,384]{1,0:T(8,128)(2,1)} %get-tuple-element.21), channel_id=1, source_target_pairs={{0,8},{8,0},{1,9},{9,1},{2,10},{10,2},{3,11},{11,3},{4,12},{12,4},... | collective-permute-start | bytes 626696 | tf_op jit(solution)/shard_map/ppermute | solution.py:406
  20.7 0.7 copy-start.2
  23.2 18.4 %copy-start = (bf16[384,3072]{1,0:T(8,128)(2,1)}, bf16[384,3072]{1,0:T(8,128)(2,1)S(1)}, u32[]{:S(2)}) copy-start(bf16[384,3072]{1,0:T(8,128)(2,1)S(1)} %collective-permute-done.1.refs_2_) | copy-start | bytes 7077892
  23.2 30.9 %collective-permute-start.3 = (bf16[512,384]{1,0:T(8,128)(2,1)}, bf16[512,384]{1,0:T(8,128)(2,1)S(1)}, u32[]{:S(2)}, u32[]{:S(2)}) collective-permute-start(bf16[512,384]{1,0:T(8,128)(2,1)} %shard_map.121.refs_2_), channel_id=1, source_target_pairs={{0,64},{64,128},{128,192},{1,65},{65,129},{129,193},{2,66},{66,130... | collective-permute-start | bytes 1179656 | tf_op jit(solution)/shard_map/ppermute | solution.py:420
  26.4 27.8 %collective-permute-start.4 = (bf16[512,384]{1,0:T(8,128)(2,1)}, bf16[512,384]{1,0:T(8,128)(2,1)S(1)}, u32[]{:S(2)}, u32[]{:S(2)}) collective-permute-start(bf16[512,384]{1,0:T(8,128)(2,1)} %shard_map.121.refs_2_), channel_id=1, source_target_pairs={{0,32},{16,48},{32,64},{48,80},{64,96},{80,112},{96,128},{112,144}... | collective-permute-start | bytes 1179656 | tf_op jit(solution)/shard_map/ppermute | solution.py:388
  31.4 14.1 %copy-start.9 = (bf16[128,384]{1,0:T(8,128)(2,1)S(1)}, bf16[128,384]{1,0:T(8,128)(2,1)}, u32[]{:S(2)}) copy-start(bf16[128,384]{1,0:T(8,128)(2,1)} %get-tuple-element.29) | copy-start | bytes 294916
  31.4 15.1 %copy-start.3 = (bf16[512,384]{1,0:T(8,128)(2,1)S(1)}, bf16[512,384]{1,0:T(8,128)(2,1)}, u32[]{:S(2)}) copy-start(bf16[512,384]{1,0:T(8,128)(2,1)} %shard_map.121.refs_2_) | copy-start | bytes 1179652
  41.6 17.3 %all-to-all-start = ((bf16[16,112,128]{2,1,0:T(8,128)(2,1)}), bf16[16,112,128]{2,1,0:T(8,128)(2,1)S(1)}, u32[]{:S(2)}, u32[]{:S(2)}) async-start(bf16[16,112,128]{2,1,0:T(8,128)(2,1)} %get-tuple-element.24), calls=%async_computation | async-start | bytes 917504 | tf_op jit(solution)/shard_map/all_to_all | solution.py:435
  45.5 8.6 %collective-permute-start.2 = (bf16[128,384]{1,0:T(8,128)(2,1)S(1)}, bf16[128,384]{1,0:T(8,128)(2,1)S(1)}, u32[]{:S(2)}, u32[]{:S(2)}) collective-permute-start(bf16[128,384]{1,0:T(8,128)(2,1)S(1)} %copy-done.9), channel_id=1, source_target_pairs={{0,8},{8,0},{1,9},{9,1},{2,10},{10,2},{3,11},{11,3},{4,12},{12,4},... | collective-permute-start | bytes 294920 | tf_op jit(solution)/shard_map/ppermute | solution.py:434
  46.5 19.3 %collective-permute-start.5 = (bf16[512,384]{1,0:T(8,128)(2,1)S(1)}, bf16[512,384]{1,0:T(8,128)(2,1)S(1)}, u32[]{:S(2)}, u32[]{:S(2)}) collective-permute-start(bf16[512,384]{1,0:T(8,128)(2,1)S(1)} %copy-done.3), channel_id=1, source_target_pairs={{0,16},{16,32},{32,48},{48,64},{64,80},{80,96},{96,112},{112,128},... | collective-permute-start | bytes 1179656 | tf_op jit(solution)/shard_map/ppermute | solution.py:388
  49.8 16.0 %collective-permute-start.6 = (bf16[512,384]{1,0:T(8,128)(2,1)S(1)}, bf16[512,384]{1,0:T(8,128)(2,1)S(1)}, u32[]{:S(2)}, u32[]{:S(2)}) collective-permute-start(bf16[512,384]{1,0:T(8,128)(2,1)S(1)} %copy-done.3), channel_id=1, source_target_pairs={{0,48},{16,64},{32,80},{48,96},{64,112},{80,128},{96,144},{112,160... | collective-permute-start | bytes 1179656 | tf_op jit(solution)/shard_map/ppermute | solution.py:388
  54.1 0.7 copy-start.6
  54.1 0.8 copy-start.7
  54.1 0.9 copy-start.8
  60.1 15.2 %all-to-all-start.1 = ((bf16[16,112,128]{2,1,0:T(8,128)(2,1)}), bf16[16,112,128]{2,1,0:T(8,128)(2,1)S(1)}, u32[]{:S(2)}, u32[]{:S(2)}) async-start(bf16[16,112,128]{2,1,0:T(8,128)(2,1)} %shard_map.123), calls=%async_computation.1 | async-start | bytes 917504 | tf_op jit(solution)/shard_map/all_to_all | solution.py:447
  65.8 0.8 copy-start.4
  65.8 0.9 copy-start.5
  75.3 0.8 copy-start.1

commit v8 on v7

--- a/solution.py
+++ b/solution.py
@@ -35,10 +35,11 @@
         return self.ref
 
 
-def call(body, outs, ins, flops, nbytes, trans=0, scratch=(), mine=(), cap=VMEM_CAP):
+def call(body, outs, ins, flops, nbytes, trans=0, scratch=(), mine=(), cap=VMEM_CAP, part=None):
+    part = part or {}
     outs = list(outs)
     n_in, n_out = len(ins), len(outs)
-    shapes = [a.shape[1:] if i in mine else a.shape for i, a in enumerate(ins)]
+    shapes = [a.shape[1:] if i in mine or i in part else a.shape for i, a in enumerate(ins)]
 
     def kernel(*refs):
         in_refs, out_refs = refs[:n_in], refs[n_in : n_in + n_out]
@@ -48,7 +49,9 @@
         zh = lax.axis_index("zh")
         lazy = []
         for i in range(n_in):
-            src = in_refs[i].at[zh] if i in mine else in_refs[i]
+            src = in_refs[i]
+            if i in mine or i in part:
+                src = src.at[part.get(i, zh)]
             copy = pltpu.make_async_copy(src, in_vm[i], in_sem.at[i])
             copy.start()
             lazy.append(Lazy(copy, in_vm[i]))
@@ -125,7 +128,7 @@
     out_ref[:, HD:] = q[128:256]
 
 
-def pack_body(k, v, r, d, q, send_ref, query_ref):
+def pack_body(k, v, r, d, send_ref):
     who = 1 - lax.axis_index("zh")
     fill(
         send_ref,
@@ -134,7 +137,6 @@
         one_of(r.get()[...], who),
         jnp.where(who == 0, d.get()[:, 0:1], d.get()[:, 1:2]),
     )
-    fold_queries(query_ref, pick(q.get(), who))
 
 
 def tail(pay_ref):
@@ -192,7 +194,7 @@
     return [scale * x for x in orthogonalize(grads)]
 
 
-def first_body(k, v, r, d, g, u, dt, step, q, upd_ref, own_ref, query_ref):
+def first_body(k, v, r, d, g, u, dt, step, q, upd_ref, own_ref, query_ref, send_ref):
     zh = lax.axis_index("zh")
     key = pick(k.get(), zh)
     value = pick(v.get(), zh)
@@ -201,6 +203,7 @@
     for i, x in enumerate(fast_updates(key, value, rate_row, g, u, dt, step)):
         upd_ref[i] = x
     fold_queries(query_ref, pick(q.get(), zh))
+    fold_queries(send_ref, pick(q.get(), 1 - zh))
 
 
 def join_body(own, recv, out_ref):
@@ -291,11 +294,11 @@
     return lax.axis_index("x") * 4 + lax.axis_index("y")
 
 
-def attend_first_body(own, recv, pair_kv, shifted, w2, acc_ref, stat_ref, score_ref):
+def attend_first_body(own, recv, pair_kv, shifted, w1, acc_ref, stat_ref, score_ref):
     zh = lax.axis_index("zh")
     q_own = queries(own.get())
     q_recv = queries(recv.get())
-    wins = {0: pair_kv.get(), 4: shifted.get(), 2: w2.get()}
+    wins = {0: pair_kv.get(), 4: shifted.get(), 1: w1.get()}
     rows_of = ordered_rows(zh)
     lane = lax.broadcasted_iota(jnp.int32, (BLK, 128), 1)
     for parity in range(2):
@@ -308,11 +311,11 @@
         stat_ref[parity] = jnp.where(lane < 64, top, total)
 
 
-def attend_second_body(own, recv, w1, w3, acc_in, stat, gain_in, out_ref, score_ref):
+def attend_second_body(own, recv, w2, w3, acc_in, stat, gain_in, out_ref, score_ref):
     zh = lax.axis_index("zh")
     q_own = queries(own.get())
     q_recv = queries(recv.get())
-    wins = {1: w1.get(), 3: w3.get()}
+    wins = {2: w2.get(), 3: w3.get()}
     gain = head_gain(gain_in, zh)
     rows_of = ordered_rows(zh)
     stats = stat.get()
@@ -365,17 +368,15 @@
                 ]
 
 
-def project_body(mix, own, other, out_ref):
+def project_body(mix, own_a, own_b, other_a, other_b, out_ref):
     core = lax.axis_index("c")
     mix_ref = mix.get()
     total = None
-    for w, which in ((own, core), (other, 1 - core)):
-        w_ref = w.get()
-        for zh in range(2):
-            part = mix_ref[which * 2 + zh]
-            part = jnp.concatenate([part[:, :HD], part[:, HD:]], axis=0)
-            part = nn(part, w_ref[zh * HD : (zh + 1) * HD, :])
-            total = part if total is None else total + part
+    for zh, w, which in ((0, own_a, core), (1, own_b, core), (0, other_a, 1 - core), (1, other_b, 1 - core)):
+        rows = mix_ref[which * 2 + zh]
+        rows = jnp.concatenate([rows[:, :HD], rows[:, HD:]], axis=0)
+        rows = nn(rows, w.get()[...])
+        total = rows if total is None else total + rows
     out_ref[...] = total.astype(BF16)
 
 
@@ -402,14 +403,14 @@
     down = jnp.swapaxes(down, 1, 2)
     step = step.reshape(1, 2)
     folded = sds((128, FD), BF16)
-    send, send_q = call(pack_body, [pay, folded], (k, v, rates, decay, q), 0, 1_000_000)
+    (send,) = call(pack_body, [pay], (k, v, rates, decay), 0, 1_000_000)
     recv = lax.ppermute(send, "zh", [(0, 1), (1, 0)])
     proj_other = lax.ppermute(proj, "c", [(0, 1), (1, 0)])
     mats = sds((3, HD, FD), F32)
     flat = pltpu.VMEM((PAIRS * CHUNK + 64, 128), F32)
-    upd, own, own_q = call(
+    upd, own, own_q, send_q = call(
         first_body,
-        [mats, pay, folded],
+        [mats, pay, folded, folded],
         (k, v, rates, decay, gate, up, down, step, q),
         6_000_000_000,
         3_000_000,
@@ -418,7 +419,7 @@
     (pair_kv,) = call(join_body, [sds((2 * BLK, FD), BF16)], (own, recv), 0, 800_000)
     pair_kv, proj_other = lax.optimization_barrier((pair_kv, proj_other))
     shifted = lax.ppermute(pair_kv, "x", [(i, i + 1) for i in range(3)])
-    w2 = behind(pair_kv, 2)
+    w1 = behind(pair_kv, 1)
     even, outgoing = call(
         second_body,
         [mats, sds((PAIRS, CROWS, 128), BF16)],
@@ -428,15 +429,15 @@
         scratch=[flat],
         mine=(1, 2, 3),
     )
-    even, later_kv, send_q = lax.optimization_barrier((even, pair_kv, send_q))
-    w1 = behind(later_kv, 1)
+    even, later_kv, later_w1, send_q = lax.optimization_barrier((even, pair_kv, w1, send_q))
+    w2 = behind(later_w1, 1)
     w3 = behind(later_kv, 3)
     recv_q = lax.ppermute(send_q, "zh", [(0, 1), (1, 0)])
     pieces = lax.all_to_all(outgoing, ("x", "y"), 0, 0, tiled=True)
     acc, stat = call(
         attend_first_body,
         [sds((2, BLK, HD), F32), sds((2, BLK, 128), F32)],
-        (own_q, recv_q, pair_kv, shifted, w2),
+        (own_q, recv_q, pair_kv, shifted, w1),
         500_000_000,
         2_000_000,
         600_000,
@@ -448,7 +449,7 @@
     (att,) = call(
         attend_second_body,
         [sds((2, BLK, HD), F32)],
-        (own_q, recv_q, w1, w3, acc, stat, attn_gain.reshape(3, 128)),
+        (own_q, recv_q, w2, w3, acc, stat, attn_gain.reshape(3, 128)),
         500_000_000,
         2_000_000,
         600_000,
@@ -464,13 +465,15 @@
         mine=(6, 7, 8),
     )
     mixed = lax.all_to_all(mixed, ("c", "zh"), 0, 0, tiled=True)
+    own_w = proj.reshape(2, HD, WIDTH)
+    other_w = proj_other.reshape(2, HD, WIDTH)
     (partial,) = call(
         project_body,
         [sds((128, WIDTH), BF16)],
-        (mixed, proj, proj_other),
+        (mixed, own_w, own_w, other_w, other_w),
         600_000_000,
         6_000_000,
-        cap=VMEM_CAP,
+        part={1: 0, 2: 1, 3: 0, 4: 1},
     )
     parts = lax.all_to_all(partial.reshape(4, 32, WIDTH), "zl", 0, 0, tiled=True)
     (result,) = call(total_body, [sds((32, WIDTH), BF16)], (parts,), 400_000, 1_000_000, cap=SMALL)

time: 131 us -> 131 us (level)
    all_to_all x1, starting transfers between devices: 3.91 us -> 6.13 us  [local(): pieces = lax.all_to_all(outgoing, ('x', 'y'), 0, 0, tiled=True)]
    ppermute x3, starting transfers between devices: 12.6 us -> 11 us  [behind(): lax.ppermute(pair_kv, ('x', 'y'), [(i, i + distance) for i in range(PAIRS...]
    unnamed x20 -> x18, local copies, waits for them, and re-layouts: 3.25 us -> 3.08 us
  transfers between devices with their start and end apart: 9 -> 9, of which waited for: 1 -> 1; matrix products, arithmetic and copies ran while one was open for 0% -> 0% of each run, Pallas kernels for 26% -> 25%
where the time goes in v8:
time: 131 us; the launch traced here: 130 us
  blocking collectives  44 us (34%)
  Pallas kernels  42.5 us (32%)
  starting transfers between devices  35.5 us (27%)
  waiting for transfers between devices  4.6 us (4%)
  local copies, waits for them, and re-layouts  3.08 us (2%)
    pallas_call x10, Pallas kernels, call(): pl.pallas_call(kernel, out_shape=outs, in_specs=[any_spec] * n_in, out_sp...  42.5 us
    all_to_all x1, blocking collectives, local(): lax.all_to_all(partial.reshape(4, 32, WIDTH), 'zl', 0, 0, tiled=True)  25.2 us
    all_to_all x1, blocking collectives, local(): mixed = lax.all_to_all(mixed, ('c', 'zh'), 0, 0, tiled=True)  18.8 us
    ppermute x3, starting transfers between devices, behind(): lax.ppermute(pair_kv, ('x', 'y'), [(i, i + distance) for i in range(PAIRS...  11 us
    all_to_all x1, starting transfers between devices, local(): pieces = lax.all_to_all(outgoing, ('x', 'y'), 0, 0, tiled=True)  6.13 us
    all_to_all x1, starting transfers between devices, local(): prefix = lax.all_to_all(sums, ('x', 'y'), 0, 0, tiled=True)  5.76 us
    ppermute x1, starting transfers between devices, local(): recv = lax.ppermute(send, 'zh', [(0, 1), (1, 0)])  5.26 us
    all_to_all x1, waiting for transfers between devices, local(): prefix = lax.all_to_all(sums, ('x', 'y'), 0, 0, tiled=True)  4.58 us
  transfers between devices with their start and end apart: 9, of which 1 were waited for; matrix products, arithmetic and copies ran while one was open for 0% of the time, Pallas kernels for 25%

profile of v8, /device:TPU:1, one launch (start us, length us, event | category | flops | bytes accessed | tf_op | source)
XLA Modules:
  0.0 130.1 jit_solution(4588848787579772455)
XLA Ops:
  0.0 3.2 %collective-permute-start.1 = (bf16[384,3072]{1,0:T(8,128)(2,1)}, bf16[384,3072]{1,0:T(8,128)(2,1)S(1)}, u32[]{:S(2)}, u32[]{:S(2)}) collective-permute-start(bf16[384,3072]{1,0:T(8,128)(2,1)} %param.23), channel_id=1, source_target_pairs={{0,1},{1,0},{2,3},{3,2},{4,5},{5,4},{6,7},{7,6},{8,9},{9,8},{10,11... | collective-permute-start | bytes 7077896 | tf_op jit(solution)/shard_map/ppermute | solution.py:408
  3.2 2.0 %shard_map.118 = bf16[272,384]{1,0:T(8,128)(2,1)} custom-call(bf16[256,384]{1,0:T(8,128)(2,1)} %refs_0_.3, bf16[256,384]{1,0:T(8,128)(2,1)} %refs_1_.4, f32[2,256]{1,0:T(2,128)} %bitcast.16, f32[1,2]{1,0:T(1,128)} %refs_3_.3), custom_call_target="tpu_custom_call" | custom-call | bytes 1000000 | tf_op jit(solution)/shard_map/pallas_call | solution.py:68
  5.3 5.3 %collective-permute-start = (bf16[272,384]{1,0:T(8,128)(2,1)}, bf16[272,384]{1,0:T(8,128)(2,1)S(1)}, u32[]{:S(2)}, u32[]{:S(2)}) collective-permute-start(bf16[272,384]{1,0:T(8,128)(2,1)} %shard_map.118), channel_id=1, source_target_pairs={{0,8},{8,0},{1,9},{9,1},{2,10},{10,2},{3,11},{11,3},{4,12},{12,4},... | collective-permute-start | bytes 626696 | tf_op jit(solution)/shard_map/ppermute | solution.py:407
  10.5 10.1 %shard_map.119 = (f32[3,192,384]{2,1,0:T(8,128)}, bf16[272,384]{1,0:T(8,128)(2,1)}, bf16[128,384]{1,0:T(8,128)(2,1)}, bf16[128,384]{1,0:T(8,128)(2,1)}) custom-call(bf16[256,384]{1,0:T(8,128)(2,1)} %refs_0_.3, bf16[256,384]{1,0:T(8,128)(2,1)} %refs_1_.4, f32[2,256]{1,0:T(2,128)} %bitcast.17, f32[1,2]{1,0:T(1,128)} %refs_3_.3, f32[2,192,384]{2,1,0:T(8,128)} %refs_6_.1, ...), custom_call_target="tpu_custom_call" | custom-call | flops 6000000000 | bytes 3000000 | tf_op jit(solution)/shard_map/pallas_call | solution.py:68
  20.6 0.0 collective-permute-done.refs_0_.refs_1_.refs_3_
  20.6 0.0 copy-start.2
  20.6 0.7 copy-done.2
  21.3 1.8 %shard_map.121.refs_2_ = bf16[512,384]{1,0:T(8,128)(2,1)} custom-call(bf16[272,384]{1,0:T(8,128)(2,1)} %get-tuple-element.21.refs_5_.refs_0_.refs_2_, bf16[272,384]{1,0:T(8,128)(2,1)} %copy-done.2), custom_call_target="tpu_custom_call" | custom-call | bytes 800000 | tf_op jit(solution)/shard_map/pallas_call | solution.py:68
  23.1 0.0 collective-permute-done.1
  23.1 0.0 copy-start
  23.1 3.1 %collective-permute-start.4 = (bf16[512,384]{1,0:T(8,128)(2,1)}, bf16[512,384]{1,0:T(8,128)(2,1)S(1)}, u32[]{:S(2)}, u32[]{:S(2)}) collective-permute-start(bf16[512,384]{1,0:T(8,128)(2,1)} %shard_map.121.refs_2_), channel_id=1, source_target_pairs={{0,64},{64,128},{128,192},{1,65},{65,129},{129,193},{2,66},{66,130... | collective-permute-start | bytes 1179656 | tf_op jit(solution)/shard_map/ppermute | solution.py:421
  26.3 3.4 %collective-permute-start.2 = (bf16[512,384]{1,0:T(8,128)(2,1)}, bf16[512,384]{1,0:T(8,128)(2,1)S(1)}, u32[]{:S(2)}, u32[]{:S(2)}) collective-permute-start(bf16[512,384]{1,0:T(8,128)(2,1)} %shard_map.121.refs_2_), channel_id=1, source_target_pairs={{0,16},{16,32},{32,48},{48,64},{64,80},{80,96},{96,112},{112,128},... | collective-permute-start | bytes 1179656 | tf_op jit(solution)/shard_map/ppermute | solution.py:389
  29.7 0.0 copy-start.3
  29.7 10.2 %shard_map.120 = (f32[3,192,384]{2,1,0:T(8,128)}, bf16[16,112,128]{2,1,0:T(8,128)(2,1)}) custom-call(bf16[272,384]{1,0:T(8,128)(2,1)} %copy-done.2, f32[2,192,384]{2,1,0:T(8,128)} %refs_6_.1, f32[2,192,384]{2,1,0:T(8,128)} %refs_7_.1, f32[2,192,384]{2,1,0:T(8,128)} %bitcast.14, f32[1,2]{1,0:T(1,128)} %bitcast.21, ...), custom_call_target="tpu_custom_call" | custom-call | flops 6000000000 | bytes 4000000 | tf_op jit(solution)/shard_map/pallas_call | solution.py:68
  39.9 0.0 copy-done
  39.9 6.1 %all-to-all-start = ((bf16[16,112,128]{2,1,0:T(8,128)(2,1)}), bf16[16,112,128]{2,1,0:T(8,128)(2,1)S(1)}, u32[]{:S(2)}, u32[]{:S(2)}) async-start(bf16[16,112,128]{2,1,0:T(8,128)(2,1)} %get-tuple-element.23), calls=%async_computation | async-start | bytes 917504 | tf_op jit(solution)/shard_map/all_to_all | solution.py:436
  46.0 0.0 collective-permute-done.2.refs_4_
  46.0 0.0 copy-start.7
  46.0 0.9 collective-permute-start.3
  47.0 3.3 %collective-permute-start.5 = (bf16[512,384]{1,0:T(8,128)(2,1)S(1)}, bf16[512,384]{1,0:T(8,128)(2,1)S(1)}, u32[]{:S(2)}, u32[]{:S(2)}) collective-permute-start(bf16[512,384]{1,0:T(8,128)(2,1)S(1)} %collective-permute-done.2.refs_4_), channel_id=1, source_target_pairs={{0,16},{16,32},{32,48},{48,64},{64,80},{80,96},{96,112},{112,128},... | collective-permute-start | bytes 1179656 | tf_op jit(solution)/shard_map/ppermute | solution.py:389
  50.3 0.0 copy-done.3
  50.3 4.3 %collective-permute-start.6 = (bf16[512,384]{1,0:T(8,128)(2,1)S(1)}, bf16[512,384]{1,0:T(8,128)(2,1)S(1)}, u32[]{:S(2)}, u32[]{:S(2)}) collective-permute-start(bf16[512,384]{1,0:T(8,128)(2,1)S(1)} %copy-done.3), channel_id=1, source_target_pairs={{0,48},{16,64},{32,80},{48,96},{64,112},{80,128},{96,144},{112,160... | collective-permute-start | bytes 1179656 | tf_op jit(solution)/shard_map/ppermute | solution.py:389
  54.6 0.0 collective-permute-done.4.refs_3_
  54.6 0.0 copy-start.8
  54.6 0.0 collective-permute-done.3.refs_1_.refs_5_
  54.6 0.0 copy-start.6
  54.6 0.0 copy-done.7
  54.6 0.7 copy-done.8
  55.3 0.0 copy-done.6
  55.4 3.8 %shard_map.122 = (f32[2,256,192]{2,1,0:T(8,128)}, f32[2,256,128]{2,1,0:T(8,128)}) custom-call(bf16[128,384]{1,0:T(8,128)(2,1)} %get-tuple-element.24.refs_0_.refs_4_, bf16[128,384]{1,0:T(8,128)(2,1)} %copy-done.6, bf16[512,384]{1,0:T(8,128)(2,1)} %shard_map.121.refs_2_, bf16[512,384]{1,0:T(8,128)(2,1)} %copy-done.8, bf16[512,384]{1,0:T(8,128)(2,1)} %copy-done.7), custom_call_target="tpu_custom_call" | custom-call | flops 500000000 | bytes 2000000 | tf_op jit(solution)/shard_map/pallas_call | solution.py:68
  59.2 0.0 all-to-all-done.refs_0_
  59.2 1.2 shard_map.123
  60.4 5.8 %all-to-all-start.1 = ((bf16[16,112,128]{2,1,0:T(8,128)(2,1)}), bf16[16,112,128]{2,1,0:T(8,128)(2,1)S(1)}, u32[]{:S(2)}, u32[]{:S(2)}) async-start(bf16[16,112,128]{2,1,0:T(8,128)(2,1)} %shard_map.123), calls=%async_computation.1 | async-start | bytes 917504 | tf_op jit(solution)/shard_map/all_to_all | solution.py:448
  66.1 0.0 collective-permute-done.5.refs_2_
  66.2 0.0 copy-start.4
  66.2 0.0 collective-permute-done.6.refs_3_
  66.2 0.0 copy-start.5
  66.2 0.7 copy-done.4
  66.9 0.1 copy-done.5
  67.1 4.1 %shard_map.124.refs_10_ = f32[2,256,192]{2,1,0:T(8,128)} custom-call(bf16[128,384]{1,0:T(8,128)(2,1)} %get-tuple-element.24.refs_0_.refs_4_, bf16[128,384]{1,0:T(8,128)(2,1)} %copy-done.6, bf16[512,384]{1,0:T(8,128)(2,1)} %copy-done.4, bf16[512,384]{1,0:T(8,128)(2,1)} %copy-done.5, f32[2,256,192]{2,1,0:T(8,128)} %get-tuple-element.34.refs_4_, ...), custom_call_target="tpu_custom_call" | custom-call | flops 500000000 | bytes 2000000 | tf_op jit(solution)/shard_map/pallas_call | solution.py:68
  71.2 4.6 %all-to-all-done.1.refs_0_ = bf16[16,112,128]{2,1,0:T(8,128)(2,1)S(1)} async-done(((bf16[16,112,128]{2,1,0:T(8,128)(2,1)}), bf16[16,112,128]{2,1,0:T(8,128)(2,1)S(1)}, u32[]{:S(2)}, u32[]{:S(2)}) %all-to-all-start.1) | async-done | bytes 458784 | tf_op jit(solution)/shard_map/all_to_all | solution.py:448
  75.8 0.0 copy-start.1
  75.8 0.8 copy-done.1
  76.5 4.7 %shard_map.125 = bf16[4,64,384]{2,1,0:T(8,128)(2,1)} custom-call(bf16[16,112,128]{2,1,0:T(8,128)(2,1)} %copy-done.1, f32[3,192,384]{2,1,0:T(8,128)} %get-tuple-element.31.refs_1_, bf16[272,384]{1,0:T(8,128)(2,1)} %get-tuple-element.21.refs_5_.refs_0_.refs_2_, bf16[272,384]{1,0:T(8,128)(2,1)} %copy-done.2, ...), custom_call_target="tpu_custom_call" | custom-call | flops 600000000 | bytes 5000000 | tf_op jit(solution)/shard_map/pallas_call | solution.py:68
  81.3 18.8 %all_to_all.20.refs_0_ = bf16[4,64,384]{2,1,0:T(8,128)(2,1)} all-to-all(bf16[4,64,384]{2,1,0:T(8,128)(2,1)} %shard_map.125), channel_id=1, replica_groups=mesh['x'=4,'y'=4,'zh'=2,'zl'=4,'c'=2] {'c','zh'}, dimensions={0} | all-to-all | bytes 393216 | tf_op jit(solution)/shard_map/all_to_all | solution.py:467
  100.1 3.8 %shard_map.126 = bf16[128,3072]{1,0:T(8,128)(2,1)} custom-call(bf16[4,64,384]{2,1,0:T(8,128)(2,1)} %all_to_all.20.refs_0_, bf16[2,192,3072]{2,1,0:T(8,128)(2,1)} %bitcast.8, bf16[2,192,3072]{2,1,0:T(8,128)(2,1)} %bitcast.9, bf16[2,192,3072]{2,1,0:T(8,128)(2,1)} %bitcast.10, bf16[2,192,3072]{2,1,0:T(8,128)(2,1)} %bitcast.11), custom_call_target="tpu_custom_call" | custom-call | flops 600000000 | bytes 6000000 | tf_op jit(solution)/shard_map/pallas_call | solution.py:68
  103.8 25.2 %all_to_all.21.refs_0_ = bf16[4,32,3072]{2,1,0:T(8,128)(2,1)S(1)} all-to-all(bf16[4,32,3072]{2,1,0:T(8,128)(2,1)} %bitcast.12), channel_id=1, replica_groups=mesh['x'=4,'y'=4,'zh'=2,'zl'=4,'c'=2] {'zl'}, dimensions={0} | all-to-all | bytes 1572864 | tf_op jit(solution)/shard_map/all_to_all | solution.py:478
  129.1 0.8 shard_map.127
Async XLA Ops:
  0.0 23.1 %collective-permute-start.1 = (bf16[384,3072]{1,0:T(8,128)(2,1)}, bf16[384,3072]{1,0:T(8,128)(2,1)S(1)}, u32[]{:S(2)}, u32[]{:S(2)}) collective-permute-start(bf16[384,3072]{1,0:T(8,128)(2,1)} %param.23), channel_id=1, source_target_pairs={{0,1},{1,0},{2,3},{3,2},{4,5},{5,4},{6,7},{7,6},{8,9},{9,8},{10,11... | collective-permute-start | bytes 7077896 | tf_op jit(solution)/shard_map/ppermute | solution.py:408
  5.3 15.3 %collective-permute-start = (bf16[272,384]{1,0:T(8,128)(2,1)}, bf16[272,384]{1,0:T(8,128)(2,1)S(1)}, u32[]{:S(2)}, u32[]{:S(2)}) collective-permute-start(bf16[272,384]{1,0:T(8,128)(2,1)} %shard_map.118), channel_id=1, source_target_pairs={{0,8},{8,0},{1,9},{9,1},{2,10},{10,2},{3,11},{11,3},{4,12},{12,4},... | collective-permute-start | bytes 626696 | tf_op jit(solution)/shard_map/ppermute | solution.py:407
  20.6 0.7 copy-start.2
  23.1 16.7 %copy-start = (bf16[384,3072]{1,0:T(8,128)(2,1)}, bf16[384,3072]{1,0:T(8,128)(2,1)S(1)}, u32[]{:S(2)}) copy-start(bf16[384,3072]{1,0:T(8,128)(2,1)S(1)} %collective-permute-done.1) | copy-start | bytes 7077892
  23.1 31.4 %collective-permute-start.4 = (bf16[512,384]{1,0:T(8,128)(2,1)}, bf16[512,384]{1,0:T(8,128)(2,1)S(1)}, u32[]{:S(2)}, u32[]{:S(2)}) collective-permute-start(bf16[512,384]{1,0:T(8,128)(2,1)} %shard_map.121.refs_2_), channel_id=1, source_target_pairs={{0,64},{64,128},{128,192},{1,65},{65,129},{129,193},{2,66},{66,130... | collective-permute-start | bytes 1179656 | tf_op jit(solution)/shard_map/ppermute | solution.py:421
  26.3 19.7 %collective-permute-start.2 = (bf16[512,384]{1,0:T(8,128)(2,1)}, bf16[512,384]{1,0:T(8,128)(2,1)S(1)}, u32[]{:S(2)}, u32[]{:S(2)}) collective-permute-start(bf16[512,384]{1,0:T(8,128)(2,1)} %shard_map.121.refs_2_), channel_id=1, source_target_pairs={{0,16},{16,32},{32,48},{48,64},{64,80},{80,96},{96,112},{112,128},... | collective-permute-start | bytes 1179656 | tf_op jit(solution)/shard_map/ppermute | solution.py:389
  29.7 20.6 %copy-start.3 = (bf16[512,384]{1,0:T(8,128)(2,1)S(1)}, bf16[512,384]{1,0:T(8,128)(2,1)}, u32[]{:S(2)}) copy-start(bf16[512,384]{1,0:T(8,128)(2,1)} %shard_map.121.refs_2_) | copy-start | bytes 1179652
  39.9 19.3 %all-to-all-start = ((bf16[16,112,128]{2,1,0:T(8,128)(2,1)}), bf16[16,112,128]{2,1,0:T(8,128)(2,1)S(1)}, u32[]{:S(2)}, u32[]{:S(2)}) async-start(bf16[16,112,128]{2,1,0:T(8,128)(2,1)} %get-tuple-element.23), calls=%async_computation | async-start | bytes 917504 | tf_op jit(solution)/shard_map/all_to_all | solution.py:436
  46.0 8.6 %copy-start.7 = (bf16[512,384]{1,0:T(8,128)(2,1)}, bf16[512,384]{1,0:T(8,128)(2,1)S(1)}, u32[]{:S(2)}) copy-start(bf16[512,384]{1,0:T(8,128)(2,1)S(1)} %collective-permute-done.2.refs_4_) | copy-start | bytes 1179652
  46.0 8.6 %collective-permute-start.3 = (bf16[128,384]{1,0:T(8,128)(2,1)}, bf16[128,384]{1,0:T(8,128)(2,1)S(1)}, u32[]{:S(2)}, u32[]{:S(2)}) collective-permute-start(bf16[128,384]{1,0:T(8,128)(2,1)} %get-tuple-element.28), channel_id=1, source_target_pairs={{0,8},{8,0},{1,9},{9,1},{2,10},{10,2},{3,11},{11,3},{4,12},{12,4},... | collective-permute-start | bytes 294920 | tf_op jit(solution)/shard_map/ppermute | solution.py:435
  47.0 19.2 %collective-permute-start.5 = (bf16[512,384]{1,0:T(8,128)(2,1)S(1)}, bf16[512,384]{1,0:T(8,128)(2,1)S(1)}, u32[]{:S(2)}, u32[]{:S(2)}) collective-permute-start(bf16[512,384]{1,0:T(8,128)(2,1)S(1)} %collective-permute-done.2.refs_4_), channel_id=1, source_target_pairs={{0,16},{16,32},{32,48},{48,64},{64,80},{80,96},{96,112},{112,128},... | collective-permute-start | bytes 1179656 | tf_op jit(solution)/shard_map/ppermute | solution.py:389
  50.3 15.9 %collective-permute-start.6 = (bf16[512,384]{1,0:T(8,128)(2,1)S(1)}, bf16[512,384]{1,0:T(8,128)(2,1)S(1)}, u32[]{:S(2)}, u32[]{:S(2)}) collective-permute-start(bf16[512,384]{1,0:T(8,128)(2,1)S(1)} %copy-done.3), channel_id=1, source_target_pairs={{0,48},{16,64},{32,80},{48,96},{64,112},{80,128},{96,144},{112,160... | collective-permute-start | bytes 1179656 | tf_op jit(solution)/shard_map/ppermute | solution.py:389
  54.6 0.7 copy-start.8
  54.6 0.8 copy-start.6
  60.4 15.4 %all-to-all-start.1 = ((bf16[16,112,128]{2,1,0:T(8,128)(2,1)}), bf16[16,112,128]{2,1,0:T(8,128)(2,1)S(1)}, u32[]{:S(2)}, u32[]{:S(2)}) async-start(bf16[16,112,128]{2,1,0:T(8,128)(2,1)} %shard_map.123), calls=%async_computation.1 | async-start | bytes 917504 | tf_op jit(solution)/shard_map/all_to_all | solution.py:448
  66.2 0.8 copy-start.4
  66.2 0.9 copy-start.5
  75.8 0.8 copy-start.1

commit v9 on v8

--- a/solution.py
+++ b/solution.py
@@ -35,8 +35,9 @@
         return self.ref
 
 
-def call(body, outs, ins, flops, nbytes, trans=0, scratch=(), mine=(), cap=VMEM_CAP, part=None):
+def call(body, outs, ins, flops, nbytes, trans=0, scratch=(), mine=(), cap=VMEM_CAP, part=None, head_rows=None):
     part = part or {}
+    head_rows = head_rows or {}
     outs = list(outs)
     n_in, n_out = len(ins), len(outs)
     shapes = [a.shape[1:] if i in mine or i in part else a.shape for i, a in enumerate(ins)]
@@ -55,7 +56,10 @@
             copy = pltpu.make_async_copy(src, in_vm[i], in_sem.at[i])
             copy.start()
             lazy.append(Lazy(copy, in_vm[i]))
-        copies = [pltpu.make_async_copy(out_vm[i], out_refs[i], out_sem.at[i]) for i in range(n_out)]
+        copies = []
+        for i in range(n_out):
+            dst = out_refs[i].at[0 : head_rows[i]] if i in head_rows else out_refs[i]
+            copies.append(pltpu.make_async_copy(out_vm[i], dst, out_sem.at[i]))
         body(*lazy, *out_vm, *extra)
         for copy in copies:
             copy.start()
@@ -71,7 +75,7 @@
         in_specs=[any_spec] * n_in,
         out_specs=[any_spec] * n_out,
         scratch_shapes=[pltpu.VMEM(sh, a.dtype) for sh, a in zip(shapes, ins)]
-        + [pltpu.VMEM(o.shape, o.dtype) for o in outs]
+        + [pltpu.VMEM((head_rows.get(i, o.shape[0]),) + o.shape[1:], o.dtype) for i, o in enumerate(outs)]
         + [pltpu.SemaphoreType.DMA((n_in,)), pltpu.SemaphoreType.DMA((n_out,))]
         + list(scratch),
         compiler_params=pltpu.CompilerParams(vmem_limit_bytes=cap),
@@ -206,19 +210,14 @@
     fold_queries(send_ref, pick(q.get(), 1 - zh))
 
 
-def join_body(own, recv, out_ref):
-    out_ref[0:BLK] = own.get()[0:BLK]
-    out_ref[BLK:] = recv.get()[0:BLK]
-
-
-def second_body(pay, g, u, dt, step, own, upd, even_ref, send_ref, flat_ref):
-    pay_ref = pay.get()
+def second_body(pair_kv, g, u, dt, step, upd, even_ref, send_ref, flat_ref):
+    pay_ref = pair_kv.get().at[PAY:]
     others = fast_updates(
         pay_ref[0:BLK, 0:HD], pay_ref[0:BLK, HD:], tail(pay_ref)[:, :BLK], g, u, dt, step
     )
     zh = lax.axis_index("zh")
     upd_ref = upd.get()
-    mine = tail(own.get())[:, BLK:]
+    mine = tail(pair_kv.get())[:, BLK:]
     theirs = tail(pay_ref)[:, BLK:]
     keep_even = jnp.where(zh == 0, mine, theirs)
     keep_odd = jnp.where(zh == 0, theirs, mine)
@@ -285,7 +284,7 @@
 def ordered_rows(zh):
     def rows_of(parity):
         slot = zh if parity == 0 else 1 - zh
-        return pl.ds(pl.multiple_of(slot * BLK, BLK), BLK)
+        return pl.ds(pl.multiple_of(slot * PAY, 16), BLK)
 
     return rows_of
 
@@ -334,9 +333,10 @@
         out_ref[parity] = att * norm * gain
 
 
-def apply_body(pre, even, own, recv, q_mine, q_theirs, g, u, dt, gain_in, att, out_ref, flat_ref):
+def apply_body(pre, even, pair_kv, q_mine, q_theirs, g, u, dt, gain_in, att, out_ref, flat_ref):
     zh = lax.axis_index("zh")
-    pre_ref, even_ref, own_ref, recv_ref, att_ref = [x.get() for x in (pre, even, own, recv, att)]
+    pre_ref, even_ref, own_ref, att_ref = [x.get() for x in (pre, even, pair_kv, att)]
+    recv_ref = own_ref.at[PAY:]
     for c in range(PAIRS):
         flat_ref[c * CHUNK : (c + 1) * CHUNK, :] = pre_ref[c].astype(F32)[0:CHUNK]
     keep = jnp.where(zh == 0, tail(own_ref)[:, BLK : BLK + 1], tail(recv_ref)[:, BLK : BLK + 1])
@@ -410,20 +410,21 @@
     flat = pltpu.VMEM((PAIRS * CHUNK + 64, 128), F32)
     upd, own, own_q, send_q = call(
         first_body,
-        [mats, pay, folded, folded],
+        [mats, sds((2 * PAY, FD), BF16), folded, folded],
         (k, v, rates, decay, gate, up, down, step, q),
         6_000_000_000,
         3_000_000,
         mine=(4, 5, 6),
-    )
-    (pair_kv,) = call(join_body, [sds((2 * BLK, FD), BF16)], (own, recv), 0, 800_000)
+        head_rows={1: PAY},
+    )
+    pair_kv = lax.dynamic_update_slice(own, recv, (PAY, 0))
     pair_kv, proj_other = lax.optimization_barrier((pair_kv, proj_other))
     shifted = lax.ppermute(pair_kv, "x", [(i, i + 1) for i in range(3)])
     w1 = behind(pair_kv, 1)
     even, outgoing = call(
         second_body,
         [mats, sds((PAIRS, CROWS, 128), BF16)],
-        (recv, gate, up, down, step, own, upd),
+        (pair_kv, gate, up, down, step, upd),
         6_000_000_000,
         4_000_000,
         scratch=[flat],
@@ -433,7 +434,9 @@
     w2 = behind(later_w1, 1)
     w3 = behind(later_kv, 3)
     recv_q = lax.ppermute(send_q, "zh", [(0, 1), (1, 0)])
+    outgoing, shifted, w1 = lax.optimization_barrier((outgoing, shifted, w1))
     pieces = lax.all_to_all(outgoing, ("x", "y"), 0, 0, tiled=True)
+    pieces, recv_q = lax.optimization_barrier((pieces, recv_q))
     acc, stat = call(
         attend_first_body,
         [sds((2, BLK, HD), F32), sds((2, BLK, 128), F32)],
@@ -443,7 +446,6 @@
         600_000,
         scratch=[pltpu.VMEM((2, 5, BLK, BLK), F32)],
     )
-    pieces, acc = lax.optimization_barrier((pieces, acc))
     (sums,) = call(scan_body, [sds((PAIRS, CROWS, 128), BF16)], (pieces,), 500_000, 1_000_000, cap=SMALL)
     prefix = lax.all_to_all(sums, ("x", "y"), 0, 0, tiled=True)
     (att,) = call(
@@ -458,11 +460,11 @@
     (mixed,) = call(
         apply_body,
         [sds((4, 64, FD), BF16)],
-        (prefix, even, own, recv, own_q, recv_q, gate, up, down, ttt_gain.reshape(3, 128), att),
+        (prefix, even, pair_kv, own_q, recv_q, gate, up, down, ttt_gain.reshape(3, 128), att),
         600_000_000,
         5_000_000,
         scratch=[flat],
-        mine=(6, 7, 8),
+        mine=(5, 6, 7),
     )
     mixed = lax.all_to_all(mixed, ("c", "zh"), 0, 0, tiled=True)
     own_w = proj.reshape(2, HD, WIDTH)

time: 131 us -> 134 us (1.023)
  starting transfers between devices: 35.5 us -> 39.8 us
  waiting for transfers between devices: 4.6 us -> 8.51 us
  blocking collectives: 44 us -> 41.3 us
  Pallas kernels: 42.5 us -> 40.9 us
    all_to_all x1, starting transfers between devices: 6.13 us -> 11 us  [local(): pieces = lax.all_to_all(outgoing, ('x', 'y'), 0, 0, tiled=True)]
    all_to_all x1, waiting for transfers between devices: 4.58 us -> 7.64 us  [local(): prefix = lax.all_to_all(sums, ('x', 'y'), 0, 0, tiled=True)]
    all_to_all x1, blocking collectives: 18.8 us -> 17 us  [local(): mixed = lax.all_to_all(mixed, ('c', 'zh'), 0, 0, tiled=True)]
    pallas_call x10 -> x9, Pallas kernels: 42.5 us -> 40.9 us  [call(): pl.pallas_call(kernel, out_shape=outs, in_specs=[any_spec] * n_in, out_sp...]
    unnamed x18 -> x16, local copies, waits for them, and re-layouts: 3.08 us -> 1.67 us
  transfers between devices with their start and end apart: 9 -> 9, of which waited for: 1 -> 2; matrix products, arithmetic and copies ran while one was open for 0% -> 1% of each run, Pallas kernels for 25% -> 24%
where the time goes in v9:
time: 134 us; the launch traced here: 133 us
  blocking collectives  41.3 us (31%)
  Pallas kernels  40.9 us (31%)
  starting transfers between devices  39.8 us (30%)
  waiting for transfers between devices  8.51 us (6%)
  local copies, waits for them, and re-layouts  2.4 us (2%)
    pallas_call x9, Pallas kernels, call(): pl.pallas_call(kernel, out_shape=outs, in_specs=[any_spec] * n_in, out_sp...  40.9 us
    all_to_all x1, blocking collectives, local(): lax.all_to_all(partial.reshape(4, 32, WIDTH), 'zl', 0, 0, tiled=True)  24.4 us
    all_to_all x1, blocking collectives, local(): mixed = lax.all_to_all(mixed, ('c', 'zh'), 0, 0, tiled=True)  17 us
    all_to_all x1, starting transfers between devices, local(): pieces = lax.all_to_all(outgoing, ('x', 'y'), 0, 0, tiled=True)  11 us
    ppermute x3, starting transfers between devices, behind(): lax.ppermute(pair_kv, ('x', 'y'), [(i, i + distance) for i in range(PAIRS...  10.8 us
    all_to_all x1, waiting for transfers between devices, local(): prefix = lax.all_to_all(sums, ('x', 'y'), 0, 0, tiled=True)  7.64 us
    all_to_all x1, starting transfers between devices, local(): prefix = lax.all_to_all(sums, ('x', 'y'), 0, 0, tiled=True)  5.55 us
    ppermute x1, starting transfers between devices, local(): recv = lax.ppermute(send, 'zh', [(0, 1), (1, 0)])  5.26 us
  transfers between devices with their start and end apart: 9, of which 2 were waited for; matrix products, arithmetic and copies ran while one was open for 1% of the time, Pallas kernels for 24%

profile of v9, /device:TPU:1, one launch (start us, length us, event | category | flops | bytes accessed | tf_op | source)
XLA Modules:
  0.0 133.3 jit_solution(14402014970082856746)
XLA Ops:
  0.0 3.2 %collective-permute-start.1 = (bf16[384,3072]{1,0:T(8,128)(2,1)}, bf16[384,3072]{1,0:T(8,128)(2,1)S(1)}, u32[]{:S(2)}, u32[]{:S(2)}) collective-permute-start(bf16[384,3072]{1,0:T(8,128)(2,1)} %param.23), channel_id=1, source_target_pairs={{0,1},{1,0},{2,3},{3,2},{4,5},{5,4},{6,7},{7,6},{8,9},{9,8},{10,11... | collective-permute-start | bytes 7077896 | tf_op jit(solution)/shard_map/ppermute | solution.py:408
  3.2 2.0 %shard_map.119 = bf16[272,384]{1,0:T(8,128)(2,1)} custom-call(bf16[256,384]{1,0:T(8,128)(2,1)} %refs_0_.3, bf16[256,384]{1,0:T(8,128)(2,1)} %refs_1_.4, f32[2,256]{1,0:T(2,128)} %bitcast.16, f32[1,2]{1,0:T(1,128)} %refs_3_.3), custom_call_target="tpu_custom_call" | custom-call | bytes 1000000 | tf_op jit(solution)/shard_map/pallas_call | solution.py:72
  5.2 5.3 %collective-permute-start = (bf16[272,384]{1,0:T(8,128)(2,1)}, bf16[272,384]{1,0:T(8,128)(2,1)S(1)}, u32[]{:S(2)}, u32[]{:S(2)}) collective-permute-start(bf16[272,384]{1,0:T(8,128)(2,1)} %shard_map.119), channel_id=1, source_target_pairs={{0,8},{8,0},{1,9},{9,1},{2,10},{10,2},{3,11},{11,3},{4,12},{12,4},... | collective-permute-start | bytes 626696 | tf_op jit(solution)/shard_map/ppermute | solution.py:407
  10.5 10.1 %shard_map.118 = (f32[3,192,384]{2,1,0:T(8,128)}, bf16[544,384]{1,0:T(8,128)(2,1)}, bf16[128,384]{1,0:T(8,128)(2,1)}, bf16[128,384]{1,0:T(8,128)(2,1)}) custom-call(bf16[256,384]{1,0:T(8,128)(2,1)} %refs_0_.3, bf16[256,384]{1,0:T(8,128)(2,1)} %refs_1_.4, f32[2,256]{1,0:T(2,128)} %bitcast.17, f32[1,2]{1,0:T(1,128)} %refs_3_.3, f32[2,192,384]{2,1,0:T(8,128)} %refs_5_.3, ...), custom_call_target="tpu_custom_call" | custom-call | flops 6000000000 | bytes 3000000 | tf_op jit(solution)/shard_map/pallas_call | solution.py:72
  20.6 0.0 collective-permute-done
  20.6 0.7 constant_dynamic-update-slice_fusion.refs_0_.refs_2_
  21.4 0.0 collective-permute-done.1
  21.4 0.0 copy-start
  21.4 3.2 %collective-permute-start.3 = (bf16[544,384]{1,0:T(8,128)(2,1)}, bf16[544,384]{1,0:T(8,128)(2,1)S(1)}, u32[]{:S(2)}, u32[]{:S(2)}) collective-permute-start(bf16[544,384]{1,0:T(8,128)(2,1)} %constant_dynamic-update-slice_fusion.refs_0_.refs_2_), channel_id=1, source_target_pairs={{0,16},{16,32},{32,48},{48,64},{64,80},{80,96},{96,112},{112,128},... | collective-permute-start | bytes 1253384 | tf_op jit(solution)/shard_map/ppermute | solution.py:389
  24.6 3.9 %collective-permute-start.2 = (bf16[544,384]{1,0:T(8,128)(2,1)}, bf16[544,384]{1,0:T(8,128)(2,1)}, u32[]{:S(2)}, u32[]{:S(2)}) collective-permute-start(bf16[544,384]{1,0:T(8,128)(2,1)} %constant_dynamic-update-slice_fusion.refs_0_.refs_2_), channel_id=1, source_target_pairs={{0,64},{64,128},{128,192},{1,65},{65,129},{129,193},{2,66},{66,130... | collective-permute-start | bytes 1253384 | tf_op jit(solution)/shard_map/ppermute | solution.py:422
  28.5 0.0 copy-start.7
  28.5 0.0 copy-start.4
  28.5 10.2 %shard_map.120 = (f32[3,192,384]{2,1,0:T(8,128)}, bf16[16,112,128]{2,1,0:T(8,128)(2,1)}) custom-call(bf16[544,384]{1,0:T(8,128)(2,1)} %constant_dynamic-update-slice_fusion.refs_0_.refs_2_, f32[2,192,384]{2,1,0:T(8,128)} %refs_5_.3, f32[2,192,384]{2,1,0:T(8,128)} %refs_6_.1, f32[2,192,384]{2,1,0:T(8,128)} %bitcast.14, f32[1,2]{1,0:T(1,128)} %bitcast.21, ...), custom_call_target="tpu_custom_call" | custom-call | flops 6000000000 | bytes 4000000 | tf_op jit(solution)/shard_map/pallas_call | solution.py:72
  38.7 0.0 copy-done
  38.7 0.0 collective-permute-done.3.refs_4_
  38.7 0.0 copy-start.6
  38.7 0.0 collective-permute-done.2.refs_3_
  38.7 11.0 %all-to-all-start = ((bf16[16,112,128]{2,1,0:T(8,128)(2,1)}), bf16[16,112,128]{2,1,0:T(8,128)(2,1)S(1)}, u32[]{:S(2)}, u32[]{:S(2)}) async-start(bf16[16,112,128]{2,1,0:T(8,128)(2,1)} %get-tuple-element.28), calls=%async_computation | async-start | bytes 917504 | tf_op jit(solution)/shard_map/all_to_all | solution.py:438
  49.7 0.0 copy-done.7
  49.7 0.1 collective-permute-start.4
  49.8 3.3 %collective-permute-start.5 = (bf16[544,384]{1,0:T(8,128)(2,1)S(1)}, bf16[544,384]{1,0:T(8,128)(2,1)S(1)}, u32[]{:S(2)}, u32[]{:S(2)}) collective-permute-start(bf16[544,384]{1,0:T(8,128)(2,1)S(1)} %collective-permute-done.3.refs_4_), channel_id=1, source_target_pairs={{0,16},{16,32},{32,48},{48,64},{64,80},{80,96},{96,112},{112,128},... | collective-permute-start | bytes 1253384 | tf_op jit(solution)/shard_map/ppermute | solution.py:389
  53.1 0.0 copy-done.4
  53.1 4.3 %collective-permute-start.6 = (bf16[544,384]{1,0:T(8,128)(2,1)S(1)}, bf16[544,384]{1,0:T(8,128)(2,1)S(1)}, u32[]{:S(2)}, u32[]{:S(2)}) collective-permute-start(bf16[544,384]{1,0:T(8,128)(2,1)S(1)} %copy-done.4), channel_id=1, source_target_pairs={{0,48},{16,64},{32,80},{48,96},{64,112},{80,128},{96,144},{112,160... | collective-permute-start | bytes 1253384 | tf_op jit(solution)/shard_map/ppermute | solution.py:389
  57.4 0.0 collective-permute-done.4.refs_1_.refs_4_
  57.5 0.0 copy-start.5
  57.5 0.9 all-to-all-done.refs_0_
  58.3 1.2 shard_map.121
  59.5 5.5 %all-to-all-start.1 = ((bf16[16,112,128]{2,1,0:T(8,128)(2,1)}), bf16[16,112,128]{2,1,0:T(8,128)(2,1)S(1)}, u32[]{:S(2)}, u32[]{:S(2)}) async-start(bf16[16,112,128]{2,1,0:T(8,128)(2,1)} %shard_map.121), calls=%async_computation.1 | async-start | bytes 917504 | tf_op jit(solution)/shard_map/all_to_all | solution.py:450
  65.0 0.0 copy-done.6
  65.1 0.0 copy-done.5
  65.1 3.9 %shard_map.122 = (f32[2,256,192]{2,1,0:T(8,128)}, f32[2,256,128]{2,1,0:T(8,128)}) custom-call(bf16[128,384]{1,0:T(8,128)(2,1)} %get-tuple-element.34.refs_0_.refs_3_, bf16[128,384]{1,0:T(8,128)(2,1)} %copy-done.5, bf16[544,384]{1,0:T(8,128)(2,1)} %constant_dynamic-update-slice_fusion.refs_0_.refs_2_, bf16[544,384]{1,0:T(8,128)(2,1)} %collective-permute-done.2.refs_3_, ...), custom_call_target="tpu_custom_call" | custom-call | flops 500000000 | bytes 2000000 | tf_op jit(solution)/shard_map/pallas_call | solution.py:72
  69.0 0.0 collective-permute-done.5.refs_2_
  69.0 0.0 copy-start.2
  69.0 0.0 collective-permute-done.6.refs_3_
  69.0 0.0 copy-start.3
  69.0 0.7 copy-done.2
  69.8 0.2 copy-done.3
  69.9 4.1 %shard_map.123.refs_9_ = f32[2,256,192]{2,1,0:T(8,128)} custom-call(bf16[128,384]{1,0:T(8,128)(2,1)} %get-tuple-element.34.refs_0_.refs_3_, bf16[128,384]{1,0:T(8,128)(2,1)} %copy-done.5, bf16[544,384]{1,0:T(8,128)(2,1)} %copy-done.2, bf16[544,384]{1,0:T(8,128)(2,1)} %copy-done.3, f32[2,256,192]{2,1,0:T(8,128)} %get-tuple-element.40.refs_4_, ...), custom_call_target="tpu_custom_call" | custom-call | flops 500000000 | bytes 2000000 | tf_op jit(solution)/shard_map/pallas_call | solution.py:72
  74.1 7.6 %all-to-all-done.1.refs_0_ = bf16[16,112,128]{2,1,0:T(8,128)(2,1)S(1)} async-done(((bf16[16,112,128]{2,1,0:T(8,128)(2,1)}), bf16[16,112,128]{2,1,0:T(8,128)(2,1)S(1)}, u32[]{:S(2)}, u32[]{:S(2)}) %all-to-all-start.1) | async-done | bytes 458784 | tf_op jit(solution)/shard_map/all_to_all | solution.py:450
  81.7 0.0 copy-start.1
  81.7 0.8 copy-done.1
  82.5 4.7 %shard_map.124 = bf16[4,64,384]{2,1,0:T(8,128)(2,1)} custom-call(bf16[16,112,128]{2,1,0:T(8,128)(2,1)} %copy-done.1, f32[3,192,384]{2,1,0:T(8,128)} %get-tuple-element.33.refs_1_, bf16[544,384]{1,0:T(8,128)(2,1)} %constant_dynamic-update-slice_fusion.refs_0_.refs_2_, bf16[128,384]{1,0:T(8,128)(2,1)} %get-tuple-element.34.refs_0_.refs_3_, ...), custom_call_target="tpu_custom_call" | custom-call | flops 600000000 | bytes 5000000 | tf_op jit(solution)/shard_map/pallas_call | solution.py:72
  87.2 17.0 %all_to_all.20.refs_0_ = bf16[4,64,384]{2,1,0:T(8,128)(2,1)} all-to-all(bf16[4,64,384]{2,1,0:T(8,128)(2,1)} %shard_map.124), channel_id=1, replica_groups=mesh['x'=4,'y'=4,'zh'=2,'zl'=4,'c'=2] {'c','zh'}, dimensions={0} | all-to-all | bytes 393216 | tf_op jit(solution)/shard_map/all_to_all | solution.py:469
  104.2 3.8 %shard_map.125 = bf16[128,3072]{1,0:T(8,128)(2,1)} custom-call(bf16[4,64,384]{2,1,0:T(8,128)(2,1)} %all_to_all.20.refs_0_, bf16[2,192,3072]{2,1,0:T(8,128)(2,1)} %bitcast.8, bf16[2,192,3072]{2,1,0:T(8,128)(2,1)} %bitcast.9, bf16[2,192,3072]{2,1,0:T(8,128)(2,1)} %bitcast.10, bf16[2,192,3072]{2,1,0:T(8,128)(2,1)} %bitcast.11), custom_call_target="tpu_custom_call" | custom-call | flops 600000000 | bytes 6000000 | tf_op jit(solution)/shard_map/pallas_call | solution.py:72
  107.9 24.4 %all_to_all.21.refs_0_ = bf16[4,32,3072]{2,1,0:T(8,128)(2,1)S(1)} all-to-all(bf16[4,32,3072]{2,1,0:T(8,128)(2,1)} %bitcast.12), channel_id=1, replica_groups=mesh['x'=4,'y'=4,'zh'=2,'zl'=4,'c'=2] {'zl'}, dimensions={0} | all-to-all | bytes 1572864 | tf_op jit(solution)/shard_map/all_to_all | solution.py:480
  132.3 0.8 shard_map.126
Async XLA Ops:
  0.0 21.4 %collective-permute-start.1 = (bf16[384,3072]{1,0:T(8,128)(2,1)}, bf16[384,3072]{1,0:T(8,128)(2,1)S(1)}, u32[]{:S(2)}, u32[]{:S(2)}) collective-permute-start(bf16[384,3072]{1,0:T(8,128)(2,1)} %param.23), channel_id=1, source_target_pairs={{0,1},{1,0},{2,3},{3,2},{4,5},{5,4},{6,7},{7,6},{8,9},{9,8},{10,11... | collective-permute-start | bytes 7077896 | tf_op jit(solution)/shard_map/ppermute | solution.py:408
  5.2 15.4 %collective-permute-start = (bf16[272,384]{1,0:T(8,128)(2,1)}, bf16[272,384]{1,0:T(8,128)(2,1)S(1)}, u32[]{:S(2)}, u32[]{:S(2)}) collective-permute-start(bf16[272,384]{1,0:T(8,128)(2,1)} %shard_map.119), channel_id=1, source_target_pairs={{0,8},{8,0},{1,9},{9,1},{2,10},{10,2},{3,11},{11,3},{4,12},{12,4},... | collective-permute-start | bytes 626696 | tf_op jit(solution)/shard_map/ppermute | solution.py:407
  21.4 17.3 %copy-start = (bf16[384,3072]{1,0:T(8,128)(2,1)}, bf16[384,3072]{1,0:T(8,128)(2,1)S(1)}, u32[]{:S(2)}) copy-start(bf16[384,3072]{1,0:T(8,128)(2,1)S(1)} %collective-permute-done.1) | copy-start | bytes 7077892
  21.4 17.3 %collective-permute-start.3 = (bf16[544,384]{1,0:T(8,128)(2,1)}, bf16[544,384]{1,0:T(8,128)(2,1)S(1)}, u32[]{:S(2)}, u32[]{:S(2)}) collective-permute-start(bf16[544,384]{1,0:T(8,128)(2,1)} %constant_dynamic-update-slice_fusion.refs_0_.refs_2_), channel_id=1, source_target_pairs={{0,16},{16,32},{32,48},{48,64},{64,80},{80,96},{96,112},{112,128},... | collective-permute-start | bytes 1253384 | tf_op jit(solution)/shard_map/ppermute | solution.py:389
  24.6 14.1 %collective-permute-start.2 = (bf16[544,384]{1,0:T(8,128)(2,1)}, bf16[544,384]{1,0:T(8,128)(2,1)}, u32[]{:S(2)}, u32[]{:S(2)}) collective-permute-start(bf16[544,384]{1,0:T(8,128)(2,1)} %constant_dynamic-update-slice_fusion.refs_0_.refs_2_), channel_id=1, source_target_pairs={{0,64},{64,128},{128,192},{1,65},{65,129},{129,193},{2,66},{66,130... | collective-permute-start | bytes 1253384 | tf_op jit(solution)/shard_map/ppermute | solution.py:422
  28.5 21.3 %copy-start.7 = (bf16[128,384]{1,0:T(8,128)(2,1)S(1)}, bf16[128,384]{1,0:T(8,128)(2,1)}, u32[]{:S(2)}) copy-start(bf16[128,384]{1,0:T(8,128)(2,1)} %get-tuple-element.31) | copy-start | bytes 294916
  28.5 24.7 %copy-start.4 = (bf16[544,384]{1,0:T(8,128)(2,1)S(1)}, bf16[544,384]{1,0:T(8,128)(2,1)}, u32[]{:S(2)}) copy-start(bf16[544,384]{1,0:T(8,128)(2,1)} %constant_dynamic-update-slice_fusion.refs_0_.refs_2_) | copy-start | bytes 1253380
  38.7 26.3 %copy-start.6 = (bf16[544,384]{1,0:T(8,128)(2,1)}, bf16[544,384]{1,0:T(8,128)(2,1)S(1)}, u32[]{:S(2)}) copy-start(bf16[544,384]{1,0:T(8,128)(2,1)S(1)} %collective-permute-done.3.refs_4_) | copy-start | bytes 1253380
  38.7 19.6 %all-to-all-start = ((bf16[16,112,128]{2,1,0:T(8,128)(2,1)}), bf16[16,112,128]{2,1,0:T(8,128)(2,1)S(1)}, u32[]{:S(2)}, u32[]{:S(2)}) async-start(bf16[16,112,128]{2,1,0:T(8,128)(2,1)} %get-tuple-element.28), calls=%async_computation | async-start | bytes 917504 | tf_op jit(solution)/shard_map/all_to_all | solution.py:438
  49.7 7.7 %collective-permute-start.4 = (bf16[128,384]{1,0:T(8,128)(2,1)S(1)}, bf16[128,384]{1,0:T(8,128)(2,1)S(1)}, u32[]{:S(2)}, u32[]{:S(2)}) collective-permute-start(bf16[128,384]{1,0:T(8,128)(2,1)S(1)} %copy-done.7), channel_id=1, source_target_pairs={{0,8},{8,0},{1,9},{9,1},{2,10},{10,2},{3,11},{11,3},{4,12},{12,4},... | collective-permute-start | bytes 294920 | tf_op jit(solution)/shard_map/ppermute | solution.py:436
  49.8 19.2 %collective-permute-start.5 = (bf16[544,384]{1,0:T(8,128)(2,1)S(1)}, bf16[544,384]{1,0:T(8,128)(2,1)S(1)}, u32[]{:S(2)}, u32[]{:S(2)}) collective-permute-start(bf16[544,384]{1,0:T(8,128)(2,1)S(1)} %collective-permute-done.3.refs_4_), channel_id=1, source_target_pairs={{0,16},{16,32},{32,48},{48,64},{64,80},{80,96},{96,112},{112,128},... | collective-permute-start | bytes 1253384 | tf_op jit(solution)/shard_map/ppermute | solution.py:389
  53.1 15.9 %collective-permute-start.6 = (bf16[544,384]{1,0:T(8,128)(2,1)S(1)}, bf16[544,384]{1,0:T(8,128)(2,1)S(1)}, u32[]{:S(2)}, u32[]{:S(2)}) collective-permute-start(bf16[544,384]{1,0:T(8,128)(2,1)S(1)} %copy-done.4), channel_id=1, source_target_pairs={{0,48},{16,64},{32,80},{48,96},{64,112},{80,128},{96,144},{112,160... | collective-permute-start | bytes 1253384 | tf_op jit(solution)/shard_map/ppermute | solution.py:389
  57.5 7.6 %copy-start.5 = (bf16[128,384]{1,0:T(8,128)(2,1)}, bf16[128,384]{1,0:T(8,128)(2,1)S(1)}, u32[]{:S(2)}) copy-start(bf16[128,384]{1,0:T(8,128)(2,1)S(1)} %collective-permute-done.4.refs_1_.refs_4_) | copy-start | bytes 294916
  59.5 22.2 %all-to-all-start.1 = ((bf16[16,112,128]{2,1,0:T(8,128)(2,1)}), bf16[16,112,128]{2,1,0:T(8,128)(2,1)S(1)}, u32[]{:S(2)}, u32[]{:S(2)}) async-start(bf16[16,112,128]{2,1,0:T(8,128)(2,1)} %shard_map.121), calls=%async_computation.1 | async-start | bytes 917504 | tf_op jit(solution)/shard_map/all_to_all | solution.py:450
  69.0 0.8 copy-start.2
  69.0 0.9 copy-start.3
  81.7 0.8 copy-start.1

commit v10 on v9

--- a/solution.py
+++ b/solution.py
@@ -434,9 +434,7 @@
     w2 = behind(later_w1, 1)
     w3 = behind(later_kv, 3)
     recv_q = lax.ppermute(send_q, "zh", [(0, 1), (1, 0)])
-    outgoing, shifted, w1 = lax.optimization_barrier((outgoing, shifted, w1))
     pieces = lax.all_to_all(outgoing, ("x", "y"), 0, 0, tiled=True)
-    pieces, recv_q = lax.optimization_barrier((pieces, recv_q))
     acc, stat = call(
         attend_first_body,
         [sds((2, BLK, HD), F32), sds((2, BLK, 128), F32)],
@@ -446,6 +444,7 @@
         600_000,
         scratch=[pltpu.VMEM((2, 5, BLK, BLK), F32)],
     )
+    pieces, acc = lax.optimization_barrier((pieces, acc))
     (sums,) = call(scan_body, [sds((PAIRS, CROWS, 128), BF16)], (pieces,), 500_000, 1_000_000, cap=SMALL)
     prefix = lax.all_to_all(sums, ("x", "y"), 0, 0, tiled=True)
     (att,) = call(

time: 134 us -> 129 us (0.963)
  starting transfers between devices: 39.8 us -> 35.4 us
  waiting for transfers between devices: 8.51 us -> 4.86 us
  blocking collectives: 41.3 us -> 43.9 us
    all_to_all x1, starting transfers between devices: 11 us -> 5.42 us  [local(): pieces = lax.all_to_all(outgoing, ('x', 'y'), 0, 0, tiled=True)]
    all_to_all x1, waiting for transfers between devices: 7.64 us -> 4.84 us  [local(): prefix = lax.all_to_all(sums, ('x', 'y'), 0, 0, tiled=True)]
    all_to_all x1, blocking collectives: 17 us -> 19.5 us  [local(): mixed = lax.all_to_all(mixed, ('c', 'zh'), 0, 0, tiled=True)]
  transfers between devices with their start and end apart: 9 -> 9, of which waited for: 2 -> 1; matrix products, arithmetic and copies ran while one was open for 1% -> 1% of each run, Pallas kernels for 24% -> 25%
where the time goes in v10:
time: 129 us; the launch traced here: 128 us
  blocking collectives  43.9 us (34%)
  Pallas kernels  40.8 us (32%)
  starting transfers between devices  35.4 us (27%)
  waiting for transfers between devices  4.86 us (4%)
  local copies, waits for them, and re-layouts  3.02 us (2%)
    pallas_call x9, Pallas kernels, call(): pl.pallas_call(kernel, out_shape=outs, in_specs=[any_spec] * n_in, out_sp...  40.8 us
    all_to_all x1, blocking collectives, local(): lax.all_to_all(partial.reshape(4, 32, WIDTH), 'zl', 0, 0, tiled=True)  24.4 us
    all_to_all x1, blocking collectives, local(): mixed = lax.all_to_all(mixed, ('c', 'zh'), 0, 0, tiled=True)  19.5 us
    ppermute x3, starting transfers between devices, behind(): lax.ppermute(pair_kv, ('x', 'y'), [(i, i + distance) for i in range(PAIRS...  11.4 us
    all_to_all x1, starting transfers between devices, local(): pieces = lax.all_to_all(outgoing, ('x', 'y'), 0, 0, tiled=True)  5.42 us
    ppermute x1, starting transfers between devices, local(): recv = lax.ppermute(send, 'zh', [(0, 1), (1, 0)])  5.26 us
    all_to_all x1, starting transfers between devices, local(): prefix = lax.all_to_all(sums, ('x', 'y'), 0, 0, tiled=True)  5.26 us
    all_to_all x1, waiting for transfers between devices, local(): prefix = lax.all_to_all(sums, ('x', 'y'), 0, 0, tiled=True)  4.84 us
  transfers between devices with their start and end apart: 9, of which 1 were waited for; matrix products, arithmetic and copies ran while one was open for 1% of the time, Pallas kernels for 25%

profile of v10, /device:TPU:1, one launch (start us, length us, event | category | flops | bytes accessed | tf_op | source)
XLA Modules:
  0.0 128.3 jit_solution(16265119613055535368)
XLA Ops:
  0.0 3.2 %collective-permute-start.1 = (bf16[384,3072]{1,0:T(8,128)(2,1)}, bf16[384,3072]{1,0:T(8,128)(2,1)S(1)}, u32[]{:S(2)}, u32[]{:S(2)}) collective-permute-start(bf16[384,3072]{1,0:T(8,128)(2,1)} %param.23), channel_id=1, source_target_pairs={{0,1},{1,0},{2,3},{3,2},{4,5},{5,4},{6,7},{7,6},{8,9},{9,8},{10,11... | collective-permute-start | bytes 7077896 | tf_op jit(solution)/shard_map/ppermute | solution.py:408
  3.2 2.0 %shard_map.119 = bf16[272,384]{1,0:T(8,128)(2,1)} custom-call(bf16[256,384]{1,0:T(8,128)(2,1)} %refs_0_.3, bf16[256,384]{1,0:T(8,128)(2,1)} %refs_1_.4, f32[2,256]{1,0:T(2,128)} %bitcast.16, f32[1,2]{1,0:T(1,128)} %refs_3_.3), custom_call_target="tpu_custom_call" | custom-call | bytes 1000000 | tf_op jit(solution)/shard_map/pallas_call | solution.py:72
  5.2 5.3 %collective-permute-start = (bf16[272,384]{1,0:T(8,128)(2,1)}, bf16[272,384]{1,0:T(8,128)(2,1)S(1)}, u32[]{:S(2)}, u32[]{:S(2)}) collective-permute-start(bf16[272,384]{1,0:T(8,128)(2,1)} %shard_map.119), channel_id=1, source_target_pairs={{0,8},{8,0},{1,9},{9,1},{2,10},{10,2},{3,11},{11,3},{4,12},{12,4},... | collective-permute-start | bytes 626696 | tf_op jit(solution)/shard_map/ppermute | solution.py:407
  10.5 10.1 %shard_map.118 = (f32[3,192,384]{2,1,0:T(8,128)}, bf16[544,384]{1,0:T(8,128)(2,1)}, bf16[128,384]{1,0:T(8,128)(2,1)}, bf16[128,384]{1,0:T(8,128)(2,1)}) custom-call(bf16[256,384]{1,0:T(8,128)(2,1)} %refs_0_.3, bf16[256,384]{1,0:T(8,128)(2,1)} %refs_1_.4, f32[2,256]{1,0:T(2,128)} %bitcast.17, f32[1,2]{1,0:T(1,128)} %refs_3_.3, f32[2,192,384]{2,1,0:T(8,128)} %refs_5_.3, ...), custom_call_target="tpu_custom_call" | custom-call | flops 6000000000 | bytes 3000000 | tf_op jit(solution)/shard_map/pallas_call | solution.py:72
  20.6 0.0 collective-permute-done
  20.6 0.7 constant_dynamic-update-slice_fusion.refs_0_.refs_2_
  21.3 0.0 collective-permute-done.1
  21.3 0.0 copy-start
  21.3 3.9 %collective-permute-start.4 = (bf16[544,384]{1,0:T(8,128)(2,1)}, bf16[544,384]{1,0:T(8,128)(2,1)}, u32[]{:S(2)}, u32[]{:S(2)}) collective-permute-start(bf16[544,384]{1,0:T(8,128)(2,1)} %constant_dynamic-update-slice_fusion.refs_0_.refs_2_), channel_id=1, source_target_pairs={{0,64},{64,128},{128,192},{1,65},{65,129},{129,193},{2,66},{66,130... | collective-permute-start | bytes 1253384 | tf_op jit(solution)/shard_map/ppermute | solution.py:422
  25.2 3.4 %collective-permute-start.2 = (bf16[544,384]{1,0:T(8,128)(2,1)}, bf16[544,384]{1,0:T(8,128)(2,1)S(1)}, u32[]{:S(2)}, u32[]{:S(2)}) collective-permute-start(bf16[544,384]{1,0:T(8,128)(2,1)} %constant_dynamic-update-slice_fusion.refs_0_.refs_2_), channel_id=1, source_target_pairs={{0,16},{16,32},{32,48},{48,64},{64,80},{80,96},{96,112},{112,128},... | collective-permute-start | bytes 1253384 | tf_op jit(solution)/shard_map/ppermute | solution.py:389
  28.6 0.0 copy-start.7
  28.6 0.0 copy-start.4
  28.6 10.2 %shard_map.120 = (f32[3,192,384]{2,1,0:T(8,128)}, bf16[16,112,128]{2,1,0:T(8,128)(2,1)}) custom-call(bf16[544,384]{1,0:T(8,128)(2,1)} %constant_dynamic-update-slice_fusion.refs_0_.refs_2_, f32[2,192,384]{2,1,0:T(8,128)} %refs_5_.3, f32[2,192,384]{2,1,0:T(8,128)} %refs_6_.1, f32[2,192,384]{2,1,0:T(8,128)} %bitcast.14, f32[1,2]{1,0:T(1,128)} %bitcast.21, ...), custom_call_target="tpu_custom_call" | custom-call | flops 6000000000 | bytes 4000000 | tf_op jit(solution)/shard_map/pallas_call | solution.py:72
  38.8 0.0 copy-done
  38.8 5.4 %all-to-all-start = ((bf16[16,112,128]{2,1,0:T(8,128)(2,1)}), bf16[16,112,128]{2,1,0:T(8,128)(2,1)S(1)}, u32[]{:S(2)}, u32[]{:S(2)}) async-start(bf16[16,112,128]{2,1,0:T(8,128)(2,1)} %get-tuple-element.24), calls=%async_computation | async-start | bytes 917504 | tf_op jit(solution)/shard_map/all_to_all | solution.py:437
  44.3 0.0 collective-permute-done.2.refs_4_
  44.3 0.0 copy-start.6
  44.3 0.0 copy-done.7
  44.3 0.9 collective-permute-start.3
  45.2 3.3 %collective-permute-start.5 = (bf16[544,384]{1,0:T(8,128)(2,1)S(1)}, bf16[544,384]{1,0:T(8,128)(2,1)S(1)}, u32[]{:S(2)}, u32[]{:S(2)}) collective-permute-start(bf16[544,384]{1,0:T(8,128)(2,1)S(1)} %collective-permute-done.2.refs_4_), channel_id=1, source_target_pairs={{0,16},{16,32},{32,48},{48,64},{64,80},{80,96},{96,112},{112,128},... | collective-permute-start | bytes 1253384 | tf_op jit(solution)/shard_map/ppermute | solution.py:389
  48.5 0.0 copy-done.4
  48.5 4.7 %collective-permute-start.6 = (bf16[544,384]{1,0:T(8,128)(2,1)S(1)}, bf16[544,384]{1,0:T(8,128)(2,1)S(1)}, u32[]{:S(2)}, u32[]{:S(2)}) collective-permute-start(bf16[544,384]{1,0:T(8,128)(2,1)S(1)} %copy-done.4), channel_id=1, source_target_pairs={{0,48},{16,64},{32,80},{48,96},{64,112},{80,128},{96,144},{112,160... | collective-permute-start | bytes 1253384 | tf_op jit(solution)/shard_map/ppermute | solution.py:389
  53.2 0.0 collective-permute-done.4.refs_3_
  53.3 0.0 collective-permute-done.3.refs_1_.refs_4_
  53.3 0.0 copy-start.5
  53.3 0.0 copy-done.6
  53.3 0.6 copy-done.5
  53.9 3.9 %shard_map.121 = (f32[2,256,192]{2,1,0:T(8,128)}, f32[2,256,128]{2,1,0:T(8,128)}) custom-call(bf16[128,384]{1,0:T(8,128)(2,1)} %get-tuple-element.25.refs_0_.refs_3_, bf16[128,384]{1,0:T(8,128)(2,1)} %copy-done.5, bf16[544,384]{1,0:T(8,128)(2,1)} %constant_dynamic-update-slice_fusion.refs_0_.refs_2_, bf16[544,384]{1,0:T(8,128)(2,1)} %collective-permute-done.4.refs_3_, ...), custom_call_target="tpu_custom_call" | custom-call | flops 500000000 | bytes 2000000 | tf_op jit(solution)/shard_map/pallas_call | solution.py:72
  57.8 0.0 all-to-all-done.refs_0_
  57.8 1.2 shard_map.122
  59.0 5.3 %all-to-all-start.1 = ((bf16[16,112,128]{2,1,0:T(8,128)(2,1)}), bf16[16,112,128]{2,1,0:T(8,128)(2,1)S(1)}, u32[]{:S(2)}, u32[]{:S(2)}) async-start(bf16[16,112,128]{2,1,0:T(8,128)(2,1)} %shard_map.122), calls=%async_computation.1 | async-start | bytes 917504 | tf_op jit(solution)/shard_map/all_to_all | solution.py:449
  64.3 0.0 collective-permute-done.5.refs_2_
  64.3 0.0 copy-start.2
  64.3 0.0 collective-permute-done.6.refs_3_
  64.3 0.0 copy-start.3
  64.3 0.7 copy-done.2
  65.0 0.1 copy-done.3
  65.2 4.1 %shard_map.123.refs_9_ = f32[2,256,192]{2,1,0:T(8,128)} custom-call(bf16[128,384]{1,0:T(8,128)(2,1)} %get-tuple-element.25.refs_0_.refs_3_, bf16[128,384]{1,0:T(8,128)(2,1)} %copy-done.5, bf16[544,384]{1,0:T(8,128)(2,1)} %copy-done.2, bf16[544,384]{1,0:T(8,128)(2,1)} %copy-done.3, f32[2,256,192]{2,1,0:T(8,128)} %get-tuple-element.34.refs_4_, ...), custom_call_target="tpu_custom_call" | custom-call | flops 500000000 | bytes 2000000 | tf_op jit(solution)/shard_map/pallas_call | solution.py:72
  69.3 4.8 %all-to-all-done.1.refs_0_ = bf16[16,112,128]{2,1,0:T(8,128)(2,1)S(1)} async-done(((bf16[16,112,128]{2,1,0:T(8,128)(2,1)}), bf16[16,112,128]{2,1,0:T(8,128)(2,1)S(1)}, u32[]{:S(2)}, u32[]{:S(2)}) %all-to-all-start.1) | async-done | bytes 458784 | tf_op jit(solution)/shard_map/all_to_all | solution.py:449
  74.2 0.0 copy-start.1
  74.2 0.8 copy-done.1
  75.0 4.7 %shard_map.124 = bf16[4,64,384]{2,1,0:T(8,128)(2,1)} custom-call(bf16[16,112,128]{2,1,0:T(8,128)(2,1)} %copy-done.1, f32[3,192,384]{2,1,0:T(8,128)} %get-tuple-element.31.refs_1_, bf16[544,384]{1,0:T(8,128)(2,1)} %constant_dynamic-update-slice_fusion.refs_0_.refs_2_, bf16[128,384]{1,0:T(8,128)(2,1)} %get-tuple-element.25.refs_0_.refs_3_, ...), custom_call_target="tpu_custom_call" | custom-call | flops 600000000 | bytes 5000000 | tf_op jit(solution)/shard_map/pallas_call | solution.py:72
  79.7 19.5 %all_to_all.20.refs_0_ = bf16[4,64,384]{2,1,0:T(8,128)(2,1)} all-to-all(bf16[4,64,384]{2,1,0:T(8,128)(2,1)} %shard_map.124), channel_id=1, replica_groups=mesh['x'=4,'y'=4,'zh'=2,'zl'=4,'c'=2] {'c','zh'}, dimensions={0} | all-to-all | bytes 393216 | tf_op jit(solution)/shard_map/all_to_all | solution.py:468
  99.2 3.8 %shard_map.125 = bf16[128,3072]{1,0:T(8,128)(2,1)} custom-call(bf16[4,64,384]{2,1,0:T(8,128)(2,1)} %all_to_all.20.refs_0_, bf16[2,192,3072]{2,1,0:T(8,128)(2,1)} %bitcast.8, bf16[2,192,3072]{2,1,0:T(8,128)(2,1)} %bitcast.9, bf16[2,192,3072]{2,1,0:T(8,128)(2,1)} %bitcast.10, bf16[2,192,3072]{2,1,0:T(8,128)(2,1)} %bitcast.11), custom_call_target="tpu_custom_call" | custom-call | flops 600000000 | bytes 6000000 | tf_op jit(solution)/shard_map/pallas_call | solution.py:72
  102.9 24.4 %all_to_all.21.refs_0_ = bf16[4,32,3072]{2,1,0:T(8,128)(2,1)S(1)} all-to-all(bf16[4,32,3072]{2,1,0:T(8,128)(2,1)} %bitcast.12), channel_id=1, replica_groups=mesh['x'=4,'y'=4,'zh'=2,'zl'=4,'c'=2] {'zl'}, dimensions={0} | all-to-all | bytes 1572864 | tf_op jit(solution)/shard_map/all_to_all | solution.py:479
  127.3 0.8 shard_map.126
Async XLA Ops:
  0.0 21.3 %collective-permute-start.1 = (bf16[384,3072]{1,0:T(8,128)(2,1)}, bf16[384,3072]{1,0:T(8,128)(2,1)S(1)}, u32[]{:S(2)}, u32[]{:S(2)}) collective-permute-start(bf16[384,3072]{1,0:T(8,128)(2,1)} %param.23), channel_id=1, source_target_pairs={{0,1},{1,0},{2,3},{3,2},{4,5},{5,4},{6,7},{7,6},{8,9},{9,8},{10,11... | collective-permute-start | bytes 7077896 | tf_op jit(solution)/shard_map/ppermute | solution.py:408
  5.2 15.3 %collective-permute-start = (bf16[272,384]{1,0:T(8,128)(2,1)}, bf16[272,384]{1,0:T(8,128)(2,1)S(1)}, u32[]{:S(2)}, u32[]{:S(2)}) collective-permute-start(bf16[272,384]{1,0:T(8,128)(2,1)} %shard_map.119), channel_id=1, source_target_pairs={{0,8},{8,0},{1,9},{9,1},{2,10},{10,2},{3,11},{11,3},{4,12},{12,4},... | collective-permute-start | bytes 626696 | tf_op jit(solution)/shard_map/ppermute | solution.py:407
  21.3 17.5 %copy-start = (bf16[384,3072]{1,0:T(8,128)(2,1)}, bf16[384,3072]{1,0:T(8,128)(2,1)S(1)}, u32[]{:S(2)}) copy-start(bf16[384,3072]{1,0:T(8,128)(2,1)S(1)} %collective-permute-done.1) | copy-start | bytes 7077892
  21.3 31.9 %collective-permute-start.4 = (bf16[544,384]{1,0:T(8,128)(2,1)}, bf16[544,384]{1,0:T(8,128)(2,1)}, u32[]{:S(2)}, u32[]{:S(2)}) collective-permute-start(bf16[544,384]{1,0:T(8,128)(2,1)} %constant_dynamic-update-slice_fusion.refs_0_.refs_2_), channel_id=1, source_target_pairs={{0,64},{64,128},{128,192},{1,65},{65,129},{129,193},{2,66},{66,130... | collective-permute-start | bytes 1253384 | tf_op jit(solution)/shard_map/ppermute | solution.py:422
  25.2 19.1 %collective-permute-start.2 = (bf16[544,384]{1,0:T(8,128)(2,1)}, bf16[544,384]{1,0:T(8,128)(2,1)S(1)}, u32[]{:S(2)}, u32[]{:S(2)}) collective-permute-start(bf16[544,384]{1,0:T(8,128)(2,1)} %constant_dynamic-update-slice_fusion.refs_0_.refs_2_), channel_id=1, source_target_pairs={{0,16},{16,32},{32,48},{48,64},{64,80},{80,96},{96,112},{112,128},... | collective-permute-start | bytes 1253384 | tf_op jit(solution)/shard_map/ppermute | solution.py:389
  28.6 15.7 %copy-start.7 = (bf16[128,384]{1,0:T(8,128)(2,1)S(1)}, bf16[128,384]{1,0:T(8,128)(2,1)}, u32[]{:S(2)}) copy-start(bf16[128,384]{1,0:T(8,128)(2,1)} %get-tuple-element.28) | copy-start | bytes 294916
  28.6 19.9 %copy-start.4 = (bf16[544,384]{1,0:T(8,128)(2,1)S(1)}, bf16[544,384]{1,0:T(8,128)(2,1)}, u32[]{:S(2)}) copy-start(bf16[544,384]{1,0:T(8,128)(2,1)} %constant_dynamic-update-slice_fusion.refs_0_.refs_2_) | copy-start | bytes 1253380
  38.8 19.0 %all-to-all-start = ((bf16[16,112,128]{2,1,0:T(8,128)(2,1)}), bf16[16,112,128]{2,1,0:T(8,128)(2,1)S(1)}, u32[]{:S(2)}, u32[]{:S(2)}) async-start(bf16[16,112,128]{2,1,0:T(8,128)(2,1)} %get-tuple-element.24), calls=%async_computation | async-start | bytes 917504 | tf_op jit(solution)/shard_map/all_to_all | solution.py:437
  44.3 9.0 %copy-start.6 = (bf16[544,384]{1,0:T(8,128)(2,1)}, bf16[544,384]{1,0:T(8,128)(2,1)S(1)}, u32[]{:S(2)}) copy-start(bf16[544,384]{1,0:T(8,128)(2,1)S(1)} %collective-permute-done.2.refs_4_) | copy-start | bytes 1253380
  44.3 9.0 %collective-permute-start.3 = (bf16[128,384]{1,0:T(8,128)(2,1)S(1)}, bf16[128,384]{1,0:T(8,128)(2,1)S(1)}, u32[]{:S(2)}, u32[]{:S(2)}) collective-permute-start(bf16[128,384]{1,0:T(8,128)(2,1)S(1)} %copy-done.7), channel_id=1, source_target_pairs={{0,8},{8,0},{1,9},{9,1},{2,10},{10,2},{3,11},{11,3},{4,12},{12,4},... | collective-permute-start | bytes 294920 | tf_op jit(solution)/shard_map/ppermute | solution.py:436
  45.2 19.1 %collective-permute-start.5 = (bf16[544,384]{1,0:T(8,128)(2,1)S(1)}, bf16[544,384]{1,0:T(8,128)(2,1)S(1)}, u32[]{:S(2)}, u32[]{:S(2)}) collective-permute-start(bf16[544,384]{1,0:T(8,128)(2,1)S(1)} %collective-permute-done.2.refs_4_), channel_id=1, source_target_pairs={{0,16},{16,32},{32,48},{48,64},{64,80},{80,96},{96,112},{112,128},... | collective-permute-start | bytes 1253384 | tf_op jit(solution)/shard_map/ppermute | solution.py:389
  48.5 15.8 %collective-permute-start.6 = (bf16[544,384]{1,0:T(8,128)(2,1)S(1)}, bf16[544,384]{1,0:T(8,128)(2,1)S(1)}, u32[]{:S(2)}, u32[]{:S(2)}) collective-permute-start(bf16[544,384]{1,0:T(8,128)(2,1)S(1)} %copy-done.4), channel_id=1, source_target_pairs={{0,48},{16,64},{32,80},{48,96},{64,112},{80,128},{96,144},{112,160... | collective-permute-start | bytes 1253384 | tf_op jit(solution)/shard_map/ppermute | solution.py:389
  53.3 0.6 copy-start.5
  59.0 15.1 %all-to-all-start.1 = ((bf16[16,112,128]{2,1,0:T(8,128)(2,1)}), bf16[16,112,128]{2,1,0:T(8,128)(2,1)S(1)}, u32[]{:S(2)}, u32[]{:S(2)}) async-start(bf16[16,112,128]{2,1,0:T(8,128)(2,1)} %shard_map.122), calls=%async_computation.1 | async-start | bytes 917504 | tf_op jit(solution)/shard_map/all_to_all | solution.py:449
  64.3 0.8 copy-start.2
  64.3 0.9 copy-start.3
  74.2 0.8 copy-start.1

commit v11 on v10

--- a/solution.py
+++ b/solution.py
@@ -430,10 +430,11 @@
         scratch=[flat],
         mine=(1, 2, 3),
     )
-    even, later_kv, later_w1, send_q = lax.optimization_barrier((even, pair_kv, w1, send_q))
+    even, later_kv, later_w1 = lax.optimization_barrier((even, pair_kv, w1))
     w2 = behind(later_w1, 1)
     w3 = behind(later_kv, 3)
     recv_q = lax.ppermute(send_q, "zh", [(0, 1), (1, 0)])
+    outgoing, recv_q = lax.optimization_barrier((outgoing, recv_q))
     pieces = lax.all_to_all(outgoing, ("x", "y"), 0, 0, tiled=True)
     acc, stat = call(
         attend_first_body,

time: 129 us -> 130 us (level)
  waiting for transfers between devices: 4.86 us -> 9.76 us
  blocking collectives: 43.9 us -> 42 us
  starting transfers between devices: 35.4 us -> 33.9 us
    all_to_all x1, waiting for transfers between devices: 4.84 us -> 9.74 us  [local(): prefix = lax.all_to_all(sums, ('x', 'y'), 0, 0, tiled=True)]
  transfers between devices with their start and end apart: 9 -> 9, of which waited for: 1 -> 1; matrix products, arithmetic and copies ran while one was open for 1% -> 1% of each run, Pallas kernels for 25% -> 24%
where the time goes in v11:
time: 130 us; the launch traced here: 129 us
  blocking collectives  42 us (32%)
  Pallas kernels  40.8 us (31%)
  starting transfers between devices  33.9 us (26%)
  waiting for transfers between devices  9.76 us (8%)
  local copies, waits for them, and re-layouts  2.42 us (2%)
    pallas_call x9, Pallas kernels, call(): pl.pallas_call(kernel, out_shape=outs, in_specs=[any_spec] * n_in, out_sp...  40.8 us
    all_to_all x1, blocking collectives, local(): lax.all_to_all(partial.reshape(4, 32, WIDTH), 'zl', 0, 0, tiled=True)  23.7 us
    all_to_all x1, blocking collectives, local(): mixed = lax.all_to_all(mixed, ('c', 'zh'), 0, 0, tiled=True)  18.3 us
    ppermute x3, starting transfers between devices, behind(): lax.ppermute(pair_kv, ('x', 'y'), [(i, i + distance) for i in range(PAIRS...  10.6 us
    all_to_all x1, waiting for transfers between devices, local(): prefix = lax.all_to_all(sums, ('x', 'y'), 0, 0, tiled=True)  9.74 us
    all_to_all x1, starting transfers between devices, local(): pieces = lax.all_to_all(outgoing, ('x', 'y'), 0, 0, tiled=True)  5.6 us
    ppermute x1, starting transfers between devices, local(): recv = lax.ppermute(send, 'zh', [(0, 1), (1, 0)])  5.26 us
    all_to_all x1, starting transfers between devices, local(): prefix = lax.all_to_all(sums, ('x', 'y'), 0, 0, tiled=True)  4.97 us
  transfers between devices with their start and end apart: 9, of which 1 were waited for; matrix products, arithmetic and copies ran while one was open for 1% of the time, Pallas kernels for 24%

profile of v11, /device:TPU:1, one launch (start us, length us, event | category | flops | bytes accessed | tf_op | source)
XLA Modules:
  0.0 129.3 jit_solution(11761841899244853598)
XLA Ops:
  0.0 3.2 %collective-permute-start.1 = (bf16[384,3072]{1,0:T(8,128)(2,1)}, bf16[384,3072]{1,0:T(8,128)(2,1)S(1)}, u32[]{:S(2)}, u32[]{:S(2)}) collective-permute-start(bf16[384,3072]{1,0:T(8,128)(2,1)} %param.23), channel_id=1, source_target_pairs={{0,1},{1,0},{2,3},{3,2},{4,5},{5,4},{6,7},{7,6},{8,9},{9,8},{10,11... | collective-permute-start | bytes 7077896 | tf_op jit(solution)/shard_map/ppermute | solution.py:408
  3.2 2.0 %shard_map.119 = bf16[272,384]{1,0:T(8,128)(2,1)} custom-call(bf16[256,384]{1,0:T(8,128)(2,1)} %refs_0_.3, bf16[256,384]{1,0:T(8,128)(2,1)} %refs_1_.4, f32[2,256]{1,0:T(2,128)} %bitcast.16, f32[1,2]{1,0:T(1,128)} %refs_3_.3), custom_call_target="tpu_custom_call" | custom-call | bytes 1000000 | tf_op jit(solution)/shard_map/pallas_call | solution.py:72
  5.2 5.3 %collective-permute-start = (bf16[272,384]{1,0:T(8,128)(2,1)}, bf16[272,384]{1,0:T(8,128)(2,1)S(1)}, u32[]{:S(2)}, u32[]{:S(2)}) collective-permute-start(bf16[272,384]{1,0:T(8,128)(2,1)} %shard_map.119), channel_id=1, source_target_pairs={{0,8},{8,0},{1,9},{9,1},{2,10},{10,2},{3,11},{11,3},{4,12},{12,4},... | collective-permute-start | bytes 626696 | tf_op jit(solution)/shard_map/ppermute | solution.py:407
  10.5 10.1 %shard_map.118 = (f32[3,192,384]{2,1,0:T(8,128)}, bf16[544,384]{1,0:T(8,128)(2,1)}, bf16[128,384]{1,0:T(8,128)(2,1)}, bf16[128,384]{1,0:T(8,128)(2,1)}) custom-call(bf16[256,384]{1,0:T(8,128)(2,1)} %refs_0_.3, bf16[256,384]{1,0:T(8,128)(2,1)} %refs_1_.4, f32[2,256]{1,0:T(2,128)} %bitcast.17, f32[1,2]{1,0:T(1,128)} %refs_3_.3, f32[2,192,384]{2,1,0:T(8,128)} %refs_5_.3, ...), custom_call_target="tpu_custom_call" | custom-call | flops 6000000000 | bytes 3000000 | tf_op jit(solution)/shard_map/pallas_call | solution.py:72
  20.6 0.3 collective-permute-start.2
  20.9 0.0 collective-permute-done
  20.9 0.7 constant_dynamic-update-slice_fusion.refs_0_.refs_2_
  21.6 0.0 collective-permute-done.1
  21.6 0.0 copy-start
  21.6 3.0 %collective-permute-start.4 = (bf16[544,384]{1,0:T(8,128)(2,1)}, bf16[544,384]{1,0:T(8,128)(2,1)S(1)}, u32[]{:S(2)}, u32[]{:S(2)}) collective-permute-start(bf16[544,384]{1,0:T(8,128)(2,1)} %constant_dynamic-update-slice_fusion.refs_0_.refs_2_), channel_id=1, source_target_pairs={{0,16},{16,32},{32,48},{48,64},{64,80},{80,96},{96,112},{112,128},... | collective-permute-start | bytes 1253384 | tf_op jit(solution)/shard_map/ppermute | solution.py:389
  24.6 3.9 %collective-permute-start.3 = (bf16[544,384]{1,0:T(8,128)(2,1)}, bf16[544,384]{1,0:T(8,128)(2,1)}, u32[]{:S(2)}, u32[]{:S(2)}) collective-permute-start(bf16[544,384]{1,0:T(8,128)(2,1)} %constant_dynamic-update-slice_fusion.refs_0_.refs_2_), channel_id=1, source_target_pairs={{0,64},{64,128},{128,192},{1,65},{65,129},{129,193},{2,66},{66,130... | collective-permute-start | bytes 1253384 | tf_op jit(solution)/shard_map/ppermute | solution.py:422
  28.5 0.0 copy-start.4
  28.5 10.2 %shard_map.120 = (f32[3,192,384]{2,1,0:T(8,128)}, bf16[16,112,128]{2,1,0:T(8,128)(2,1)}) custom-call(bf16[544,384]{1,0:T(8,128)(2,1)} %constant_dynamic-update-slice_fusion.refs_0_.refs_2_, f32[2,192,384]{2,1,0:T(8,128)} %refs_5_.3, f32[2,192,384]{2,1,0:T(8,128)} %refs_6_.1, f32[2,192,384]{2,1,0:T(8,128)} %bitcast.14, f32[1,2]{1,0:T(1,128)} %bitcast.21, ...), custom_call_target="tpu_custom_call" | custom-call | flops 6000000000 | bytes 4000000 | tf_op jit(solution)/shard_map/pallas_call | solution.py:72
  38.7 0.0 copy-done
  38.7 0.0 collective-permute-done.2.refs_1_.refs_4_
  38.8 0.0 copy-start.5
  38.8 5.6 %all-to-all-start = ((bf16[16,112,128]{2,1,0:T(8,128)(2,1)}), bf16[16,112,128]{2,1,0:T(8,128)(2,1)S(1)}, u32[]{:S(2)}, u32[]{:S(2)}) async-start(bf16[16,112,128]{2,1,0:T(8,128)(2,1)} %get-tuple-element.27), calls=%async_computation | async-start | bytes 917504 | tf_op jit(solution)/shard_map/all_to_all | solution.py:438
  44.4 0.0 collective-permute-done.4.refs_4_
  44.4 0.0 copy-start.6
  44.4 3.3 %collective-permute-start.5 = (bf16[544,384]{1,0:T(8,128)(2,1)S(1)}, bf16[544,384]{1,0:T(8,128)(2,1)S(1)}, u32[]{:S(2)}, u32[]{:S(2)}) collective-permute-start(bf16[544,384]{1,0:T(8,128)(2,1)S(1)} %collective-permute-done.4.refs_4_), channel_id=1, source_target_pairs={{0,16},{16,32},{32,48},{48,64},{64,80},{80,96},{96,112},{112,128},... | collective-permute-start | bytes 1253384 | tf_op jit(solution)/shard_map/ppermute | solution.py:389
  47.7 0.0 copy-done.4
  47.7 4.3 %collective-permute-start.6 = (bf16[544,384]{1,0:T(8,128)(2,1)S(1)}, bf16[544,384]{1,0:T(8,128)(2,1)S(1)}, u32[]{:S(2)}, u32[]{:S(2)}) collective-permute-start(bf16[544,384]{1,0:T(8,128)(2,1)S(1)} %copy-done.4), channel_id=1, source_target_pairs={{0,48},{16,64},{32,80},{48,96},{64,112},{80,128},{96,144},{112,160... | collective-permute-start | bytes 1253384 | tf_op jit(solution)/shard_map/ppermute | solution.py:389
  52.0 0.0 collective-permute-done.3.refs_3_
  52.0 0.0 copy-done.5
  52.0 0.0 copy-done.6
  52.0 3.9 %shard_map.121 = (f32[2,256,192]{2,1,0:T(8,128)}, f32[2,256,128]{2,1,0:T(8,128)}) custom-call(bf16[128,384]{1,0:T(8,128)(2,1)} %get-tuple-element.28.refs_0_.refs_3_, bf16[128,384]{1,0:T(8,128)(2,1)} %copy-done.5, bf16[544,384]{1,0:T(8,128)(2,1)} %constant_dynamic-update-slice_fusion.refs_0_.refs_2_, bf16[544,384]{1,0:T(8,128)(2,1)} %collective-permute-done.3.refs_3_, ...), custom_call_target="tpu_custom_call" | custom-call | flops 500000000 | bytes 2000000 | tf_op jit(solution)/shard_map/pallas_call | solution.py:72
  56.0 0.0 all-to-all-done.refs_0_
  56.0 1.2 shard_map.122
  57.2 5.0 %all-to-all-start.1 = ((bf16[16,112,128]{2,1,0:T(8,128)(2,1)}), bf16[16,112,128]{2,1,0:T(8,128)(2,1)S(1)}, u32[]{:S(2)}, u32[]{:S(2)}) async-start(bf16[16,112,128]{2,1,0:T(8,128)(2,1)} %shard_map.122), calls=%async_computation.1 | async-start | bytes 917504 | tf_op jit(solution)/shard_map/all_to_all | solution.py:450
  62.1 0.0 collective-permute-done.5.refs_2_
  62.1 0.0 copy-start.2
  62.2 0.0 collective-permute-done.6.refs_3_
  62.2 0.0 copy-start.3
  62.2 0.7 copy-done.2
  62.9 0.2 copy-done.3
  63.1 4.1 %shard_map.123.refs_9_ = f32[2,256,192]{2,1,0:T(8,128)} custom-call(bf16[128,384]{1,0:T(8,128)(2,1)} %get-tuple-element.28.refs_0_.refs_3_, bf16[128,384]{1,0:T(8,128)(2,1)} %copy-done.5, bf16[544,384]{1,0:T(8,128)(2,1)} %copy-done.2, bf16[544,384]{1,0:T(8,128)(2,1)} %copy-done.3, f32[2,256,192]{2,1,0:T(8,128)} %get-tuple-element.36.refs_4_, ...), custom_call_target="tpu_custom_call" | custom-call | flops 500000000 | bytes 2000000 | tf_op jit(solution)/shard_map/pallas_call | solution.py:72
  67.2 9.7 %all-to-all-done.1.refs_0_ = bf16[16,112,128]{2,1,0:T(8,128)(2,1)S(1)} async-done(((bf16[16,112,128]{2,1,0:T(8,128)(2,1)}), bf16[16,112,128]{2,1,0:T(8,128)(2,1)S(1)}, u32[]{:S(2)}, u32[]{:S(2)}) %all-to-all-start.1) | async-done | bytes 458784 | tf_op jit(solution)/shard_map/all_to_all | solution.py:450
  76.9 0.0 copy-start.1
  76.9 0.8 copy-done.1
  77.7 4.7 %shard_map.124 = bf16[4,64,384]{2,1,0:T(8,128)(2,1)} custom-call(bf16[16,112,128]{2,1,0:T(8,128)(2,1)} %copy-done.1, f32[3,192,384]{2,1,0:T(8,128)} %get-tuple-element.33.refs_1_, bf16[544,384]{1,0:T(8,128)(2,1)} %constant_dynamic-update-slice_fusion.refs_0_.refs_2_, bf16[128,384]{1,0:T(8,128)(2,1)} %get-tuple-element.28.refs_0_.refs_3_, ...), custom_call_target="tpu_custom_call" | custom-call | flops 600000000 | bytes 5000000 | tf_op jit(solution)/shard_map/pallas_call | solution.py:72
  82.5 18.3 %all_to_all.20.refs_0_ = bf16[4,64,384]{2,1,0:T(8,128)(2,1)} all-to-all(bf16[4,64,384]{2,1,0:T(8,128)(2,1)} %shard_map.124), channel_id=1, replica_groups=mesh['x'=4,'y'=4,'zh'=2,'zl'=4,'c'=2] {'c','zh'}, dimensions={0} | all-to-all | bytes 393216 | tf_op jit(solution)/shard_map/all_to_all | solution.py:469
  100.7 3.8 %shard_map.125 = bf16[128,3072]{1,0:T(8,128)(2,1)} custom-call(bf16[4,64,384]{2,1,0:T(8,128)(2,1)} %all_to_all.20.refs_0_, bf16[2,192,3072]{2,1,0:T(8,128)(2,1)} %bitcast.8, bf16[2,192,3072]{2,1,0:T(8,128)(2,1)} %bitcast.9, bf16[2,192,3072]{2,1,0:T(8,128)(2,1)} %bitcast.10, bf16[2,192,3072]{2,1,0:T(8,128)(2,1)} %bitcast.11), custom_call_target="tpu_custom_call" | custom-call | flops 600000000 | bytes 6000000 | tf_op jit(solution)/shard_map/pallas_call | solution.py:72
  104.5 23.7 %all_to_all.21.refs_0_ = bf16[4,32,3072]{2,1,0:T(8,128)(2,1)S(1)} all-to-all(bf16[4,32,3072]{2,1,0:T(8,128)(2,1)} %bitcast.12), channel_id=1, replica_groups=mesh['x'=4,'y'=4,'zh'=2,'zl'=4,'c'=2] {'zl'}, dimensions={0} | all-to-all | bytes 1572864 | tf_op jit(solution)/shard_map/all_to_all | solution.py:480
  128.3 0.8 shard_map.126
Async XLA Ops:
  0.0 21.6 %collective-permute-start.1 = (bf16[384,3072]{1,0:T(8,128)(2,1)}, bf16[384,3072]{1,0:T(8,128)(2,1)S(1)}, u32[]{:S(2)}, u32[]{:S(2)}) collective-permute-start(bf16[384,3072]{1,0:T(8,128)(2,1)} %param.23), channel_id=1, source_target_pairs={{0,1},{1,0},{2,3},{3,2},{4,5},{5,4},{6,7},{7,6},{8,9},{9,8},{10,11... | collective-permute-start | bytes 7077896 | tf_op jit(solution)/shard_map/ppermute | solution.py:408
  5.2 15.6 %collective-permute-start = (bf16[272,384]{1,0:T(8,128)(2,1)}, bf16[272,384]{1,0:T(8,128)(2,1)S(1)}, u32[]{:S(2)}, u32[]{:S(2)}) collective-permute-start(bf16[272,384]{1,0:T(8,128)(2,1)} %shard_map.119), channel_id=1, source_target_pairs={{0,8},{8,0},{1,9},{9,1},{2,10},{10,2},{3,11},{11,3},{4,12},{12,4},... | collective-permute-start | bytes 626696 | tf_op jit(solution)/shard_map/ppermute | solution.py:407
  20.6 18.2 %collective-permute-start.2 = (bf16[128,384]{1,0:T(8,128)(2,1)}, bf16[128,384]{1,0:T(8,128)(2,1)S(1)}, u32[]{:S(2)}, u32[]{:S(2)}) collective-permute-start(bf16[128,384]{1,0:T(8,128)(2,1)} %get-tuple-element.26), channel_id=1, source_target_pairs={{0,8},{8,0},{1,9},{9,1},{2,10},{10,2},{3,11},{11,3},{4,12},{12,4},... | collective-permute-start | bytes 294920 | tf_op jit(solution)/shard_map/ppermute | solution.py:436
  21.6 17.2 %copy-start = (bf16[384,3072]{1,0:T(8,128)(2,1)}, bf16[384,3072]{1,0:T(8,128)(2,1)S(1)}, u32[]{:S(2)}) copy-start(bf16[384,3072]{1,0:T(8,128)(2,1)S(1)} %collective-permute-done.1) | copy-start | bytes 7077892
  21.6 22.8 %collective-permute-start.4 = (bf16[544,384]{1,0:T(8,128)(2,1)}, bf16[544,384]{1,0:T(8,128)(2,1)S(1)}, u32[]{:S(2)}, u32[]{:S(2)}) collective-permute-start(bf16[544,384]{1,0:T(8,128)(2,1)} %constant_dynamic-update-slice_fusion.refs_0_.refs_2_), channel_id=1, source_target_pairs={{0,16},{16,32},{32,48},{48,64},{64,80},{80,96},{96,112},{112,128},... | collective-permute-start | bytes 1253384 | tf_op jit(solution)/shard_map/ppermute | solution.py:389
  24.6 27.4 %collective-permute-start.3 = (bf16[544,384]{1,0:T(8,128)(2,1)}, bf16[544,384]{1,0:T(8,128)(2,1)}, u32[]{:S(2)}, u32[]{:S(2)}) collective-permute-start(bf16[544,384]{1,0:T(8,128)(2,1)} %constant_dynamic-update-slice_fusion.refs_0_.refs_2_), channel_id=1, source_target_pairs={{0,64},{64,128},{128,192},{1,65},{65,129},{129,193},{2,66},{66,130... | collective-permute-start | bytes 1253384 | tf_op jit(solution)/shard_map/ppermute | solution.py:422
  28.5 19.2 %copy-start.4 = (bf16[544,384]{1,0:T(8,128)(2,1)S(1)}, bf16[544,384]{1,0:T(8,128)(2,1)}, u32[]{:S(2)}) copy-start(bf16[544,384]{1,0:T(8,128)(2,1)} %constant_dynamic-update-slice_fusion.refs_0_.refs_2_) | copy-start | bytes 1253380
  38.8 13.3 %copy-start.5 = (bf16[128,384]{1,0:T(8,128)(2,1)}, bf16[128,384]{1,0:T(8,128)(2,1)S(1)}, u32[]{:S(2)}) copy-start(bf16[128,384]{1,0:T(8,128)(2,1)S(1)} %collective-permute-done.2.refs_1_.refs_4_) | copy-start | bytes 294916
  38.8 17.2 %all-to-all-start = ((bf16[16,112,128]{2,1,0:T(8,128)(2,1)}), bf16[16,112,128]{2,1,0:T(8,128)(2,1)S(1)}, u32[]{:S(2)}, u32[]{:S(2)}) async-start(bf16[16,112,128]{2,1,0:T(8,128)(2,1)} %get-tuple-element.27), calls=%async_computation | async-start | bytes 917504 | tf_op jit(solution)/shard_map/all_to_all | solution.py:438
  44.4 7.7 %copy-start.6 = (bf16[544,384]{1,0:T(8,128)(2,1)}, bf16[544,384]{1,0:T(8,128)(2,1)S(1)}, u32[]{:S(2)}) copy-start(bf16[544,384]{1,0:T(8,128)(2,1)S(1)} %collective-permute-done.4.refs_4_) | copy-start | bytes 1253380
  44.4 17.7 %collective-permute-start.5 = (bf16[544,384]{1,0:T(8,128)(2,1)S(1)}, bf16[544,384]{1,0:T(8,128)(2,1)S(1)}, u32[]{:S(2)}, u32[]{:S(2)}) collective-permute-start(bf16[544,384]{1,0:T(8,128)(2,1)S(1)} %collective-permute-done.4.refs_4_), channel_id=1, source_target_pairs={{0,16},{16,32},{32,48},{48,64},{64,80},{80,96},{96,112},{112,128},... | collective-permute-start | bytes 1253384 | tf_op jit(solution)/shard_map/ppermute | solution.py:389
  47.7 14.5 %collective-permute-start.6 = (bf16[544,384]{1,0:T(8,128)(2,1)S(1)}, bf16[544,384]{1,0:T(8,128)(2,1)S(1)}, u32[]{:S(2)}, u32[]{:S(2)}) collective-permute-start(bf16[544,384]{1,0:T(8,128)(2,1)S(1)} %copy-done.4), channel_id=1, source_target_pairs={{0,48},{16,64},{32,80},{48,96},{64,112},{80,128},{96,144},{112,160... | collective-permute-start | bytes 1253384 | tf_op jit(solution)/shard_map/ppermute | solution.py:389
  57.2 19.8 %all-to-all-start.1 = ((bf16[16,112,128]{2,1,0:T(8,128)(2,1)}), bf16[16,112,128]{2,1,0:T(8,128)(2,1)S(1)}, u32[]{:S(2)}, u32[]{:S(2)}) async-start(bf16[16,112,128]{2,1,0:T(8,128)(2,1)} %shard_map.122), calls=%async_computation.1 | async-start | bytes 917504 | tf_op jit(solution)/shard_map/all_to_all | solution.py:450
  62.1 0.8 copy-start.2
  62.2 0.9 copy-start.3
  76.9 0.8 copy-start.1

commit v12 on v11

--- a/solution.py
+++ b/solution.py
@@ -293,11 +293,11 @@
     return lax.axis_index("x") * 4 + lax.axis_index("y")
 
 
-def attend_first_body(own, recv, pair_kv, shifted, w1, acc_ref, stat_ref, score_ref):
+def attend_first_body(own, recv, pair_kv, shifted, w1, w3, acc_ref, stat_ref, score_ref):
     zh = lax.axis_index("zh")
     q_own = queries(own.get())
     q_recv = queries(recv.get())
-    wins = {0: pair_kv.get(), 4: shifted.get(), 1: w1.get()}
+    wins = {0: pair_kv.get(), 4: shifted.get(), 1: w1.get(), 3: w3.get()}
     rows_of = ordered_rows(zh)
     lane = lax.broadcasted_iota(jnp.int32, (BLK, 128), 1)
     for parity in range(2):
@@ -310,11 +310,11 @@
         stat_ref[parity] = jnp.where(lane < 64, top, total)
 
 
-def attend_second_body(own, recv, w2, w3, acc_in, stat, gain_in, out_ref, score_ref):
+def attend_second_body(own, recv, w2, acc_in, stat, gain_in, out_ref, score_ref):
     zh = lax.axis_index("zh")
     q_own = queries(own.get())
     q_recv = queries(recv.get())
-    wins = {2: w2.get(), 3: w3.get()}
+    wins = {2: w2.get()}
     gain = head_gain(gain_in, zh)
     rows_of = ordered_rows(zh)
     stats = stat.get()
@@ -421,6 +421,7 @@
     pair_kv, proj_other = lax.optimization_barrier((pair_kv, proj_other))
     shifted = lax.ppermute(pair_kv, "x", [(i, i + 1) for i in range(3)])
     w1 = behind(pair_kv, 1)
+    w3 = behind(pair_kv, 3)
     even, outgoing = call(
         second_body,
         [mats, sds((PAIRS, CROWS, 128), BF16)],
@@ -430,20 +431,19 @@
         scratch=[flat],
         mine=(1, 2, 3),
     )
-    even, later_kv, later_w1 = lax.optimization_barrier((even, pair_kv, w1))
+    even, later_w1 = lax.optimization_barrier((even, w1))
     w2 = behind(later_w1, 1)
-    w3 = behind(later_kv, 3)
     recv_q = lax.ppermute(send_q, "zh", [(0, 1), (1, 0)])
     outgoing, recv_q = lax.optimization_barrier((outgoing, recv_q))
     pieces = lax.all_to_all(outgoing, ("x", "y"), 0, 0, tiled=True)
     acc, stat = call(
         attend_first_body,
         [sds((2, BLK, HD), F32), sds((2, BLK, 128), F32)],
-        (own_q, recv_q, pair_kv, shifted, w1),
+        (own_q, recv_q, pair_kv, shifted, w1, w3),
         500_000_000,
         2_000_000,
         600_000,
-        scratch=[pltpu.VMEM((2, 5, BLK, BLK), F32)],
+        scratch=[pltpu.VMEM((2, 7, BLK, BLK), F32)],
     )
     pieces, acc = lax.optimization_barrier((pieces, acc))
     (sums,) = call(scan_body, [sds((PAIRS, CROWS, 128), BF16)], (pieces,), 500_000, 1_000_000, cap=SMALL)
@@ -451,11 +451,11 @@
     (att,) = call(
         attend_second_body,
         [sds((2, BLK, HD), F32)],
-        (own_q, recv_q, w2, w3, acc, stat, attn_gain.reshape(3, 128)),
+        (own_q, recv_q, w2, acc, stat, attn_gain.reshape(3, 128)),
         500_000_000,
         2_000_000,
         600_000,
-        scratch=[pltpu.VMEM((2, 4, BLK, BLK), F32)],
+        scratch=[pltpu.VMEM((2, 2, BLK, BLK), F32)],
     )
     (mixed,) = call(
         apply_body,

time: 130 us -> 130 us (level)
  starting transfers between devices: 33.9 us -> 30.6 us
  waiting for transfers between devices: 9.76 us -> 12.3 us
    all_to_all x1, waiting for transfers between devices: 0.01 us -> 7.84 us  [local(): pieces = lax.all_to_all(outgoing, ('x', 'y'), 0, 0, tiled=True)]
    all_to_all x1, waiting for transfers between devices: 9.74 us -> 4.44 us  [local(): prefix = lax.all_to_all(sums, ('x', 'y'), 0, 0, tiled=True)]
    all_to_all x1, starting transfers between devices: 5.6 us -> 3.57 us  [local(): pieces = lax.all_to_all(outgoing, ('x', 'y'), 0, 0, tiled=True)]
  transfers between devices with their start and end apart: 9 -> 9, of which waited for: 1 -> 2; matrix products, arithmetic and copies ran while one was open for 1% -> 1% of each run, Pallas kernels for 24% -> 24%
where the time goes in v12:
time: 130 us
  blocking collectives  42.5 us (33%)
  Pallas kernels  40.8 us (31%)
  starting transfers between devices  30.6 us (24%)
  waiting for transfers between devices  12.3 us (9%)
  local copies, waits for them, and re-layouts  2.95 us (2%)
    pallas_call x9, Pallas kernels, call(): pl.pallas_call(kernel, out_shape=outs, in_specs=[any_spec] * n_in, out_sp...  40.8 us
    all_to_all x1, blocking collectives, local(): lax.all_to_all(partial.reshape(4, 32, WIDTH), 'zl', 0, 0, tiled=True)  23.7 us
    all_to_all x1, blocking collectives, local(): mixed = lax.all_to_all(mixed, ('c', 'zh'), 0, 0, tiled=True)  18.8 us
    ppermute x3, starting transfers between devices, behind(): lax.ppermute(pair_kv, ('x', 'y'), [(i, i + distance) for i in range(PAIRS...  11.4 us
    all_to_all x1, waiting for transfers between devices, local(): pieces = lax.all_to_all(outgoing, ('x', 'y'), 0, 0, tiled=True)  7.84 us
    ppermute x1, starting transfers between devices, local(): recv = lax.ppermute(send, 'zh', [(0, 1), (1, 0)])  5.26 us
    all_to_all x1, waiting for transfers between devices, local(): prefix = lax.all_to_all(sums, ('x', 'y'), 0, 0, tiled=True)  4.44 us
    all_to_all x1, starting transfers between devices, local(): prefix = lax.all_to_all(sums, ('x', 'y'), 0, 0, tiled=True)  3.93 us
  transfers between devices with their start and end apart: 9, of which 2 were waited for; matrix products, arithmetic and copies ran while one was open for 1% of the time, Pallas kernels for 24%

profile of v12, /device:TPU:1, one launch (start us, length us, event | category | flops | bytes accessed | tf_op | source)
XLA Modules:
  0.0 129.5 jit_solution(16861901009637163149)
XLA Ops:
  0.0 3.2 %collective-permute-start.1 = (bf16[384,3072]{1,0:T(8,128)(2,1)}, bf16[384,3072]{1,0:T(8,128)(2,1)S(1)}, u32[]{:S(2)}, u32[]{:S(2)}) collective-permute-start(bf16[384,3072]{1,0:T(8,128)(2,1)} %param.23), channel_id=1, source_target_pairs={{0,1},{1,0},{2,3},{3,2},{4,5},{5,4},{6,7},{7,6},{8,9},{9,8},{10,11... | collective-permute-start | bytes 7077896 | tf_op jit(solution)/shard_map/ppermute | solution.py:408
  3.2 2.0 %shard_map.119 = bf16[272,384]{1,0:T(8,128)(2,1)} custom-call(bf16[256,384]{1,0:T(8,128)(2,1)} %refs_0_.3, bf16[256,384]{1,0:T(8,128)(2,1)} %refs_1_.4, f32[2,256]{1,0:T(2,128)} %bitcast.16, f32[1,2]{1,0:T(1,128)} %refs_3_.3), custom_call_target="tpu_custom_call" | custom-call | bytes 1000000 | tf_op jit(solution)/shard_map/pallas_call | solution.py:72
  5.3 5.3 %collective-permute-start = (bf16[272,384]{1,0:T(8,128)(2,1)}, bf16[272,384]{1,0:T(8,128)(2,1)S(1)}, u32[]{:S(2)}, u32[]{:S(2)}) collective-permute-start(bf16[272,384]{1,0:T(8,128)(2,1)} %shard_map.119), channel_id=1, source_target_pairs={{0,8},{8,0},{1,9},{9,1},{2,10},{10,2},{3,11},{11,3},{4,12},{12,4},... | collective-permute-start | bytes 626696 | tf_op jit(solution)/shard_map/ppermute | solution.py:407
  10.5 10.0 %shard_map.118 = (f32[3,192,384]{2,1,0:T(8,128)}, bf16[544,384]{1,0:T(8,128)(2,1)}, bf16[128,384]{1,0:T(8,128)(2,1)}, bf16[128,384]{1,0:T(8,128)(2,1)}) custom-call(bf16[256,384]{1,0:T(8,128)(2,1)} %refs_0_.3, bf16[256,384]{1,0:T(8,128)(2,1)} %refs_1_.4, f32[2,256]{1,0:T(2,128)} %bitcast.17, f32[1,2]{1,0:T(1,128)} %refs_3_.3, f32[2,192,384]{2,1,0:T(8,128)} %refs_5_.3, ...), custom_call_target="tpu_custom_call" | custom-call | flops 6000000000 | bytes 3000000 | tf_op jit(solution)/shard_map/pallas_call | solution.py:72
  20.6 0.3 collective-permute-start.2
  20.9 0.0 collective-permute-done
  20.9 0.7 constant_dynamic-update-slice_fusion.refs_0_.refs_2_
  21.6 0.0 collective-permute-done.1
  21.6 0.0 copy-start
  21.6 3.0 %collective-permute-start.3 = (bf16[544,384]{1,0:T(8,128)(2,1)}, bf16[544,384]{1,0:T(8,128)(2,1)S(1)}, u32[]{:S(2)}, u32[]{:S(2)}) collective-permute-start(bf16[544,384]{1,0:T(8,128)(2,1)} %constant_dynamic-update-slice_fusion.refs_0_.refs_2_), channel_id=1, source_target_pairs={{0,64},{64,128},{128,192},{1,65},{65,129},{129,193},{2,66},{66,130... | collective-permute-start | bytes 1253384 | tf_op jit(solution)/shard_map/ppermute | solution.py:422
  24.5 3.2 %collective-permute-start.4 = (bf16[544,384]{1,0:T(8,128)(2,1)}, bf16[544,384]{1,0:T(8,128)(2,1)S(1)}, u32[]{:S(2)}, u32[]{:S(2)}) collective-permute-start(bf16[544,384]{1,0:T(8,128)(2,1)} %constant_dynamic-update-slice_fusion.refs_0_.refs_2_), channel_id=1, source_target_pairs={{0,16},{16,32},{32,48},{48,64},{64,80},{80,96},{96,112},{112,128},... | collective-permute-start | bytes 1253384 | tf_op jit(solution)/shard_map/ppermute | solution.py:389
  27.8 5.0 %collective-permute-start.5 = (bf16[544,384]{1,0:T(8,128)(2,1)}, bf16[544,384]{1,0:T(8,128)(2,1)}, u32[]{:S(2)}, u32[]{:S(2)}) collective-permute-start(bf16[544,384]{1,0:T(8,128)(2,1)} %constant_dynamic-update-slice_fusion.refs_0_.refs_2_), channel_id=1, source_target_pairs={{0,48},{16,64},{32,80},{48,96},{64,112},{80,128},{96,144},{112,160... | collective-permute-start | bytes 1253384 | tf_op jit(solution)/shard_map/ppermute | solution.py:389
  32.8 10.1 %shard_map.120 = (f32[3,192,384]{2,1,0:T(8,128)}, bf16[16,112,128]{2,1,0:T(8,128)(2,1)}) custom-call(bf16[544,384]{1,0:T(8,128)(2,1)} %constant_dynamic-update-slice_fusion.refs_0_.refs_2_, f32[2,192,384]{2,1,0:T(8,128)} %refs_5_.3, f32[2,192,384]{2,1,0:T(8,128)} %refs_6_.1, f32[2,192,384]{2,1,0:T(8,128)} %bitcast.14, f32[1,2]{1,0:T(1,128)} %bitcast.21, ...), custom_call_target="tpu_custom_call" | custom-call | flops 6000000000 | bytes 4000000 | tf_op jit(solution)/shard_map/pallas_call | solution.py:72
  42.9 0.0 copy-done
  42.9 0.0 collective-permute-done.2.refs_1_.refs_4_
  42.9 0.0 copy-start.2
  42.9 3.6 %all-to-all-start = ((bf16[16,112,128]{2,1,0:T(8,128)(2,1)}), bf16[16,112,128]{2,1,0:T(8,128)(2,1)S(1)}, u32[]{:S(2)}, u32[]{:S(2)}) async-start(bf16[16,112,128]{2,1,0:T(8,128)(2,1)} %get-tuple-element.26), calls=%async_computation | async-start | bytes 917504 | tf_op jit(solution)/shard_map/all_to_all | solution.py:438
  46.5 0.0 collective-permute-done.4.refs_4_
  46.5 0.0 copy-start.3
  46.5 3.2 %collective-permute-start.6 = (bf16[544,384]{1,0:T(8,128)(2,1)S(1)}, bf16[544,384]{1,0:T(8,128)(2,1)S(1)}, u32[]{:S(2)}, u32[]{:S(2)}) collective-permute-start(bf16[544,384]{1,0:T(8,128)(2,1)S(1)} %collective-permute-done.4.refs_4_), channel_id=1, source_target_pairs={{0,16},{16,32},{32,48},{48,64},{64,80},{80,96},{96,112},{112,128},... | collective-permute-start | bytes 1253384 | tf_op jit(solution)/shard_map/ppermute | solution.py:389
  49.7 0.0 collective-permute-done.3.refs_3_
  49.7 0.0 copy-start.4
  49.7 0.0 collective-permute-done.5.refs_5_
  49.7 0.0 copy-done.2
  49.7 0.0 copy-done.3
  49.7 0.7 copy-done.4
  50.5 4.6 %shard_map.121 = (f32[2,256,192]{2,1,0:T(8,128)}, f32[2,256,128]{2,1,0:T(8,128)}) custom-call(bf16[128,384]{1,0:T(8,128)(2,1)} %get-tuple-element.27.refs_0_.refs_3_, bf16[128,384]{1,0:T(8,128)(2,1)} %copy-done.2, bf16[544,384]{1,0:T(8,128)(2,1)} %constant_dynamic-update-slice_fusion.refs_0_.refs_2_, bf16[544,384]{1,0:T(8,128)(2,1)} %copy-done.4, ...), custom_call_target="tpu_custom_call" | custom-call | flops 500000000 | bytes 2000000 | tf_op jit(solution)/shard_map/pallas_call | solution.py:72
  55.1 7.8 %all-to-all-done.refs_0_ = bf16[16,112,128]{2,1,0:T(8,128)(2,1)S(1)} async-done(((bf16[16,112,128]{2,1,0:T(8,128)(2,1)}), bf16[16,112,128]{2,1,0:T(8,128)(2,1)S(1)}, u32[]{:S(2)}, u32[]{:S(2)}) %all-to-all-start) | async-done | bytes 458784 | tf_op jit(solution)/shard_map/all_to_all | solution.py:438
  62.9 1.2 shard_map.122
  64.1 3.9 %all-to-all-start.1 = ((bf16[16,112,128]{2,1,0:T(8,128)(2,1)}), bf16[16,112,128]{2,1,0:T(8,128)(2,1)S(1)}, u32[]{:S(2)}, u32[]{:S(2)}) async-start(bf16[16,112,128]{2,1,0:T(8,128)(2,1)} %shard_map.122), calls=%async_computation.1 | async-start | bytes 917504 | tf_op jit(solution)/shard_map/all_to_all | solution.py:450
  68.0 0.0 collective-permute-done.6.refs_2_
  68.1 0.0 copy-start.5
  68.1 0.7 copy-done.5
  68.8 3.5 %shard_map.123.refs_9_ = f32[2,256,192]{2,1,0:T(8,128)} custom-call(bf16[128,384]{1,0:T(8,128)(2,1)} %get-tuple-element.27.refs_0_.refs_3_, bf16[128,384]{1,0:T(8,128)(2,1)} %copy-done.2, bf16[544,384]{1,0:T(8,128)(2,1)} %copy-done.5, f32[2,256,192]{2,1,0:T(8,128)} %get-tuple-element.34.refs_3_, f32[2,256,128]{2,1,0:T(8,128)} %get-tuple-element.35.refs_4_, ...), custom_call_target="tpu_custom_call" | custom-call | flops 500000000 | bytes 2000000 | tf_op jit(solution)/shard_map/pallas_call | solution.py:72
  72.3 4.4 %all-to-all-done.1.refs_0_ = bf16[16,112,128]{2,1,0:T(8,128)(2,1)S(1)} async-done(((bf16[16,112,128]{2,1,0:T(8,128)(2,1)}), bf16[16,112,128]{2,1,0:T(8,128)(2,1)S(1)}, u32[]{:S(2)}, u32[]{:S(2)}) %all-to-all-start.1) | async-done | bytes 458784 | tf_op jit(solution)/shard_map/all_to_all | solution.py:450
  76.7 0.0 copy-start.1
  76.7 0.8 copy-done.1
  77.5 4.7 %shard_map.124 = bf16[4,64,384]{2,1,0:T(8,128)(2,1)} custom-call(bf16[16,112,128]{2,1,0:T(8,128)(2,1)} %copy-done.1, f32[3,192,384]{2,1,0:T(8,128)} %get-tuple-element.32.refs_1_, bf16[544,384]{1,0:T(8,128)(2,1)} %constant_dynamic-update-slice_fusion.refs_0_.refs_2_, bf16[128,384]{1,0:T(8,128)(2,1)} %get-tuple-element.27.refs_0_.refs_3_, ...), custom_call_target="tpu_custom_call" | custom-call | flops 600000000 | bytes 5000000 | tf_op jit(solution)/shard_map/pallas_call | solution.py:72
  82.2 18.8 %all_to_all.20.refs_0_ = bf16[4,64,384]{2,1,0:T(8,128)(2,1)} all-to-all(bf16[4,64,384]{2,1,0:T(8,128)(2,1)} %shard_map.124), channel_id=1, replica_groups=mesh['x'=4,'y'=4,'zh'=2,'zl'=4,'c'=2] {'c','zh'}, dimensions={0} | all-to-all | bytes 393216 | tf_op jit(solution)/shard_map/all_to_all | solution.py:469
  101.0 3.8 %shard_map.125 = bf16[128,3072]{1,0:T(8,128)(2,1)} custom-call(bf16[4,64,384]{2,1,0:T(8,128)(2,1)} %all_to_all.20.refs_0_, bf16[2,192,3072]{2,1,0:T(8,128)(2,1)} %bitcast.8, bf16[2,192,3072]{2,1,0:T(8,128)(2,1)} %bitcast.9, bf16[2,192,3072]{2,1,0:T(8,128)(2,1)} %bitcast.10, bf16[2,192,3072]{2,1,0:T(8,128)(2,1)} %bitcast.11), custom_call_target="tpu_custom_call" | custom-call | flops 600000000 | bytes 6000000 | tf_op jit(solution)/shard_map/pallas_call | solution.py:72
  104.8 23.7 %all_to_all.21.refs_0_ = bf16[4,32,3072]{2,1,0:T(8,128)(2,1)S(1)} all-to-all(bf16[4,32,3072]{2,1,0:T(8,128)(2,1)} %bitcast.12), channel_id=1, replica_groups=mesh['x'=4,'y'=4,'zh'=2,'zl'=4,'c'=2] {'zl'}, dimensions={0} | all-to-all | bytes 1572864 | tf_op jit(solution)/shard_map/all_to_all | solution.py:480
  128.5 0.8 shard_map.126
Async XLA Ops:
  0.0 21.6 %collective-permute-start.1 = (bf16[384,3072]{1,0:T(8,128)(2,1)}, bf16[384,3072]{1,0:T(8,128)(2,1)S(1)}, u32[]{:S(2)}, u32[]{:S(2)}) collective-permute-start(bf16[384,3072]{1,0:T(8,128)(2,1)} %param.23), channel_id=1, source_target_pairs={{0,1},{1,0},{2,3},{3,2},{4,5},{5,4},{6,7},{7,6},{8,9},{9,8},{10,11... | collective-permute-start | bytes 7077896 | tf_op jit(solution)/shard_map/ppermute | solution.py:408
  5.3 15.6 %collective-permute-start = (bf16[272,384]{1,0:T(8,128)(2,1)}, bf16[272,384]{1,0:T(8,128)(2,1)S(1)}, u32[]{:S(2)}, u32[]{:S(2)}) collective-permute-start(bf16[272,384]{1,0:T(8,128)(2,1)} %shard_map.119), channel_id=1, source_target_pairs={{0,8},{8,0},{1,9},{9,1},{2,10},{10,2},{3,11},{11,3},{4,12},{12,4},... | collective-permute-start | bytes 626696 | tf_op jit(solution)/shard_map/ppermute | solution.py:407
  20.6 22.3 %collective-permute-start.2 = (bf16[128,384]{1,0:T(8,128)(2,1)}, bf16[128,384]{1,0:T(8,128)(2,1)S(1)}, u32[]{:S(2)}, u32[]{:S(2)}) collective-permute-start(bf16[128,384]{1,0:T(8,128)(2,1)} %get-tuple-element.25), channel_id=1, source_target_pairs={{0,8},{8,0},{1,9},{9,1},{2,10},{10,2},{3,11},{11,3},{4,12},{12,4},... | collective-permute-start | bytes 294920 | tf_op jit(solution)/shard_map/ppermute | solution.py:436
  21.6 21.3 %copy-start = (bf16[384,3072]{1,0:T(8,128)(2,1)}, bf16[384,3072]{1,0:T(8,128)(2,1)S(1)}, u32[]{:S(2)}) copy-start(bf16[384,3072]{1,0:T(8,128)(2,1)S(1)} %collective-permute-done.1) | copy-start | bytes 7077892
  21.6 28.1 %collective-permute-start.3 = (bf16[544,384]{1,0:T(8,128)(2,1)}, bf16[544,384]{1,0:T(8,128)(2,1)S(1)}, u32[]{:S(2)}, u32[]{:S(2)}) collective-permute-start(bf16[544,384]{1,0:T(8,128)(2,1)} %constant_dynamic-update-slice_fusion.refs_0_.refs_2_), channel_id=1, source_target_pairs={{0,64},{64,128},{128,192},{1,65},{65,129},{129,193},{2,66},{66,130... | collective-permute-start | bytes 1253384 | tf_op jit(solution)/shard_map/ppermute | solution.py:422
  24.5 22.0 %collective-permute-start.4 = (bf16[544,384]{1,0:T(8,128)(2,1)}, bf16[544,384]{1,0:T(8,128)(2,1)S(1)}, u32[]{:S(2)}, u32[]{:S(2)}) collective-permute-start(bf16[544,384]{1,0:T(8,128)(2,1)} %constant_dynamic-update-slice_fusion.refs_0_.refs_2_), channel_id=1, source_target_pairs={{0,16},{16,32},{32,48},{48,64},{64,80},{80,96},{96,112},{112,128},... | collective-permute-start | bytes 1253384 | tf_op jit(solution)/shard_map/ppermute | solution.py:389
  27.8 21.9 %collective-permute-start.5 = (bf16[544,384]{1,0:T(8,128)(2,1)}, bf16[544,384]{1,0:T(8,128)(2,1)}, u32[]{:S(2)}, u32[]{:S(2)}) collective-permute-start(bf16[544,384]{1,0:T(8,128)(2,1)} %constant_dynamic-update-slice_fusion.refs_0_.refs_2_), channel_id=1, source_target_pairs={{0,48},{16,64},{32,80},{48,96},{64,112},{80,128},{96,144},{112,160... | collective-permute-start | bytes 1253384 | tf_op jit(solution)/shard_map/ppermute | solution.py:389
  42.9 6.8 %copy-start.2 = (bf16[128,384]{1,0:T(8,128)(2,1)}, bf16[128,384]{1,0:T(8,128)(2,1)S(1)}, u32[]{:S(2)}) copy-start(bf16[128,384]{1,0:T(8,128)(2,1)S(1)} %collective-permute-done.2.refs_1_.refs_4_) | copy-start | bytes 294916
  42.9 20.0 %all-to-all-start = ((bf16[16,112,128]{2,1,0:T(8,128)(2,1)}), bf16[16,112,128]{2,1,0:T(8,128)(2,1)S(1)}, u32[]{:S(2)}, u32[]{:S(2)}) async-start(bf16[16,112,128]{2,1,0:T(8,128)(2,1)} %get-tuple-element.26), calls=%async_computation | async-start | bytes 917504 | tf_op jit(solution)/shard_map/all_to_all | solution.py:438
  46.5 3.2 %copy-start.3 = (bf16[544,384]{1,0:T(8,128)(2,1)}, bf16[544,384]{1,0:T(8,128)(2,1)S(1)}, u32[]{:S(2)}) copy-start(bf16[544,384]{1,0:T(8,128)(2,1)S(1)} %collective-permute-done.4.refs_4_) | copy-start | bytes 1253380
  46.5 21.5 %collective-permute-start.6 = (bf16[544,384]{1,0:T(8,128)(2,1)S(1)}, bf16[544,384]{1,0:T(8,128)(2,1)S(1)}, u32[]{:S(2)}, u32[]{:S(2)}) collective-permute-start(bf16[544,384]{1,0:T(8,128)(2,1)S(1)} %collective-permute-done.4.refs_4_), channel_id=1, source_target_pairs={{0,16},{16,32},{32,48},{48,64},{64,80},{80,96},{96,112},{112,128},... | collective-permute-start | bytes 1253384 | tf_op jit(solution)/shard_map/ppermute | solution.py:389
  49.7 0.7 copy-start.4
  64.1 12.6 %all-to-all-start.1 = ((bf16[16,112,128]{2,1,0:T(8,128)(2,1)}), bf16[16,112,128]{2,1,0:T(8,128)(2,1)S(1)}, u32[]{:S(2)}, u32[]{:S(2)}) async-start(bf16[16,112,128]{2,1,0:T(8,128)(2,1)} %shard_map.122), calls=%async_computation.1 | async-start | bytes 917504 | tf_op jit(solution)/shard_map/all_to_all | solution.py:450
  68.1 0.7 copy-start.5
  76.7 0.8 copy-start.1
